TPU v7x, 32 devices: a whole 2x2x4 slice. The times are simulated.
32 devices in a mesh: parts: 2 (over y), strip: 4 (over z), col: 2 (over x), probe: 2 (over core).
Axes of the slice: x: 2, y: 2, z: 4, core: 2. Of those that a mesh axis runs over, the one named last changes fastest.
Arguments:
- signs: int32 [16, 256, 1024], P(('parts', 'probe'), 'strip', 'col'), parts along dimension 0, may hold values from -1 to 1, as said below
- onsite: float32 [512, 1024], P(('parts', 'strip'), 'col'), parts along dimension 0, may hold values from -1 to 1
- hop_right: float32 [512, 1024], P(('parts', 'strip'), 'col'), parts along dimension 0, may hold values from -1.5 to -0.5
- hop_down: float32 [512, 1024], P(('parts', 'strip'), 'col'), parts along dimension 0, may hold values from -1.5 to -0.5
- moment_weights: float32 [3], replicated, may hold values from 0.5 to 1.5
- forward_now: float32 [16, 256, 1024], P(('parts', 'probe'), 'strip', 'col'), parts along dimension 0, may hold values from -6 to 6
- forward_next: float32 [16, 256, 1024], P(('parts', 'probe'), 'strip', 'col'), parts along dimension 0, may hold values from -6 to 6
- adjoint_now: float32 [16, 256, 1024], P(('parts', 'probe'), 'strip', 'col'), parts along dimension 0, may hold values from -6 to 6
- adjoint_next: float32 [16, 256, 1024], P(('parts', 'probe'), 'strip', 'col'), parts along dimension 0, may hold values from -6 to 6
Outputs:
- right_force: float32 [512, 1024], P(('parts', 'strip'), 'col'), parts along dimension 0
- down_force: float32 [512, 1024], P(('parts', 'strip'), 'col'), parts along dimension 0
- site_force: float32 [512, 1024], P(('parts', 'strip'), 'col'), parts along dimension 0
- forward_out: float32 [16, 256, 1024], P(('parts', 'probe'), 'strip', 'col'), parts along dimension 0
- adjoint_out: float32 [16, 256, 1024], P(('parts', 'probe'), 'strip', 'col'), parts along dimension 0
There are 2 independent parts, one for each index of `parts`. A program takes and returns all parts, laid end to end along the dimension named above; an argument that names none is the same for every part. Nothing has to cross between parts.
Inputs may be any that keep to these rules, and one draw needn't show every extreme that they name: `signs`: each entry is -1 or 1.
All inputs are finite; a program needn't handle non-finite values.
Results may differ from a plain program's by a relative error of at most 0.0001.
Values sent between devices are 32-bit elements; how exact they have to be, the bound alone decides.
No kernel may reach another device: no remote copies, remote signals or barrier semaphores. Data moves between devices by JAX's collectives and lax.ppermute only.
A program may use at most 64 MiB of HBM per device.

v0:
```python
import jax
import jax.numpy as jnp
from jax import lax
from jax.sharding import PartitionSpec as P

STEPS = 3


spectral_half = 7.5


def shifted(x, axis, by):
    size = lax.axis_size(axis)
    return lax.ppermute(x, axis, [(i, (i + by) % size) for i in range(size)])


def with_halo(block, sides, width):
    for axis, dim in sides:
        count = lax.axis_size(axis)
        forward = [(i, i + 1) for i in range(count - 1)]
        forward.append((count - 1, 0))
        backward = [(target, source) for source, target in forward]
        low = lax.ppermute(
            lax.slice_in_dim(block, block.shape[dim] - width, None, axis=dim), axis, forward
        )
        high = lax.ppermute(lax.slice_in_dim(block, 0, width, axis=dim), axis, backward)
        block = jnp.concatenate([low, block, high], axis=dim)
    return block


def stencil(field, onsite, right_hop, down_hop):
    total = onsite * field[..., 1:-1, 1:-1]
    total = total + right_hop[1:-1, 1:-1] * field[..., 1:-1, 2:]
    total = total + right_hop[1:-1, :-2] * field[..., 1:-1, :-2]
    total = total + down_hop[1:-1, 1:-1] * field[..., 2:, 1:-1]
    total = total + down_hop[:-2, 1:-1] * field[..., :-2, 1:-1]
    return total / spectral_half


def bond_terms(forward, adjoint, margin):
    span_rows = forward.shape[-2] - 2 * margin
    span_cols = forward.shape[-1] - 2 * margin
    lo_row, lo_col = (margin, margin)
    fwd_centre = forward[:, lo_row : lo_row + span_rows, lo_col : lo_col + span_cols]
    fwd_right = forward[:, lo_row : lo_row + span_rows, lo_col + 1 : lo_col + 1 + span_cols]
    fwd_below = forward[:, lo_row + 1 : lo_row + 1 + span_rows, lo_col : lo_col + span_cols]
    adj_centre = adjoint[:, lo_row : lo_row + span_rows, lo_col : lo_col + span_cols]
    adj_right = adjoint[:, lo_row : lo_row + span_rows, lo_col + 1 : lo_col + 1 + span_cols]
    adj_below = adjoint[:, lo_row + 1 : lo_row + 1 + span_rows, lo_col : lo_col + span_cols]
    right_term = jnp.sum(adj_centre * fwd_right + adj_right * fwd_centre, axis=0)
    down_term = jnp.sum(adj_centre * fwd_below + adj_below * fwd_centre, axis=0)
    site_term = jnp.sum(adj_centre * fwd_centre, axis=0)
    return (right_term, down_term, site_term)


def local(
    signs,
    onsite,
    hop_right,
    hop_down,
    moment_weights,
    forward_now,
    forward_next,
    adjoint_now,
    adjoint_next,
):
    sign_field = signs.astype(jnp.float32)
    right_acc = jnp.zeros(onsite.shape, jnp.float32)
    down_acc = jnp.zeros(onsite.shape, jnp.float32)
    site_acc = jnp.zeros(onsite.shape, jnp.float32)
    row_count, col_count = onsite.shape
    left_column = shifted(hop_right[:, col_count - 1 :], "col", 1)
    upper_row = shifted(hop_down[row_count - 1 :, :], "strip", 1)
    right_full = jnp.concatenate(
        [left_column, hop_right, jnp.zeros((row_count, 1), jnp.float32)], axis=1
    )
    right_full = jnp.pad(right_full, ((1, 1), (0, 0)))
    down_full = jnp.concatenate(
        [upper_row, hop_down, jnp.zeros((1, col_count), jnp.float32)], axis=0
    )
    down_full = jnp.pad(down_full, ((0, 0), (1, 1)))
    current, previous = (forward_now, forward_next)
    adjoint, adjoint_prev = (adjoint_now, adjoint_next)
    for moment in range(STEPS):
        padded = with_halo(jnp.stack([current, adjoint]), (("strip", 2), ("col", 3)), 1)
        right_term, down_term, site_term = bond_terms(padded[0], padded[1], 1)
        right_acc = right_acc + right_term
        down_acc = down_acc + down_term
        site_acc = site_acc + site_term
        images = stencil(padded, onsite, right_full, down_full)
        adjoint_new = moment_weights[moment] * sign_field + 2.0 * images[1] - adjoint_prev
        current_new = 2.0 * images[0] - previous
        previous, current = (current, current_new)
        adjoint_prev, adjoint = (adjoint, adjoint_new)
    right_sum, down_sum, site_sum = lax.psum((right_acc, down_acc, site_acc), "probe")
    factor = 2.0 / spectral_half
    return (right_sum * factor, down_sum * factor, site_sum * factor, current, adjoint)


def solution(mesh):
    placed = (
        P(("parts", "probe"), "strip", "col"),
        P(("parts", "strip"), "col"),
        P(("parts", "strip"), "col"),
        P(("parts", "strip"), "col"),
        P(),
        P(("parts", "probe"), "strip", "col"),
        P(("parts", "probe"), "strip", "col"),
        P(("parts", "probe"), "strip", "col"),
        P(("parts", "probe"), "strip", "col"),
    )
    return jax.shard_map(
        local,
        mesh=mesh,
        in_specs=placed,
        out_specs=(
            P(("parts", "strip"), "col"),
            P(("parts", "strip"), "col"),
            P(("parts", "strip"), "col"),
            P(("parts", "probe"), "strip", "col"),
            P(("parts", "probe"), "strip", "col"),
        ),
        check_vma=False,
    )
```

profile of v0, /device:TPU:0, one launch (start us, length us, event | category | flops | bytes accessed | tf_op | source)
XLA Modules:
  0.0 108.6 jit_solution(12117120292399665729)
XLA Ops:
  7.2 0.0 copy-start
  7.2 0.0 copy-start.1
  7.2 0.0 all-reduce.3.cloned.1.call-start
  7.2 0.8 slice.226
  8.0 3.0 %collective-permute-start.5 = (f32[1,512]{1,0:T(1,128)S(1)}, f32[1,512]{1,0:T(1,128)S(1)}, u32[]{:S(2)}, u32[]{:S(2)}) collective-permute-start(f32[1,512]{1,0:T(1,128)S(1)} %slice.226), channel_id=1, source_target_pairs={{0,4},{4,8},{8,12},{12,0},{1,5},{5,9},{9,13},{13,1},{2,6},{6,10},{... | collective-permute-start | bytes 6152 | tf_op jit(solution)/shard_map/ppermute | solution.py:14
  11.1 1.0 fusion.66
  12.1 2.1 %collective-permute-start.1 = (f32[2,4,1,512]{3,2,1,0:T(1,128)S(1)}, f32[2,4,1,512]{3,2,1,0:T(1,128)S(1)}, u32[]{:S(2)}, u32[]{:S(2)}) collective-permute-start(f32[2,4,1,512]{3,2,1,0:T(1,128)S(1)} %get-tuple-element.39), channel_id=1, source_target_pairs={{4,0},{8,4},{12,8},{0,12},{5,1},{9,5},{13,9},{1,13},{6,2},{10,6},{... | collective-permute-start | bytes 49160 | tf_op jit(solution)/shard_map/ppermute | solution.py:26
  14.2 0.8 slice.222
  15.0 1.7 %collective-permute-start.4 = (f32[64,1]{1,0:T(8,128)S(1)}, f32[64,1]{1,0:T(8,128)S(1)}, u32[]{:S(2)}, u32[]{:S(2)}) collective-permute-start(f32[64,1]{1,0:T(8,128)S(1)} %slice.222), channel_id=1, source_target_pairs={{0,2},{2,0},{1,3},{3,1},{4,6},{6,4},{5,7},{7,5},{8,10},{10,8},{9,1... | collective-permute-start | bytes 776 | tf_op jit(solution)/shard_map/ppermute | solution.py:14
  16.7 1.4 %fusion.67 = (f32[1]{0:T(128)}, f32[1]{0:T(128)}, f32[1]{0:T(128)}) fusion(f32[3]{0:T(128)} %param.13), kind=kLoop, calls=%fused_computation.168 | loop fusion | bytes 24 | tf_op jit(solution)/shard_map/slice | solution.py:91
  18.1 0.9 collective-permute-done.4
  18.9 1.0 pad_maximum_fusion.55
  20.0 0.2 pad_maximum_fusion.50
  20.1 1.8 %collective-permute-start.3 = (f32[2,4,66,1]{3,2,1,0:T(8,128)S(1)}, f32[2,4,66,1]{3,2,1,0:T(8,128)S(1)}, u32[]{:S(2)}, u32[]{:S(2)}) collective-permute-start(f32[2,4,66,1]{3,2,1,0:T(8,128)S(1)} %get-tuple-element.29), channel_id=1, source_target_pairs={{2,0},{0,2},{3,1},{1,3},{6,4},{4,6},{7,5},{5,7},{10,8},{8,10},{11,... | collective-permute-start | bytes 6344 | tf_op jit(solution)/shard_map/ppermute | solution.py:26
  21.9 0.3 collective-permute-start.2
  22.3 0.0 copy-start.6
  22.3 0.0 copy-start.2
  22.3 0.0 copy-start.8
  22.3 0.0 copy-start.10
  22.3 7.8 %collective-permute-done.3 = f32[2,4,66,1]{3,2,1,0:T(8,128)S(1)} collective-permute-done((f32[2,4,66,1]{3,2,1,0:T(8,128)S(1)}, f32[2,4,66,1]{3,2,1,0:T(8,128)S(1)}, u32[]{:S(2)}, u32[]{:S(2)}) %collective-permute-start.3) | collective-permute-done | bytes 2144 | tf_op jit(solution)/shard_map/ppermute | solution.py:26
  30.2 3.7 %collective-permute-done.2 = f32[2,4,66,1]{3,2,1,0:T(8,128)S(1)} collective-permute-done((f32[2,4,66,1]{3,2,1,0:T(8,128)S(1)}, f32[2,4,66,1]{3,2,1,0:T(8,128)S(1)}, u32[]{:S(2)}, u32[]{:S(2)}) %collective-permute-start.2) | collective-permute-done | bytes 2144 | tf_op jit(solution)/shard_map/ppermute | solution.py:23
  33.8 0.9 fusion.17
  34.8 1.0 fusion.59
  35.8 3.6 %collective-permute-start.7 = (f32[2,4,1,512]{3,2,1,0:T(1,128)S(1)}, f32[2,4,1,512]{3,2,1,0:T(1,128)S(1)}, u32[]{:S(2)}, u32[]{:S(2)}) collective-permute-start(f32[2,4,1,512]{3,2,1,0:T(1,128)S(1)} %get-tuple-element.35), channel_id=1, source_target_pairs={{4,0},{8,4},{12,8},{0,12},{5,1},{9,5},{13,9},{1,13},{6,2},{10,6},{... | collective-permute-start | bytes 49160 | tf_op jit(solution)/shard_map/ppermute | solution.py:26
  39.4 0.7 pad_maximum_fusion
  40.0 0.1 slice_bitcast_fusion.5
  40.1 0.7 collective-permute-done.7
  40.8 4.1 %collective-permute-done.6 = f32[2,4,1,512]{3,2,1,0:T(1,128)S(1)} collective-permute-done((f32[2,4,1,512]{3,2,1,0:T(1,128)S(1)}, f32[2,4,1,512]{3,2,1,0:T(1,128)S(1)}, u32[]{:S(2)}, u32[]{:S(2)}) %collective-permute-start.6) | collective-permute-done | bytes 16416 | tf_op jit(solution)/shard_map/ppermute | solution.py:23
  44.9 0.2 pad_maximum_fusion.46
  45.1 1.6 %collective-permute-start.9 = (f32[2,4,66,1]{3,2,1,0:T(8,128)S(1)}, f32[2,4,66,1]{3,2,1,0:T(8,128)S(1)}, u32[]{:S(2)}, u32[]{:S(2)}) collective-permute-start(f32[2,4,66,1]{3,2,1,0:T(8,128)S(1)} %get-tuple-element.27), channel_id=1, source_target_pairs={{2,0},{0,2},{3,1},{1,3},{6,4},{4,6},{7,5},{5,7},{10,8},{8,10},{11,... | collective-permute-start | bytes 6344 | tf_op jit(solution)/shard_map/ppermute | solution.py:26
  46.6 0.5 collective-permute-start.8
  47.2 1.0 multiply_reduce_fusion.2
  48.1 4.9 %collective-permute-done.9 = f32[2,4,66,1]{3,2,1,0:T(8,128)S(1)} collective-permute-done((f32[2,4,66,1]{3,2,1,0:T(8,128)S(1)}, f32[2,4,66,1]{3,2,1,0:T(8,128)S(1)}, u32[]{:S(2)}, u32[]{:S(2)}) %collective-permute-start.9) | collective-permute-done | bytes 2144 | tf_op jit(solution)/shard_map/ppermute | solution.py:26
  53.0 3.2 %collective-permute-done.8 = f32[2,4,66,1]{3,2,1,0:T(8,128)S(1)} collective-permute-done((f32[2,4,66,1]{3,2,1,0:T(8,128)S(1)}, f32[2,4,66,1]{3,2,1,0:T(8,128)S(1)}, u32[]{:S(2)}, u32[]{:S(2)}) %collective-permute-start.8) | collective-permute-done | bytes 2144 | tf_op jit(solution)/shard_map/ppermute | solution.py:23
  56.1 0.9 fusion.11
  57.0 0.9 fusion.46
  58.0 0.1 collective-permute-start.10
  58.1 3.8 %collective-permute-start.11 = (f32[2,4,1,512]{3,2,1,0:T(1,128)S(1)}, f32[2,4,1,512]{3,2,1,0:T(1,128)S(1)}, u32[]{:S(2)}, u32[]{:S(2)}) collective-permute-start(f32[2,4,1,512]{3,2,1,0:T(1,128)S(1)} %get-tuple-element.32), channel_id=1, source_target_pairs={{4,0},{8,4},{12,8},{0,12},{5,1},{9,5},{13,9},{1,13},{6,2},{10,6},{... | collective-permute-start | bytes 49160 | tf_op jit(solution)/shard_map/ppermute | solution.py:26
  61.9 0.7 pad_maximum_fusion.1
  62.6 0.1 slice_bitcast_fusion.3
  62.7 1.0 collective-permute-done.10
  63.6 0.2 pad_maximum_fusion.45
  63.8 1.4 %collective-permute-start.12 = (f32[2,4,66,1]{3,2,1,0:T(8,128)S(1)}, f32[2,4,66,1]{3,2,1,0:T(8,128)S(1)}, u32[]{:S(2)}, u32[]{:S(2)}) collective-permute-start(f32[2,4,66,1]{3,2,1,0:T(8,128)S(1)} %get-tuple-element.25), channel_id=1, source_target_pairs={{0,2},{2,0},{1,3},{3,1},{4,6},{6,4},{5,7},{7,5},{8,10},{10,8},{9,1... | collective-permute-start | bytes 6344 | tf_op jit(solution)/shard_map/ppermute | solution.py:23
  65.1 0.7 collective-permute-start.13
  65.9 1.0 multiply_reduce_fusion.1
  66.8 3.7 %collective-permute-done.12 = f32[2,4,66,1]{3,2,1,0:T(8,128)S(1)} collective-permute-done((f32[2,4,66,1]{3,2,1,0:T(8,128)S(1)}, f32[2,4,66,1]{3,2,1,0:T(8,128)S(1)}, u32[]{:S(2)}, u32[]{:S(2)}) %collective-permute-start.12) | collective-permute-done | bytes 2144 | tf_op jit(solution)/shard_map/ppermute | solution.py:23
  70.6 3.2 %collective-permute-done.13 = f32[2,4,66,1]{3,2,1,0:T(8,128)S(1)} collective-permute-done((f32[2,4,66,1]{3,2,1,0:T(8,128)S(1)}, f32[2,4,66,1]{3,2,1,0:T(8,128)S(1)}, u32[]{:S(2)}, u32[]{:S(2)}) %collective-permute-start.13) | collective-permute-done | bytes 2144 | tf_op jit(solution)/shard_map/ppermute | solution.py:26
  73.7 0.7 pad_maximum_fusion.2
  74.4 0.1 copy-done.12
  74.4 0.1 slice_bitcast_fusion.1
  74.5 1.0 multiply_reduce_fusion
  75.5 0.0 copy-start.7
  75.5 0.7 add_add_fusion.2
  76.2 0.8 add_add_fusion
  77.0 0.0 all-reduce.3.cloned.1.call-update
  77.0 0.0 copy-start.3
  77.0 0.0 copy-start.9
  77.0 0.0 copy-start.11
  77.0 2.0 %fusion.5 = f32[2,4,64,512]{3,2,1,0:T(8,128)S(1)} fusion(f32[1,4,64,512]{3,2,1,0:T(8,128)S(1)} %get-tuple-element.33, f32[1,4,64,512]{3,2,1,0:T(8,128)S(1)} %get-tuple-element.34, f32[2,4,1,512]{3,2,1,0:T(1,128)S(1)} %collective-permute-done.10, f32[2,4,1,512]{3,2,1,0:T(1,128)S(1)} %collective-permute-done.11, ...), kind=kLoop, calls=%fused_computation.23 | loop fusion | flops 6029312 | bytes 2789504 | tf_op jit(solution)/shard_map/div | solution.py:37
  79.0 2.7 %fusion.32 = (f32[4,64,512]{2,1,0:T(8,128)}, f32[4,64,512]{2,1,0:T(8,128)}) fusion(f32[2,4,64,512]{3,2,1,0:T(8,128)S(1)} %fusion.5, s32[4,64,512]{2,1,0:T(8,128)S(1)} %copy-done.3, f32[]{:T(128)} %bitcast.19, f32[4,64,512]{2,1,0:T(8,128)S(1)} %copy-done.11, f32[2,4,64,512]{3,2,1,0:T(8,128)S(1)} %fusion.17, f32[]{:T(128)} %bitcast.6, ...), kind=kLoop, calls=%fused_computation.93 | loop fusion | flops 1703936 | bytes 4718600 | tf_op jit(solution)/shard_map/sub | solution.py:91
  81.8 15.2 %all-reduce.3.cloned.1.call-done = (f32[64,512]{1,0:T(8,128)}, f32[64,512]{1,0:T(8,128)}, f32[64,512]{1,0:T(8,128)}) async-done(((f32[64,512]{1,0:T(8,128)}, f32[64,512]{1,0:T(8,128)}, f32[64,512]{1,0:T(8,128)}), (f32[64,512]{1,0:T(8,128)}, f32[64,512]{1,0:T(8,128)}, f32[64,512]{1,0:T(8,128)})) %all-reduce.3.cloned.1.call-update) | async-done | bytes 393232 | tf_op jit(solution)/shard_map/psum | solution.py:95
  97.0 1.6 %broadcast_multiply_fusion.2 = f32[64,512]{1,0:T(8,128)} fusion(f32[64,512]{1,0:T(8,128)} %get-tuple-element.14), kind=kLoop, calls=%fused_computation.161 | loop fusion | flops 32768 | bytes 262144 | tf_op jit(solution)/shard_map/mul | solution.py:97
  98.6 1.6 %broadcast_multiply_fusion.1 = f32[64,512]{1,0:T(8,128)} fusion(f32[64,512]{1,0:T(8,128)} %get-tuple-element.15), kind=kLoop, calls=%fused_computation.160 | loop fusion | flops 32768 | bytes 262144 | tf_op jit(solution)/shard_map/mul | solution.py:97
  100.1 1.6 %broadcast_multiply_fusion = f32[64,512]{1,0:T(8,128)} fusion(f32[64,512]{1,0:T(8,128)} %get-tuple-element.16), kind=kLoop, calls=%fused_computation.159 | loop fusion | flops 32768 | bytes 262144 | tf_op jit(solution)/shard_map/mul | solution.py:97
  (26 shorter events, 0.1 us)
Async XLA Ops:
  7.2 12.8 %copy-start = (f32[4,64,512]{2,1,0:T(8,128)S(1)}, f32[4,64,512]{2,1,0:T(8,128)}, u32[]{:S(2)}) copy-start(f32[4,64,512]{2,1,0:T(8,128)} %param.16) | copy-start | bytes 1572868
  7.2 12.8 %copy-start.1 = (f32[4,64,512]{2,1,0:T(8,128)S(1)}, f32[4,64,512]{2,1,0:T(8,128)}, u32[]{:S(2)}) copy-start(f32[4,64,512]{2,1,0:T(8,128)} %param.14) | copy-start | bytes 1572868
  7.2 89.8 %all-reduce.3.cloned.1.call-start = ((), (), s32[]{:S(2)}) async-start(), calls=%async_computation | async-start | bytes 786432 | tf_op jit(solution)/shard_map/psum | solution.py:95
  8.0 14.2 %collective-permute-start.5 = (f32[1,512]{1,0:T(1,128)S(1)}, f32[1,512]{1,0:T(1,128)S(1)}, u32[]{:S(2)}, u32[]{:S(2)}) collective-permute-start(f32[1,512]{1,0:T(1,128)S(1)} %slice.226), channel_id=1, source_target_pairs={{0,4},{4,8},{8,12},{12,0},{1,5},{5,9},{9,13},{13,1},{2,6},{6,10},{... | collective-permute-start | bytes 6152 | tf_op jit(solution)/shard_map/ppermute | solution.py:14
  11.1 11.2 %copy-start.5 = (f32[64,512]{1,0:T(8,128)S(1)}, f32[64,512]{1,0:T(8,128)}, u32[]{:S(2)}) copy-start(f32[64,512]{1,0:T(8,128)} %param.12) | copy-start | bytes 393220
  11.1 22.8 %copy-start.4 = (f32[64,512]{1,0:T(8,128)S(1)}, f32[64,512]{1,0:T(8,128)}, u32[]{:S(2)}) copy-start(f32[64,512]{1,0:T(8,128)} %param.11) | copy-start | bytes 393220
  11.1 22.8 %copy-start.13 = (f32[64,512]{1,0:T(8,128)S(1)}, f32[64,512]{1,0:T(8,128)}, u32[]{:S(2)}) copy-start(f32[64,512]{1,0:T(8,128)} %param.10) | copy-start | bytes 393220
  12.1 7.9 %collective-permute-start.1 = (f32[2,4,1,512]{3,2,1,0:T(1,128)S(1)}, f32[2,4,1,512]{3,2,1,0:T(1,128)S(1)}, u32[]{:S(2)}, u32[]{:S(2)}) collective-permute-start(f32[2,4,1,512]{3,2,1,0:T(1,128)S(1)} %get-tuple-element.39), channel_id=1, source_target_pairs={{4,0},{8,4},{12,8},{0,12},{5,1},{9,5},{13,9},{1,13},{6,2},{10,6},{... | collective-permute-start | bytes 49160 | tf_op jit(solution)/shard_map/ppermute | solution.py:26
  14.2 5.8 %collective-permute-start = (f32[2,4,1,512]{3,2,1,0:T(1,128)S(1)}, f32[2,4,1,512]{3,2,1,0:T(1,128)S(1)}, u32[]{:S(2)}, u32[]{:S(2)}) collective-permute-start(f32[2,4,1,512]{3,2,1,0:T(1,128)S(1)} %get-tuple-element.40), channel_id=1, source_target_pairs={{0,4},{4,8},{8,12},{12,0},{1,5},{5,9},{9,13},{13,1},{2,6},{6,10},{... | collective-permute-start | bytes 49160 | tf_op jit(solution)/shard_map/ppermute | solution.py:23
  15.0 3.9 %collective-permute-start.4 = (f32[64,1]{1,0:T(8,128)S(1)}, f32[64,1]{1,0:T(8,128)S(1)}, u32[]{:S(2)}, u32[]{:S(2)}) collective-permute-start(f32[64,1]{1,0:T(8,128)S(1)} %slice.222), channel_id=1, source_target_pairs={{0,2},{2,0},{1,3},{3,1},{4,6},{6,4},{5,7},{7,5},{8,10},{10,8},{9,1... | collective-permute-start | bytes 776 | tf_op jit(solution)/shard_map/ppermute | solution.py:14
  20.1 10.0 %collective-permute-start.3 = (f32[2,4,66,1]{3,2,1,0:T(8,128)S(1)}, f32[2,4,66,1]{3,2,1,0:T(8,128)S(1)}, u32[]{:S(2)}, u32[]{:S(2)}) collective-permute-start(f32[2,4,66,1]{3,2,1,0:T(8,128)S(1)} %get-tuple-element.29), channel_id=1, source_target_pairs={{2,0},{0,2},{3,1},{1,3},{6,4},{4,6},{7,5},{5,7},{10,8},{8,10},{11,... | collective-permute-start | bytes 6344 | tf_op jit(solution)/shard_map/ppermute | solution.py:26
  21.9 11.9 %collective-permute-start.2 = (f32[2,4,66,1]{3,2,1,0:T(8,128)S(1)}, f32[2,4,66,1]{3,2,1,0:T(8,128)S(1)}, u32[]{:S(2)}, u32[]{:S(2)}) collective-permute-start(f32[2,4,66,1]{3,2,1,0:T(8,128)S(1)} %get-tuple-element.30), channel_id=1, source_target_pairs={{0,2},{2,0},{1,3},{3,1},{4,6},{6,4},{5,7},{7,5},{8,10},{10,8},{9,1... | collective-permute-start | bytes 6344 | tf_op jit(solution)/shard_map/ppermute | solution.py:23
  22.3 33.9 %copy-start.6 = (f32[64,512]{1,0:T(8,128)}, f32[64,512]{1,0:T(8,128)S(1)}, u32[]{:S(2)}) copy-start(f32[64,512]{1,0:T(8,128)S(1)} %pad_maximum_fusion.54) | copy-start | bytes 393220
  22.3 12.5 %copy-start.2 = (s32[4,64,512]{2,1,0:T(8,128)S(1)}, s32[4,64,512]{2,1,0:T(8,128)}, u32[]{:S(2)}) copy-start(s32[4,64,512]{2,1,0:T(8,128)} %param.9) | copy-start | bytes 1572868
  22.3 12.5 %copy-start.8 = (f32[4,64,512]{2,1,0:T(8,128)S(1)}, f32[4,64,512]{2,1,0:T(8,128)}, u32[]{:S(2)}) copy-start(f32[4,64,512]{2,1,0:T(8,128)} %param.15) | copy-start | bytes 1572868
  22.3 12.5 %copy-start.10 = (f32[4,64,512]{2,1,0:T(8,128)S(1)}, f32[4,64,512]{2,1,0:T(8,128)}, u32[]{:S(2)}) copy-start(f32[4,64,512]{2,1,0:T(8,128)} %param.17) | copy-start | bytes 1572868
  35.8 5.0 %collective-permute-start.7 = (f32[2,4,1,512]{3,2,1,0:T(1,128)S(1)}, f32[2,4,1,512]{3,2,1,0:T(1,128)S(1)}, u32[]{:S(2)}, u32[]{:S(2)}) collective-permute-start(f32[2,4,1,512]{3,2,1,0:T(1,128)S(1)} %get-tuple-element.35), channel_id=1, source_target_pairs={{4,0},{8,4},{12,8},{0,12},{5,1},{9,5},{13,9},{1,13},{6,2},{10,6},{... | collective-permute-start | bytes 49160 | tf_op jit(solution)/shard_map/ppermute | solution.py:26
  39.4 5.5 %collective-permute-start.6 = (f32[2,4,1,512]{3,2,1,0:T(1,128)S(1)}, f32[2,4,1,512]{3,2,1,0:T(1,128)S(1)}, u32[]{:S(2)}, u32[]{:S(2)}) collective-permute-start(f32[2,4,1,512]{3,2,1,0:T(1,128)S(1)} %get-tuple-element.36), channel_id=1, source_target_pairs={{0,4},{4,8},{8,12},{12,0},{1,5},{5,9},{9,13},{13,1},{2,6},{6,10},{... | collective-permute-start | bytes 49160 | tf_op jit(solution)/shard_map/ppermute | solution.py:23
  45.1 7.9 %collective-permute-start.9 = (f32[2,4,66,1]{3,2,1,0:T(8,128)S(1)}, f32[2,4,66,1]{3,2,1,0:T(8,128)S(1)}, u32[]{:S(2)}, u32[]{:S(2)}) collective-permute-start(f32[2,4,66,1]{3,2,1,0:T(8,128)S(1)} %get-tuple-element.27), channel_id=1, source_target_pairs={{2,0},{0,2},{3,1},{1,3},{6,4},{4,6},{7,5},{5,7},{10,8},{8,10},{11,... | collective-permute-start | bytes 6344 | tf_op jit(solution)/shard_map/ppermute | solution.py:26
  46.6 9.5 %collective-permute-start.8 = (f32[2,4,66,1]{3,2,1,0:T(8,128)S(1)}, f32[2,4,66,1]{3,2,1,0:T(8,128)S(1)}, u32[]{:S(2)}, u32[]{:S(2)}) collective-permute-start(f32[2,4,66,1]{3,2,1,0:T(8,128)S(1)} %get-tuple-element.28), channel_id=1, source_target_pairs={{0,2},{2,0},{1,3},{3,1},{4,6},{6,4},{5,7},{7,5},{8,10},{10,8},{9,1... | collective-permute-start | bytes 6344 | tf_op jit(solution)/shard_map/ppermute | solution.py:23
  58.0 5.6 %collective-permute-start.10 = (f32[2,4,1,512]{3,2,1,0:T(1,128)S(1)}, f32[2,4,1,512]{3,2,1,0:T(1,128)S(1)}, u32[]{:S(2)}, u32[]{:S(2)}) collective-permute-start(f32[2,4,1,512]{3,2,1,0:T(1,128)S(1)} %get-tuple-element.31), channel_id=1, source_target_pairs={{0,4},{4,8},{8,12},{12,0},{1,5},{5,9},{9,13},{13,1},{2,6},{6,10},{... | collective-permute-start | bytes 49160 | tf_op jit(solution)/shard_map/ppermute | solution.py:23
  58.1 5.5 %collective-permute-start.11 = (f32[2,4,1,512]{3,2,1,0:T(1,128)S(1)}, f32[2,4,1,512]{3,2,1,0:T(1,128)S(1)}, u32[]{:S(2)}, u32[]{:S(2)}) collective-permute-start(f32[2,4,1,512]{3,2,1,0:T(1,128)S(1)} %get-tuple-element.32), channel_id=1, source_target_pairs={{4,0},{8,4},{12,8},{0,12},{5,1},{9,5},{13,9},{1,13},{6,2},{10,6},{... | collective-permute-start | bytes 49160 | tf_op jit(solution)/shard_map/ppermute | solution.py:26
  63.8 6.8 %collective-permute-start.12 = (f32[2,4,66,1]{3,2,1,0:T(8,128)S(1)}, f32[2,4,66,1]{3,2,1,0:T(8,128)S(1)}, u32[]{:S(2)}, u32[]{:S(2)}) collective-permute-start(f32[2,4,66,1]{3,2,1,0:T(8,128)S(1)} %get-tuple-element.25), channel_id=1, source_target_pairs={{0,2},{2,0},{1,3},{3,1},{4,6},{6,4},{5,7},{7,5},{8,10},{10,8},{9,1... | collective-permute-start | bytes 6344 | tf_op jit(solution)/shard_map/ppermute | solution.py:23
  65.1 8.6 %collective-permute-start.13 = (f32[2,4,66,1]{3,2,1,0:T(8,128)S(1)}, f32[2,4,66,1]{3,2,1,0:T(8,128)S(1)}, u32[]{:S(2)}, u32[]{:S(2)}) collective-permute-start(f32[2,4,66,1]{3,2,1,0:T(8,128)S(1)} %get-tuple-element.26), channel_id=1, source_target_pairs={{2,0},{0,2},{3,1},{1,3},{6,4},{4,6},{7,5},{5,7},{10,8},{8,10},{11,... | collective-permute-start | bytes 6344 | tf_op jit(solution)/shard_map/ppermute | solution.py:26
  73.7 0.7 copy-start.12
  75.5 1.5 %copy-start.7 = (f32[64,512]{1,0:T(8,128)S(1)}, f32[64,512]{1,0:T(8,128)}, u32[]{:S(2)}) copy-start(f32[64,512]{1,0:T(8,128)} %copy-done.6) | copy-start | bytes 393220
  77.0 2.0 %copy-start.3 = (s32[4,64,512]{2,1,0:T(8,128)S(1)}, s32[4,64,512]{2,1,0:T(8,128)}, u32[]{:S(2)}) copy-start(s32[4,64,512]{2,1,0:T(8,128)} %param.9) | copy-start | bytes 1572868
  77.0 2.0 %copy-start.9 = (f32[4,64,512]{2,1,0:T(8,128)S(1)}, f32[4,64,512]{2,1,0:T(8,128)}, u32[]{:S(2)}) copy-start(f32[4,64,512]{2,1,0:T(8,128)} %param.15) | copy-start | bytes 1572868
  77.0 2.0 %copy-start.11 = (f32[4,64,512]{2,1,0:T(8,128)S(1)}, f32[4,64,512]{2,1,0:T(8,128)}, u32[]{:S(2)}) copy-start(f32[4,64,512]{2,1,0:T(8,128)} %param.17) | copy-start | bytes 1572868
Sparse Core Ops, SparseCore 0:
  77.1 19.8 all-reduce.2
where the time goes:
time: 109 us
  waiting for transfers between devices  48.3 us (44%)
  other arithmetic  21.9 us (20%)
  starting transfers between devices  20.6 us (19%)
  between operations  14.3 us (13%)
  local copies, waits for them, and re-layouts  3.41 us (3%)
    ppermute x6, waiting for transfers between devices, with_halo(): lax.ppermute(lax.slice_in_dim(block, 0, width, axis=dim), axis, backward)  16.6 us
    ppermute x6, waiting for transfers between devices, with_halo(): lax.ppermute(lax.slice_in_dim(block, block.shape[dim] - width, None, axis...  15.6 us
    psum x1, waiting for transfers between devices, local(): lax.psum((right_acc, down_acc, site_acc), 'probe')  15.2 us
    ppermute x6, starting transfers between devices, with_halo(): lax.ppermute(lax.slice_in_dim(block, 0, width, axis=dim), axis, backward)  13.6 us
    ppermute x2, starting transfers between devices, shifted(): return lax.ppermute(x, axis, [(i, (i + by) % size) for i in range(size)])  4.72 us
    div x3, other arithmetic, stencil(): return total / spectral_half  3.74 us
    another operation x5, other arithmetic, local(): jnp.stack([current, adjoint])  2.97 us
    reduce_sum x3, other arithmetic, bond_terms(): site_term = jnp.sum(adj_centre * fwd_centre, axis=0)  2.87 us
  transfers between devices with their start and end apart: 15, of which 11 were waited for; matrix products, arithmetic and copies ran while one was open for 11% of the time, Pallas kernels for 0%

commit v1 on v0

v1 whole, which is shorter than its diff:
```python
import jax
import jax.numpy as jnp
from jax import lax
from jax.experimental import pallas as pl
from jax.experimental.pallas import tpu as pltpu
from jax.sharding import PartitionSpec as P

STEPS = 3
LANES = 128
TILE = 8
spectral_half = 7.5
SCALE = 2.0 / spectral_half

WIDE = 2 * STEPS
VMEM_LIMIT = 48 * 1024 * 1024


def shifted(x, axis, by):
    size = lax.axis_size(axis)
    return lax.ppermute(x, axis, [(i, (i + by) % size) for i in range(size)])


def lane_of(shape):
    return lax.broadcasted_iota(jnp.int32, shape, len(shape) - 1)


def turned(x, by):
    return pltpu.roll(x, by % x.shape[1], 1)


def edge_kernel(weights, *refs):
    *sources, out = refs
    lows, highs = sources[0::2], sources[1::2]
    probes = lows[0].shape[0]
    span = WIDE * 2 * probes
    lane = lane_of(out.shape)

    def joined(at, probe=None):
        if probe is None:
            return jnp.where(lane < LANES // 2, lows[at][...], highs[at][...])
        return jnp.where(lane < LANES // 2, lows[at][probe], highs[at][probe])

    packed = jnp.zeros(out.shape, jnp.float32)

    def put(packed, x, start):
        return jnp.where((lane >= start) & (lane < start + WIDE), turned(x, start + STEPS), packed)

    first, last = LANES - STEPS, STEPS - 1
    for probe in range(probes):
        group = WIDE * probe
        sign = joined(4, probe).astype(jnp.float32)
        base = weights[0] * sign - joined(2, probe)
        base = jnp.where(lane == first, turned(sign, -2), jnp.where(lane == last, turned(sign, 2), base))
        packed = put(packed, joined(0, probe), group)
        packed = put(packed, base, span + group)
        group = WIDE * (probes + probe)
        base = jnp.where((lane == first) | (lane == last), 0.0, -joined(3, probe))
        packed = put(packed, joined(1, probe), group)
        packed = put(packed, base, span + group)
    for at in range(3):
        packed = put(packed, joined(5 + at), 2 * span + WIDE * at)
    out[...] = packed


def strips(own, left, right, span):
    lane = lane_of(own.shape)
    inner = lax.rem(lane, WIDE) < STEPS
    low = jnp.where(inner, left, own)
    high = jnp.where(inner, own, right)
    below = lane < span
    field = jnp.where(below, low, turned(high, span))
    base = jnp.where(below, turned(low, -span), high)
    coefficients = []
    for at in range(3):
        start = 2 * span + WIDE * at
        x = jnp.where(
            lane < WIDE,
            turned(low, -start),
            jnp.where((lane >= span) & (lane < span + WIDE), turned(high, span - start), 0.0),
        )
        reach = WIDE
        while reach < span:
            x = x + turned(x, reach)
            reach *= 2
        coefficients.append(x * SCALE)
    return field, base, coefficients


def column_of(row, groups, at):
    shape = (groups, LANES)
    wanted = WIDE * lax.broadcasted_iota(jnp.int32, shape, 0) + at
    return jnp.sum(jnp.where(lane_of(shape) == wanted, row, 0.0), axis=1, keepdims=True)


def sideways(x, hop, strip_row, hop_row, span):
    groups, cols = x.shape
    lane = lane_of(x.shape)
    before = jnp.where(lane == 0, column_of(strip_row, groups, STEPS - 1), turned(x, 1))
    after = jnp.where(lane == cols - 1, column_of(strip_row, groups, span + STEPS), turned(x, -1))
    hop = jnp.broadcast_to(hop, x.shape)
    hop_before = jnp.where(lane == 0, hop_row[:, STEPS - 1 : STEPS], turned(hop, 1))
    return hop * after + hop_before * before


def edge_rows(weights, refs, rows, out):
    adj, fwd, adj_next, fwd_next, signs, onsite, hop_right, hop_down, own, left, right = refs
    edge, second, third = rows
    probes = adj.shape[0]
    groups = 2 * probes
    span = WIDE * groups

    def pair(top, bottom, at):
        return jnp.concatenate([top[:, at, :], bottom[:, at, :]], axis=0)

    def sign_pair(weight, at):
        sign = weight * signs[:, at, :].astype(jnp.float32)
        return jnp.concatenate([sign, jnp.zeros_like(sign)], axis=0)

    def bond(at, other):
        return min(at, other)

    def scaled(ref, at):
        return ref[at : at + 1, :] * SCALE

    field, base, (s_on, s_right, s_down) = strips(own[...], left[...], right[...], span)
    x_edge, x_second, x_third = (pair(adj, fwd, at) for at in rows)
    one = (
        sign_pair(weights[0], second)
        - pair(adj_next, fwd_next, second)
        + scaled(onsite, second) * x_second
        + sideways(
            x_second,
            scaled(hop_right, second),
            field[second : second + 1, :],
            s_right[second : second + 1, :],
            span,
        )
        + scaled(hop_down, bond(edge, second)) * x_edge
        + scaled(hop_down, bond(second, third)) * x_third
    )
    part_one = (
        sign_pair(weights[0], edge)
        - pair(adj_next, fwd_next, edge)
        + scaled(onsite, edge) * x_edge
        + sideways(
            x_edge, scaled(hop_right, edge), field[edge : edge + 1, :], s_right[edge : edge + 1, :], span
        )
        + scaled(hop_down, bond(edge, second)) * x_second
    )
    part_two = sign_pair(weights[1], edge) - x_edge + scaled(hop_down, bond(edge, second)) * one
    level = (
        base
        + s_on * field
        + s_right * turned(field, -1)
        + turned(s_right, 1) * turned(field, 1)
    )
    down = bond(edge, second)
    strip_one = level[edge : edge + 1, :] + s_down[down : down + 1, :] * field[second : second + 1, :]
    strip_row = jnp.concatenate(
        [field[edge : edge + 1, :], strip_one, s_down[edge : edge + 1, :], s_right[edge : edge + 1, :]], axis=1
    )
    out[0:groups, :] = x_edge
    out[groups : 2 * groups, :] = part_one
    out[2 * groups : 3 * groups, :] = part_two
    at = 3 * groups
    out[at : at + 1, :] = scaled(onsite, edge)
    out[at + 1 : at + 2, :] = scaled(hop_right, edge)
    out[at + 2 : at + 3, :] = scaled(hop_down, edge)
    out[at + 3 : at + 4, 0 : 4 * LANES] = strip_row
    out[at + 4 : at + TILE, :] = jnp.zeros((TILE - 4, out.shape[1]), jnp.float32)


def rows_kernel(weights, *refs):
    *sources, first_out, last_out = refs
    edge_rows(weights, sources[0::2], (0, 1, 2), first_out)
    edge_rows(weights, sources[1::2], (TILE - 1, TILE - 2, TILE - 3), last_out)


def main_kernel(
    weights,
    adj,
    fwd,
    adj_next,
    fwd_next,
    signs,
    onsite,
    hop_right,
    hop_down,
    own,
    left,
    right,
    above,
    below,
    forces,
    fwd_out,
    adj_out,
    x,
    strip,
    strip_base,
    strip_hops,
    hops,
    halo,
):
    probes, rows, cols = adj.shape
    groups = 2 * probes
    span = WIDE * groups
    tiles = cols // LANES
    tall = rows + 2 * TILE
    top, bottom = TILE, TILE + rows
    lane = lane_of((TILE, LANES))
    misc = 3 * groups

    def lanes(c):
        return pl.ds(c * LANES, LANES)

    def fields_at(step, c, row):
        return (step, pl.ds(c * tall + row, groups, stride=tiles * tall), slice(None))

    field, base, (s_on, s_right, s_down) = strips(own[...], left[...], right[...], span)
    below_span = lane_of(base.shape) < span
    sign_strip = jnp.where(below_span, turned(base, 2), turned(base, -2))
    corner_above = above[misc + 3 : misc + 4, 0 : 4 * LANES]
    corner_below = below[misc + 3 : misc + 4, 0 : 4 * LANES]
    strip[0, top:bottom, :] = field
    strip[0, top - 1 : top, :] = corner_above[:, :LANES]
    strip[0, bottom : bottom + 1, :] = corner_below[:, :LANES]
    strip_base[0] = base
    strip_base[1] = weights[1] * sign_strip - field
    strip_hops[0, top:bottom, :] = s_on
    strip_hops[1, top:bottom, :] = s_right
    strip_hops[2, top:bottom, :] = s_down
    strip_hops[2, top - 1 : top, :] = corner_above[:, 2 * LANES : 3 * LANES]
    edge_above = corner_above[:, 2 * LANES : 3 * LANES]
    edge_below = s_down[rows - 1 : rows, :]
    one_above = corner_above[:, LANES : 2 * LANES] + edge_above * field[0:1, :]
    one_below = corner_below[:, LANES : 2 * LANES] + edge_below * field[rows - 1 : rows, :]
    strip[1, top - 1 : top, :] = one_above
    strip[1, bottom : bottom + 1, :] = one_below

    hop_before = turned(s_right, -(STEPS - 1))
    wide_lane = lane_of((rows, LANES))
    for c in range(tiles):
        hop = hop_right[:, lanes(c)] * SCALE
        hop_turned = turned(hop, 1)
        hops[0, c, top:bottom, :] = onsite[:, lanes(c)] * SCALE
        hops[1, c, top:bottom, :] = hop
        hops[2, c, top:bottom, :] = jnp.where(wide_lane == 0, hop_before, hop_turned)
        hops[3, c, top:bottom, :] = hop_down[:, lanes(c)] * SCALE
        hops[3, c, top - 1 : top, :] = above[misc + 2 : misc + 3, lanes(c)]
        hop_before = hop_turned

    for g in range(groups):
        source = adj if g < probes else fwd
        for c in range(tiles):
            x[0, pl.ds((g * tiles + c) * tall + top, rows), :] = source[g % probes, :, lanes(c)]
    for c in range(tiles):
        x[fields_at(0, c, top - 1)] = above[0:groups, lanes(c)]
        x[fields_at(0, c, bottom)] = below[0:groups, lanes(c)]

    def set_halo(step):
        now = strip[step, top:bottom, :]
        wide = lane_of(now.shape)
        picked = (lax.rem(wide, WIDE) == STEPS - 1) & (wide < span)
        halo[...] = jnp.where(picked, now, turned(now, -(span + 2)))

    def strip_step(step):
        now = strip[step, top:bottom, :]
        s_right = strip_hops[1, top:bottom, :]
        strip[step + 1, top:bottom, :] = (
            strip_base[step]
            + strip_hops[0, top:bottom, :] * now
            + s_right * turned(now, -1)
            + turned(s_right, 1) * turned(now, 1)
            + strip_hops[2, top:bottom, :] * strip[step, top + 1 : bottom + 1, :]
            + strip_hops[2, top - 1 : bottom - 1, :] * strip[step, top - 1 : bottom - 1, :]
        )

    def gathered(step, row):
        return jnp.concatenate([x[fields_at(step, c, row)] for c in range(tiles)], axis=1)

    def scattered(step, row, value):
        for c in range(tiles):
            x[fields_at(step, c, row)] = value[:, c * LANES : (c + 1) * LANES]

    hop_above = above[misc + 2 : misc + 3, :]
    hop_below = hop_down[rows - 1 : rows, :] * SCALE

    def beyond_one():
        scattered(1, top - 1, above[groups : 2 * groups, :] + hop_above * gathered(0, top))
        scattered(1, bottom, below[groups : 2 * groups, :] + hop_below * gathered(0, bottom - 1))

    def beyond_two():
        for source, hop, corner, strip_row, edge, inside in (
            (above, hop_above, corner_above, one_above, top - 1, top),
            (below, hop_below, corner_below, one_below, bottom, bottom - 1),
        ):
            now = gathered(1, edge)
            value = (
                source[2 * groups : 3 * groups, :]
                + source[misc : misc + 1, :] * now
                + sideways(now, source[misc + 1 : misc + 2, :], strip_row, corner[:, 3 * LANES :], span)
                + hop * gathered(1, inside)
            )
            scattered(2, edge, value)

    def step_of(step):
        def body(t, carry):
            row = pl.multiple_of(t * TILE, TILE)

            def load(at, g, c, by):
                return x[at, pl.ds((g * tiles + c) * tall + top + by + row, TILE), :]

            def hop(kind, c, by=0):
                return hops[kind, c, pl.ds(top + by + row, TILE), :]

            beside = halo[pl.ds(row, TILE), :]
            right_sum = [None] * tiles
            down_sum = [None] * tiles
            site_sum = [None] * tiles
            for p in range(probes):
                kept = []
                for f in range(2):
                    g = f * probes + p
                    outer = turned(beside, -(WIDE * g + STEPS - 1))
                    centre = [load(step, g, c, 0) for c in range(tiles)]
                    low = [turned(v, 1) for v in centre]
                    high = [turned(v, -1) for v in centre]
                    before = [jnp.where(lane == 0, (low[c - 1] if c else outer), low[c]) for c in range(tiles)]
                    after = [
                        jnp.where(lane == LANES - 1, (high[c + 1] if c < tiles - 1 else outer), high[c])
                        for c in range(tiles)
                    ]
                    under = [load(step, g, c, 1) for c in range(tiles)]
                    for c in range(tiles):
                        if step > 0:
                            previous = load(step - 1, g, c, 0)
                        else:
                            previous = (fwd_next if f else adj_next)[p, pl.ds(row, TILE), lanes(c)]
                        total = hop(0, c) * centre[c] - previous
                        total = total + hop(1, c) * after[c]
                        total = total + hop(2, c) * before[c]
                        total = total + hop(3, c) * under[c]
                        total = total + hop(3, c, -1) * load(step, g, c, -1)
                        if f == 0:
                            sign = signs[p, pl.ds(row, TILE), lanes(c)].astype(jnp.float32)
                            total = total + weights[step] * sign
                        if step < STEPS - 1:
                            x[step + 1, pl.ds((g * tiles + c) * tall + top + row, TILE), :] = total
                        else:
                            (fwd_out if f else adj_out)[p, pl.ds(row, TILE), lanes(c)] = total
                    kept.append((centre, after, under))
                (a_centre, a_after, a_under), (q_centre, q_after, q_under) = kept
                for c in range(tiles):
                    r_term = a_centre[c] * q_after[c] + a_after[c] * q_centre[c]
                    d_term = a_centre[c] * q_under[c] + a_under[c] * q_centre[c]
                    s_term = a_centre[c] * q_centre[c]
                    right_sum[c] = r_term if p == 0 else right_sum[c] + r_term
                    down_sum[c] = d_term if p == 0 else down_sum[c] + d_term
                    site_sum[c] = s_term if p == 0 else site_sum[c] + s_term
            for c in range(tiles):
                for kind, term in enumerate((right_sum[c], down_sum[c], site_sum[c])):
                    spot = (kind, pl.ds(row, TILE), lanes(c))
                    forces[spot] = term if step == 0 else forces[spot] + term
            return carry

        lax.fori_loop(0, rows // TILE, body, 0)

    set_halo(0)
    step_of(0)
    strip_step(0)
    beyond_one()
    set_halo(1)
    step_of(1)
    strip_step(1)
    beyond_two()
    set_halo(2)
    step_of(2)


def sum_kernel(mine, other, right_out, down_out, site_out):
    for at, out in enumerate((right_out, down_out, site_out)):
        out[...] = (mine[at] + other[at]) * SCALE


def local(
    signs,
    onsite,
    hop_right,
    hop_down,
    moment_weights,
    forward_now,
    forward_next,
    adjoint_now,
    adjoint_next,
):
    probes, rows, cols = forward_now.shape
    groups = 2 * probes
    f32 = jnp.float32
    fields = (adjoint_now, forward_now, adjoint_next, forward_next, signs)
    lattice = (onsite, hop_right, hop_down)
    in_smem = pl.BlockSpec(memory_space=pltpu.SMEM)
    params = pltpu.CompilerParams(vmem_limit_bytes=VMEM_LIMIT)

    last = cols // LANES - 1
    field_specs = [pl.BlockSpec((probes, rows, LANES), lambda i, c=c: (0, 0, c)) for c in (0, last)]
    lattice_specs = [pl.BlockSpec((rows, LANES), lambda i, c=c: (0, c)) for c in (0, last)]
    packed = pl.pallas_call(
        edge_kernel,
        grid=(1,),
        out_shape=jax.ShapeDtypeStruct((rows, LANES), f32),
        in_specs=[in_smem] + field_specs * len(fields) + lattice_specs * len(lattice),
        out_specs=pl.BlockSpec((rows, LANES), lambda i: (0, 0)),
        compiler_params=params,
        name="edge_columns",
    )(moment_weights, *(v for v in fields + lattice for _ in range(2)))
    left = shifted(packed, "col", 1)
    right = left if lax.axis_size("col") == 2 else shifted(packed, "col", -1)

    last = rows // TILE - 1
    field_specs = [pl.BlockSpec((probes, TILE, cols), lambda i, r=r: (0, r, 0)) for r in (0, last)]
    lattice_specs = [pl.BlockSpec((TILE, cols), lambda i, r=r: (r, 0)) for r in (0, last)]
    strip_specs = [pl.BlockSpec((TILE, LANES), lambda i, r=r: (r, 0)) for r in (0, last)]
    message = jax.ShapeDtypeStruct((3 * groups + TILE, cols), f32)
    whole = pl.BlockSpec(message.shape, lambda i: (0, 0))
    first_rows, last_rows = pl.pallas_call(
        rows_kernel,
        grid=(1,),
        out_shape=(message, message),
        in_specs=[in_smem] + field_specs * len(fields) + lattice_specs * len(lattice) + strip_specs * 3,
        out_specs=(whole, whole),
        compiler_params=params,
        name="edge_rows",
    )(moment_weights, *(v for v in fields + lattice + (packed, left, right) for _ in range(2)))
    above = shifted(last_rows, "strip", 1)
    below = shifted(first_rows, "strip", -1)

    tiles = cols // LANES
    tall = rows + 2 * TILE
    in_vmem = pl.BlockSpec(memory_space=pltpu.VMEM)
    forces, forward_out, adjoint_out = pl.pallas_call(
        main_kernel,
        out_shape=(
            jax.ShapeDtypeStruct((3, rows, cols), f32),
            jax.ShapeDtypeStruct(forward_now.shape, f32),
            jax.ShapeDtypeStruct(forward_now.shape, f32),
        ),
        in_specs=[in_smem] + [in_vmem] * 13,
        out_specs=(in_vmem,) * 3,
        scratch_shapes=[
            pltpu.VMEM((STEPS, groups * tiles * tall, LANES), f32),
            pltpu.VMEM((STEPS, tall, LANES), f32),
            pltpu.VMEM((2, rows, LANES), f32),
            pltpu.VMEM((3, tall, LANES), f32),
            pltpu.VMEM((4, tiles, tall, LANES), f32),
            pltpu.VMEM((rows, LANES), f32),
        ],
        compiler_params=params,
        name="steps",
    )(moment_weights, *fields, *lattice, packed, left, right, above, below)

    other = shifted(forces, "probe", 1)
    right_force, down_force, site_force = pl.pallas_call(
        sum_kernel,
        out_shape=(jax.ShapeDtypeStruct((rows, cols), f32),) * 3,
        in_specs=[in_vmem] * 2,
        out_specs=(in_vmem,) * 3,
        compiler_params=params,
        name="force_sums",
    )(forces, other)
    return right_force, down_force, site_force, forward_out, adjoint_out


def solution(mesh):
    placed = (
        P(("parts", "probe"), "strip", "col"),
        P(("parts", "strip"), "col"),
        P(("parts", "strip"), "col"),
        P(("parts", "strip"), "col"),
        P(),
        P(("parts", "probe"), "strip", "col"),
        P(("parts", "probe"), "strip", "col"),
        P(("parts", "probe"), "strip", "col"),
        P(("parts", "probe"), "strip", "col"),
    )
    return jax.shard_map(
        local,
        mesh=mesh,
        in_specs=placed,
        out_specs=(
            P(("parts", "strip"), "col"),
            P(("parts", "strip"), "col"),
            P(("parts", "strip"), "col"),
            P(("parts", "probe"), "strip", "col"),
            P(("parts", "probe"), "strip", "col"),
        ),
        check_vma=False,
    )
```

time: 109 us -> 32.4 us (0.30)
  waiting for transfers between devices: 48.3 us -> 6.49 us
  other arithmetic: 21.9 us -> 0 us
  between operations: 14.3 us -> 0.67 us
  starting transfers between devices: 20.6 us -> 7.26 us
  Pallas kernels: 0 us -> 9.05 us
  local copies, waits for them, and re-layouts: 3.41 us -> 8.56 us
    ppermute x12 -> x0, waiting for transfers between devices: 32.2 us -> none  [the longest x6 16.6 us: with_halo(): lax.ppermute(lax.slice_in_dim(block, 0, width, axis=dim), axis, backward)]
    ppermute x12 -> x0, starting transfers between devices: 15.8 us -> none  [the longest x6 13.6 us: with_halo(): lax.ppermute(lax.slice_in_dim(block, 0, width, axis=dim), axis, backward)]
    psum x1 -> x0, waiting for transfers between devices: 15.2 us -> none  [local(): lax.psum((right_acc, down_acc, site_acc), 'probe')]
    pallas_call x0 -> x4, Pallas kernels: none -> 9.05 us  [the longest x1 6.32 us: local(): pl.pallas_call(main_kernel, out_shape=(jax.ShapeDtypeStruct((3, rows, col...]
    unnamed x28 -> x18, local copies, waits for them, and re-layouts: 0.13 us -> 8.56 us
    ppermute x2 -> x4, waiting for transfers between devices: 0.87 us -> 6.49 us  [shifted(): return lax.ppermute(x, axis, [(i, (i + by) % size) for i in range(size)])]
    mul x3 -> x0, other arithmetic: 4.71 us -> none  [the longest x1 1.57 us: local(): right_sum * factor]
    div x3 -> x0, other arithmetic: 3.74 us -> none  [stencil(): return total / spectral_half]
  transfers between devices with their start and end apart: 15 -> 4, of which waited for: 11 -> 4; matrix products, arithmetic and copies ran while one was open for 11% -> 0% of each run, Pallas kernels for 0% -> 0%
where the time goes in v1:
time: 32.4 us; the launch traced here: 32 us
  Pallas kernels  9.05 us (28%)
  local copies, waits for them, and re-layouts  8.56 us (26%)
  starting transfers between devices  7.26 us (22%)
  waiting for transfers between devices  6.49 us (20%)
  between operations  0.67 us (2%)
    unnamed x18, local copies, waits for them, and re-layouts  8.56 us
    ppermute x4, starting transfers between devices, shifted(): return lax.ppermute(x, axis, [(i, (i + by) % size) for i in range(size)])  7.26 us
    ppermute x4, waiting for transfers between devices, shifted(): return lax.ppermute(x, axis, [(i, (i + by) % size) for i in range(size)])  6.49 us
    pallas_call x1, Pallas kernels, local(): pl.pallas_call(main_kernel, out_shape=(jax.ShapeDtypeStruct((3, rows, col...  6.32 us
    pallas_call x1, Pallas kernels, local(): pl.pallas_call(edge_kernel, grid=(1,), out_shape=jax.ShapeDtypeStruct((ro...  0.98 us
    pallas_call x1, Pallas kernels, local(): pl.pallas_call(rows_kernel, grid=(1,), out_shape=(message, message), in_s...  0.96 us
    pallas_call x1, Pallas kernels, local(): pl.pallas_call(sum_kernel, out_shape=(jax.ShapeDtypeStruct((rows, cols),...  0.79 us
  transfers between devices with their start and end apart: 4, of which 4 were waited for; matrix products, arithmetic and copies ran while one was open for 0% of the time, Pallas kernels for 0%

profile of v1, /device:TPU:0, one launch (start us, length us, event | category | flops | bytes accessed | tf_op | source)
XLA Modules:
  0.0 32.0 jit_solution(3127794066637361636)
XLA Ops:
  0.6 0.0 copy-start
  0.6 1.0 %copy-done = f32[4,64,512]{2,1,0:T(8,128)S(1)} copy-done((f32[4,64,512]{2,1,0:T(8,128)S(1)}, f32[4,64,512]{2,1,0:T(8,128)}, u32[]{:S(2)}) %copy-start) | copy-done | bytes 524312
  1.7 0.0 copy-start.1
  1.7 1.0 %copy-done.1 = f32[4,64,512]{2,1,0:T(8,128)S(1)} copy-done((f32[4,64,512]{2,1,0:T(8,128)S(1)}, f32[4,64,512]{2,1,0:T(8,128)}, u32[]{:S(2)}) %copy-start.1) | copy-done | bytes 524312
  2.7 0.0 copy-start.2
  2.7 1.0 %copy-done.2 = f32[4,64,512]{2,1,0:T(8,128)S(1)} copy-done((f32[4,64,512]{2,1,0:T(8,128)S(1)}, f32[4,64,512]{2,1,0:T(8,128)}, u32[]{:S(2)}) %copy-start.2) | copy-done | bytes 524312
  3.8 0.0 copy-start.3
  3.8 1.0 %copy-done.3 = f32[4,64,512]{2,1,0:T(8,128)S(1)} copy-done((f32[4,64,512]{2,1,0:T(8,128)S(1)}, f32[4,64,512]{2,1,0:T(8,128)}, u32[]{:S(2)}) %copy-start.3) | copy-done | bytes 524312
  4.8 0.0 copy-start.4
  4.8 1.0 %copy-done.4 = s32[4,64,512]{2,1,0:T(8,128)S(1)} copy-done((s32[4,64,512]{2,1,0:T(8,128)S(1)}, s32[4,64,512]{2,1,0:T(8,128)}, u32[]{:S(2)}) %copy-start.4) | copy-done | bytes 524312
  5.8 0.0 copy-start.5
  5.8 0.9 %copy-done.5 = f32[64,512]{1,0:T(8,128)S(1)} copy-done((f32[64,512]{1,0:T(8,128)S(1)}, f32[64,512]{1,0:T(8,128)}, u32[]{:S(2)}) %copy-start.5) | copy-done | bytes 131096
  6.8 0.0 copy-start.6
  6.8 0.9 %copy-done.6 = f32[64,512]{1,0:T(8,128)S(1)} copy-done((f32[64,512]{1,0:T(8,128)S(1)}, f32[64,512]{1,0:T(8,128)}, u32[]{:S(2)}) %copy-start.6) | copy-done | bytes 131096
  7.7 0.0 copy-start.7
  7.7 0.9 %copy-done.7 = f32[64,512]{1,0:T(8,128)S(1)} copy-done((f32[64,512]{1,0:T(8,128)S(1)}, f32[64,512]{1,0:T(8,128)}, u32[]{:S(2)}) %copy-start.7) | copy-done | bytes 131096
  8.6 0.0 copy-start.8
  8.6 0.7 %copy-done.8 = f32[3]{0:T(128)S(1)} copy-done((f32[3]{0:T(128)S(1)}, f32[3]{0:T(128)}, u32[]{:S(2)}) %copy-start.8) | copy-done | bytes 36
  9.2 1.0 %edge_columns.1.refs_16_.refs_17_.own = f32[64,128]{1,0:T(8,128)S(1)} custom-call(f32[3]{0:T(128)S(1)} %copy-done.8, f32[4,64,512]{2,1,0:T(8,128)S(1)} %copy-done, f32[4,64,512]{2,1,0:T(8,128)S(1)} %copy-done, f32[4,64,512]{2,1,0:T(8,128)S(1)} %copy-done.1, f32[4,64,512]{2,1,0:T(8,128)S(1)} %copy-done.1, f32[4,64,512]{2,1,0:T(8,128)S(1)} %copy-done.2, ...), custom_call_target="tpu_custom_call" | custom-call | tf_op jit(solution)/shard_map/edge_columns/pallas_call | solution.py:407
  10.2 3.0 %collective-permute-start = (f32[64,128]{1,0:T(8,128)S(1)}, f32[64,128]{1,0:T(8,128)S(1)}, u32[]{:S(2)}, u32[]{:S(2)}) collective-permute-start(f32[64,128]{1,0:T(8,128)S(1)} %edge_columns.1.refs_16_.refs_17_.own), channel_id=1, source_target_pairs={{0,2},{2,0},{1,3},{3,1},{4,6},{6,4},{5,7},{7,5},{8,10},{10,8},{9,1... | collective-permute-start | bytes 98312 | tf_op jit(solution)/shard_map/ppermute | solution.py:20
  13.2 1.9 %collective-permute-done.refs_18_.refs_19_.refs_20_.refs_21_.left.right = f32[64,128]{1,0:T(8,128)S(1)} collective-permute-done((f32[64,128]{1,0:T(8,128)S(1)}, f32[64,128]{1,0:T(8,128)S(1)}, u32[]{:S(2)}, u32[]{:S(2)}) %collective-permute-start) | collective-permute-done | bytes 32800 | tf_op jit(solution)/shard_map/ppermute | solution.py:20
  15.1 1.0 %edge_rows.1 = (f32[32,512]{1,0:T(8,128)S(1)}, f32[32,512]{1,0:T(8,128)S(1)}) custom-call(f32[3]{0:T(128)S(1)} %copy-done.8, f32[4,64,512]{2,1,0:T(8,128)S(1)} %copy-done, f32[4,64,512]{2,1,0:T(8,128)S(1)} %copy-done, f32[4,64,512]{2,1,0:T(8,128)S(1)} %copy-done.1, f32[4,64,512]{2,1,0:T(8,128)S(1)} %copy-done.1, f32[4,64,512]{2,1,0:T(8,128)S(1)} %copy-done.2, ...), custom_call_target="tpu_custom_call" | custom-call | tf_op jit(solution)/shard_map/edge_rows/pallas_call | solution.py:425
  16.1 2.2 %collective-permute-start.1 = (f32[32,512]{1,0:T(8,128)S(1)}, f32[32,512]{1,0:T(8,128)S(1)}, u32[]{:S(2)}, u32[]{:S(2)}) collective-permute-start(f32[32,512]{1,0:T(8,128)S(1)} %get-tuple-element.13), channel_id=1, source_target_pairs={{0,4},{4,8},{8,12},{12,0},{1,5},{5,9},{9,13},{13,1},{2,6},{6,10},{... | collective-permute-start | bytes 196616 | tf_op jit(solution)/shard_map/ppermute | solution.py:20
  18.2 2.1 %collective-permute-start.2 = (f32[32,512]{1,0:T(8,128)S(1)}, f32[32,512]{1,0:T(8,128)S(1)}, u32[]{:S(2)}, u32[]{:S(2)}) collective-permute-start(f32[32,512]{1,0:T(8,128)S(1)} %get-tuple-element.14), channel_id=1, source_target_pairs={{0,12},{4,0},{8,4},{12,8},{1,13},{5,1},{9,5},{13,9},{2,14},{6,2},{... | collective-permute-start | bytes 196616 | tf_op jit(solution)/shard_map/ppermute | solution.py:20
  20.3 2.4 %collective-permute-done.1.above = f32[32,512]{1,0:T(8,128)S(1)} collective-permute-done((f32[32,512]{1,0:T(8,128)S(1)}, f32[32,512]{1,0:T(8,128)S(1)}, u32[]{:S(2)}, u32[]{:S(2)}) %collective-permute-start.1) | collective-permute-done | bytes 65568 | tf_op jit(solution)/shard_map/ppermute | solution.py:20
  22.7 0.5 %collective-permute-done.2.below = f32[32,512]{1,0:T(8,128)S(1)} collective-permute-done((f32[32,512]{1,0:T(8,128)S(1)}, f32[32,512]{1,0:T(8,128)S(1)}, u32[]{:S(2)}, u32[]{:S(2)}) %collective-permute-start.2) | collective-permute-done | bytes 65568 | tf_op jit(solution)/shard_map/ppermute | solution.py:20
  23.2 6.3 %steps.1 = (f32[3,64,512]{2,1,0:T(8,128)S(1)}, f32[4,64,512]{2,1,0:T(8,128)}, f32[4,64,512]{2,1,0:T(8,128)}) custom-call(f32[3]{0:T(128)S(1)} %copy-done.8, f32[4,64,512]{2,1,0:T(8,128)S(1)} %copy-done, f32[4,64,512]{2,1,0:T(8,128)S(1)} %copy-done.1, f32[4,64,512]{2,1,0:T(8,128)S(1)} %copy-done.2, f32[4,64,512]{2,1,0:T(8,128)S(1)} %copy-done.3, ...), custom_call_target="tpu_custom_call" | custom-call | tf_op jit(solution)/shard_map/steps/pallas_call | solution.py:440
  29.5 0.0 collective-permute-start.3
  29.5 1.7 %collective-permute-done.3.other = f32[3,64,512]{2,1,0:T(8,128)S(1)} collective-permute-done((f32[3,64,512]{2,1,0:T(8,128)S(1)}, f32[3,64,512]{2,1,0:T(8,128)S(1)}, u32[]{:S(2)}, u32[]{:S(2)}) %collective-permute-start.3) | collective-permute-done | bytes 393248 | tf_op jit(solution)/shard_map/ppermute | solution.py:20
  31.2 0.8 %force_sums.1 = (f32[64,512]{1,0:T(8,128)}, f32[64,512]{1,0:T(8,128)}, f32[64,512]{1,0:T(8,128)}) custom-call(f32[3,64,512]{2,1,0:T(8,128)S(1)} %get-tuple-element.15.mine, f32[3,64,512]{2,1,0:T(8,128)S(1)} %collective-permute-done.3.other), custom_call_target="tpu_custom_call" | custom-call | tf_op jit(solution)/shard_map/force_sums/pallas_call | solution.py:462
Async XLA Ops:
  0.6 1.0 %copy-start = (f32[4,64,512]{2,1,0:T(8,128)S(1)}, f32[4,64,512]{2,1,0:T(8,128)}, u32[]{:S(2)}) copy-start(f32[4,64,512]{2,1,0:T(8,128)} %adj.1) | copy-start | bytes 1572868
  1.7 1.0 %copy-start.1 = (f32[4,64,512]{2,1,0:T(8,128)S(1)}, f32[4,64,512]{2,1,0:T(8,128)}, u32[]{:S(2)}) copy-start(f32[4,64,512]{2,1,0:T(8,128)} %fwd.1) | copy-start | bytes 1572868
  2.7 1.0 %copy-start.2 = (f32[4,64,512]{2,1,0:T(8,128)S(1)}, f32[4,64,512]{2,1,0:T(8,128)}, u32[]{:S(2)}) copy-start(f32[4,64,512]{2,1,0:T(8,128)} %adj_next.1) | copy-start | bytes 1572868
  3.8 1.0 %copy-start.3 = (f32[4,64,512]{2,1,0:T(8,128)S(1)}, f32[4,64,512]{2,1,0:T(8,128)}, u32[]{:S(2)}) copy-start(f32[4,64,512]{2,1,0:T(8,128)} %fwd_next.1) | copy-start | bytes 1572868
  4.8 1.0 %copy-start.4 = (s32[4,64,512]{2,1,0:T(8,128)S(1)}, s32[4,64,512]{2,1,0:T(8,128)}, u32[]{:S(2)}) copy-start(s32[4,64,512]{2,1,0:T(8,128)} %signs.1) | copy-start | bytes 1572868
  5.8 0.9 %copy-start.5 = (f32[64,512]{1,0:T(8,128)S(1)}, f32[64,512]{1,0:T(8,128)}, u32[]{:S(2)}) copy-start(f32[64,512]{1,0:T(8,128)} %onsite.1) | copy-start | bytes 393220
  6.8 0.9 %copy-start.6 = (f32[64,512]{1,0:T(8,128)S(1)}, f32[64,512]{1,0:T(8,128)}, u32[]{:S(2)}) copy-start(f32[64,512]{1,0:T(8,128)} %hop_right.1) | copy-start | bytes 393220
  7.7 0.9 %copy-start.7 = (f32[64,512]{1,0:T(8,128)S(1)}, f32[64,512]{1,0:T(8,128)}, u32[]{:S(2)}) copy-start(f32[64,512]{1,0:T(8,128)} %hop_down.1) | copy-start | bytes 393220
  8.6 0.7 %copy-start.8 = (f32[3]{0:T(128)S(1)}, f32[3]{0:T(128)}, u32[]{:S(2)}) copy-start(f32[3]{0:T(128)} %weights.5) | copy-start | bytes 40
  10.2 4.9 %collective-permute-start = (f32[64,128]{1,0:T(8,128)S(1)}, f32[64,128]{1,0:T(8,128)S(1)}, u32[]{:S(2)}, u32[]{:S(2)}) collective-permute-start(f32[64,128]{1,0:T(8,128)S(1)} %edge_columns.1.refs_16_.refs_17_.own), channel_id=1, source_target_pairs={{0,2},{2,0},{1,3},{3,1},{4,6},{6,4},{5,7},{7,5},{8,10},{10,8},{9,1... | collective-permute-start | bytes 98312 | tf_op jit(solution)/shard_map/ppermute | solution.py:20
  16.1 6.6 %collective-permute-start.1 = (f32[32,512]{1,0:T(8,128)S(1)}, f32[32,512]{1,0:T(8,128)S(1)}, u32[]{:S(2)}, u32[]{:S(2)}) collective-permute-start(f32[32,512]{1,0:T(8,128)S(1)} %get-tuple-element.13), channel_id=1, source_target_pairs={{0,4},{4,8},{8,12},{12,0},{1,5},{5,9},{9,13},{13,1},{2,6},{6,10},{... | collective-permute-start | bytes 196616 | tf_op jit(solution)/shard_map/ppermute | solution.py:20
  18.2 5.0 %collective-permute-start.2 = (f32[32,512]{1,0:T(8,128)S(1)}, f32[32,512]{1,0:T(8,128)S(1)}, u32[]{:S(2)}, u32[]{:S(2)}) collective-permute-start(f32[32,512]{1,0:T(8,128)S(1)} %get-tuple-element.14), channel_id=1, source_target_pairs={{0,12},{4,0},{8,4},{12,8},{1,13},{5,1},{9,5},{13,9},{2,14},{6,2},{... | collective-permute-start | bytes 196616 | tf_op jit(solution)/shard_map/ppermute | solution.py:20
  29.5 1.7 %collective-permute-start.3 = (f32[3,64,512]{2,1,0:T(8,128)S(1)}, f32[3,64,512]{2,1,0:T(8,128)S(1)}, u32[]{:S(2)}, u32[]{:S(2)}) collective-permute-start(f32[3,64,512]{2,1,0:T(8,128)S(1)} %get-tuple-element.15.mine), channel_id=1, source_target_pairs={{0,1},{1,0},{2,3},{3,2},{4,5},{5,4},{6,7},{7,6},{8,9},{9,8},{10,11... | collective-permute-start | bytes 1179656 | tf_op jit(solution)/shard_map/ppermute | solution.py:20

commit v2 on v0

v2 whole, which is shorter than its diff:
```python
import jax
import jax.numpy as jnp
from jax import lax
from jax.experimental import pallas as pl
from jax.experimental.pallas import tpu as pltpu
from jax.sharding import PartitionSpec as P

STEPS = 3
LANES = 128
TILE = 8
spectral_half = 7.5
SCALE = 2.0 / spectral_half

WIDE = 2 * STEPS
VMEM_LIMIT = 16 * 1024 * 1024
COST = 4_000_000


def shifted(x, axis, by):
    size = lax.axis_size(axis)
    return lax.ppermute(x, axis, [(i, (i + by) % size) for i in range(size)])


def lane_of(shape):
    return lax.broadcasted_iota(jnp.int32, shape, len(shape) - 1)


def turned(x, by):
    return pltpu.roll(x, by % x.shape[1], 1)


def pair_swap(x, axis, odd):
    size = lax.axis_size(axis)
    pairs = []
    for i in range(odd, size, 2):
        pairs += [(i, (i + 1) % size), ((i + 1) % size, i)]
    return lax.ppermute(x, axis, pairs)


def load_kernel(
    weights_in,
    adj_in,
    fwd_in,
    adj_next_in,
    fwd_next_in,
    signs_in,
    onsite_in,
    hop_right_in,
    hop_down_in,
    x0,
    adj_next,
    fwd_next,
    signs,
    onsite,
    hop_right,
    hop_down,
    weights,
    out,
    done,
):
    probes, rows, cols = adj_in.shape
    tiles = cols // LANES
    span = WIDE * 2 * probes
    lane = lane_of(out.shape)
    copies = []

    def copy(source, target):
        copies.append(pltpu.make_async_copy(source, target, done.at[len(copies)]))
        copies[-1].start()

    def copy_tile(c):
        for f, source in enumerate((adj_in, fwd_in)):
            copy(
                source.at[:, :, pl.ds(c * LANES, LANES)],
                x0.at[pl.ds(f * probes, probes), c, pl.ds(TILE, rows), :],
            )

    copy(weights_in, weights)
    copy_tile(0)
    copy_tile(tiles - 1)
    copy(signs_in, signs)
    copy(adj_next_in, adj_next)
    copy(fwd_next_in, fwd_next)
    copy(onsite_in, onsite)
    copy(hop_right_in, hop_right)
    copy(hop_down_in, hop_down)
    needed = len(copies)
    for c in range(1, tiles - 1):
        copy_tile(c)
    for at in range(needed):
        copies[at].wait()

    first_lanes, last_lanes = pl.ds(0, LANES), pl.ds(cols - LANES, LANES)

    def joined(low, high):
        return jnp.where(lane < LANES // 2, low, high)

    def joined_field(ref, probe):
        return joined(ref[probe, :, first_lanes], ref[probe, :, last_lanes])

    def joined_now(g):
        return joined(x0[g, 0, pl.ds(TILE, rows), :], x0[g, tiles - 1, pl.ds(TILE, rows), :])

    packed = jnp.zeros(out.shape, jnp.float32)

    def put(packed, x, start):
        return jnp.where((lane >= start) & (lane < start + WIDE), turned(x, start + STEPS), packed)

    first, last = LANES - STEPS, STEPS - 1
    weight = weights[0:1, 0:1]
    for probe in range(probes):
        group = WIDE * probe
        sign = joined_field(signs, probe).astype(jnp.float32)
        base = weight * sign - joined_field(adj_next, probe)
        base = jnp.where(lane == first, turned(sign, -2), jnp.where(lane == last, turned(sign, 2), base))
        packed = put(packed, joined_now(probe), group)
        packed = put(packed, base, span + group)
        group = WIDE * (probes + probe)
        base = jnp.where((lane == first) | (lane == last), 0.0, -joined_field(fwd_next, probe))
        packed = put(packed, joined_now(probes + probe), group)
        packed = put(packed, base, span + group)
    for at, ref in enumerate((onsite, hop_right, hop_down)):
        packed = put(packed, joined(ref[:, first_lanes], ref[:, last_lanes]), 2 * span + WIDE * at)
    out[...] = packed
    for at in range(needed, len(copies)):
        copies[at].wait()


def strips(own, left, right, span):
    lane = lane_of(own.shape)
    inner = lax.rem(lane, WIDE) < STEPS
    low = jnp.where(inner, left, own)
    high = jnp.where(inner, own, right)
    below = lane < span
    field = jnp.where(below, low, turned(high, span))
    base = jnp.where(below, turned(low, -span), high)
    coefficients = []
    for at in range(3):
        start = 2 * span + WIDE * at
        x = jnp.where(
            lane < WIDE,
            turned(low, -start),
            jnp.where((lane >= span) & (lane < span + WIDE), turned(high, span - start), 0.0),
        )
        reach = WIDE
        while reach < span:
            x = x + turned(x, reach)
            reach *= 2
        coefficients.append(x * SCALE)
    return field, base, coefficients


def column_of(row, groups, at):
    shape = (groups, LANES)
    wanted = WIDE * lax.broadcasted_iota(jnp.int32, shape, 0) + at
    return jnp.sum(jnp.where(lane_of(shape) == wanted, row, 0.0), axis=1, keepdims=True)


def sideways(x, hop, strip_row, hop_row, span):
    groups, cols = x.shape
    lane = lane_of(x.shape)
    before = jnp.where(lane == 0, column_of(strip_row, groups, STEPS - 1), turned(x, 1))
    after = jnp.where(lane == cols - 1, column_of(strip_row, groups, span + STEPS), turned(x, -1))
    hop = jnp.broadcast_to(hop, x.shape)
    hop_before = jnp.where(lane == 0, hop_row[:, STEPS - 1 : STEPS], turned(hop, 1))
    return hop * after + hop_before * before


class Block:
    def __init__(self, probes, rows, cols):
        self.probes, self.rows, self.cols = probes, rows, cols
        self.groups = 2 * probes
        self.span = WIDE * self.groups
        self.tiles = cols // LANES
        self.tall = rows + 2 * TILE
        self.field_shape = (self.groups * self.tiles * self.tall, LANES)

    def at(self, g, c, row, count=TILE):
        return (pl.ds((g * self.tiles + c) * self.tall + TILE + row, count), slice(None))

    def across(self, c, row):
        return (pl.ds(c * self.tall + TILE + row, self.groups, stride=self.tiles * self.tall), slice(None))

    def gathered(self, ref, row):
        return jnp.concatenate([ref[self.across(c, row)] for c in range(self.tiles)], axis=1)

    def scattered(self, ref, row, value):
        for c in range(self.tiles):
            ref[self.across(c, row)] = value[:, c * LANES : (c + 1) * LANES]

    def hop_row(self, hops, kind, row):
        at = TILE + row
        return jnp.concatenate([hops[kind, c, at : at + 1, :] for c in range(self.tiles)], axis=1)


def lanes(c):
    return pl.ds(c * LANES, LANES)


def beside(block, strip_tile):
    lane = lane_of(strip_tile.shape)
    picked = (lax.rem(lane, WIDE) == STEPS - 1) & (lane < block.span)
    both = jnp.where(picked, strip_tile, turned(strip_tile, -(block.span + 2)))
    return [turned(both, -(WIDE * g + STEPS - 1)) for g in range(block.groups)]


def tile_step(block, row, now, hops, sides, previous, sign, store, add):
    lane = lane_of((TILE, LANES))
    tiles = block.tiles
    for c in range(tiles):
        at = pl.ds(TILE + row, TILE)
        hop_site, hop_after, hop_before, hop_under = (hops[kind, c, at, :] for kind in range(4))
        hop_over = hops[3, c, pl.ds(TILE + row - 1, TILE), :]
        sums = None
        for p in range(block.probes):
            kept = []
            for f in range(2):
                g = f * block.probes + p
                side = 0.0 if sides is None else sides[g]
                centre = now[block.at(g, c, row)]
                if c > 0:
                    before = turned(jnp.where(lane == LANES - 1, now[block.at(g, c - 1, row)], centre), 1)
                else:
                    before = jnp.where(lane == 0, side, turned(centre, 1))
                if c < tiles - 1:
                    after = turned(jnp.where(lane == 0, now[block.at(g, c + 1, row)], centre), -1)
                else:
                    after = jnp.where(lane == LANES - 1, side, turned(centre, -1))
                under = now[block.at(g, c, row + 1)]
                over = now[block.at(g, c, row - 1)]
                total = hop_site * centre - previous(f, p, c)
                total = total + (hop_after * after + hop_before * before)
                total = total + (hop_under * under + hop_over * over)
                if f == 0:
                    total = total + sign(p, c)
                store(f, p, c, total)
                kept.append((centre, after, under))
            if add is not None:
                (a_centre, a_after, a_under), (q_centre, q_after, q_under) = kept
                terms = (
                    a_centre * q_after + a_after * q_centre,
                    a_centre * q_under + a_under * q_centre,
                    a_centre * q_centre,
                )
                sums = terms if p == 0 else tuple(x + y for x, y in zip(sums, terms))
        if add is not None:
            add(c, *sums)


def force_adder(forces, row, first):
    def add(c, *sums):
        for kind, term in enumerate(sums):
            spot = (kind, pl.ds(row, TILE), lanes(c))
            forces[spot] = term if first else forces[spot] + term

    return add


def sign_reader(signs, weights, step, row):
    weight = jnp.broadcast_to(weights[0:1, step : step + 1], (TILE, LANES))
    return lambda p, c: weight * signs[p, pl.ds(row, TILE), lanes(c)].astype(jnp.float32)


def field_storer(block, target, row):
    def store(f, p, c, tile):
        target[block.at(f * block.probes + p, c, row)] = tile

    return store


def field_reader(block, source, row):
    return lambda f, p, c: source[block.at(f * block.probes + p, c, row)]


def block_reader(adj, fwd, row):
    return lambda f, p, c: (fwd if f else adj)[p, pl.ds(row, TILE), lanes(c)]


def block_storer(adj, fwd, row):
    def store(f, p, c, tile):
        (fwd if f else adj)[p, pl.ds(row, TILE), lanes(c)] = tile

    return store


def first_kernel(weights, x0, adj_next, fwd_next, signs, onsite, hop_right, hop_down, x1, hops, forces):
    block = Block(*signs.shape)
    rows = block.rows
    wide_lane = lane_of((rows, LANES))
    inside = pl.ds(TILE, rows)
    hop_before = 0.0
    for c in range(block.tiles):
        hop = hop_right[:, lanes(c)] * SCALE
        hop_turned = turned(hop, 1)
        hops[0, c, inside, :] = onsite[:, lanes(c)] * SCALE
        hops[1, c, inside, :] = hop
        hops[2, c, inside, :] = jnp.where(wide_lane == 0, hop_before, hop_turned)
        hops[3, c, inside, :] = hop_down[:, lanes(c)] * SCALE
        hop_before = hop_turned
    for row in range(0, rows, TILE):
        inner = 0 < row < rows - TILE
        tile_step(
            block,
            row,
            x0,
            hops,
            None,
            block_reader(adj_next, fwd_next, row),
            sign_reader(signs, weights, 0, row),
            field_storer(block, x1, row),
            force_adder(forces, row, True) if inner else None,
        )


def edge_rows(block, weights, x0, adj_next, fwd_next, signs, hops, strip_tile, rows, at, out):
    edge, second, third = rows
    groups, span = block.groups, block.span
    field, base, (s_on, s_right, s_down) = strip_tile

    def line(x, i):
        return x[i : i + 1, :]

    def next_rows(row):
        return jnp.concatenate([adj_next[:, row, :], fwd_next[:, row, :]], axis=0)

    def sign_rows(step, row):
        sign = weights[0:1, step : step + 1] * signs[:, row, :].astype(jnp.float32)
        return jnp.concatenate([sign, jnp.zeros_like(sign)], axis=0)

    x_edge, x_second, x_third = (block.gathered(x0, row) for row in rows)
    down = block.hop_row(hops, 3, min(edge, second))

    def across(x, row, i):
        return block.hop_row(hops, 0, row) * x + sideways(
            x, block.hop_row(hops, 1, row), line(field, i), line(s_right, i), span
        )

    one = (
        sign_rows(0, second)
        - next_rows(second)
        + across(x_second, second, at[1])
        + down * x_edge
        + block.hop_row(hops, 3, min(second, third)) * x_third
    )
    part_one = sign_rows(0, edge) - next_rows(edge) + across(x_edge, edge, at[0]) + down * x_second
    part_two = sign_rows(1, edge) - x_edge + down * one
    level = base + s_on * field + s_right * turned(field, -1) + turned(s_right, 1) * turned(field, 1)
    strip_one = line(level, at[0]) + line(s_down, min(at[0], at[1])) * line(field, at[1])
    out[0:groups, :] = x_edge
    out[groups : 2 * groups, :] = part_one
    out[2 * groups : 3 * groups, :] = part_two
    misc = 3 * groups
    out[misc : misc + 1, :] = block.hop_row(hops, 0, edge)
    out[misc + 1 : misc + 2, :] = block.hop_row(hops, 1, edge)
    out[misc + 2 : misc + 3, :] = block.hop_row(hops, 3, edge)
    out[misc + 3 : misc + 4, 0 : 4 * LANES] = jnp.concatenate(
        [line(field, at[0]), strip_one, line(s_down, at[0]), line(s_right, at[0])], axis=1
    )
    out[misc + 4 : misc + TILE, :] = jnp.zeros((TILE - 4, out.shape[1]), jnp.float32)


def rows_kernel(weights, x0, adj_next, fwd_next, signs, hops, own, left, right, out_odd, out_even, message):
    block = Block(*signs.shape)
    rows = block.rows
    for side, (lines, at, start) in enumerate(
        (((0, 1, 2), (0, 1, 2), 0), ((rows - 1, rows - 2, rows - 3), (TILE - 1, TILE - 2, TILE - 3), rows - TILE))
    ):
        part = pl.ds(start, TILE)
        strip_tile = strips(own[part, :], left[part, :], right[part, :], block.span)
        edge_rows(
            block, weights, x0, adj_next, fwd_next, signs, hops, strip_tile, lines, at, message.at[side]
        )
    odd = lax.rem(lax.axis_index("strip"), 2) == 1
    out_odd[...] = jnp.where(odd, message[1], message[0])
    out_even[...] = jnp.where(odd, message[0], message[1])


def strip_rows(block, strip, strip_base, strip_hops, step, row, count):
    here = pl.ds(TILE + row, count)
    now = strip[step, here, :]
    s_right = strip_hops[1, here, :]
    strip[step + 1, here, :] = (
        strip_base[step, pl.ds(row, count), :]
        + strip_hops[0, here, :] * now
        + s_right * turned(now, -1)
        + turned(s_right, 1) * turned(now, 1)
        + strip_hops[2, here, :] * strip[step, pl.ds(TILE + row + 1, count), :]
        + strip_hops[2, pl.ds(TILE + row - 1, count), :] * strip[step, pl.ds(TILE + row - 1, count), :]
    )


def inner_kernel(
    weights,
    x0,
    signs,
    own,
    left,
    right,
    sent,
    x1_in,
    hops_in,
    forces_in,
    x1,
    hops,
    forces,
    x2,
    adj_out,
    fwd_out,
    strip,
    strip_base,
    strip_hops,
):
    del sent, x1_in, hops_in, forces_in
    block = Block(*signs.shape)
    rows, tiles, probes = block.rows, block.tiles, block.probes
    inside = pl.ds(TILE, rows)
    lane = lane_of((TILE, LANES))
    field, base, (s_on, s_right, s_down) = strips(own[...], left[...], right[...], block.span)
    sign_strip = jnp.where(lane_of(base.shape) < block.span, turned(base, 2), turned(base, -2))
    strip[0, inside, :] = field
    strip_base[0] = base
    strip_base[1] = weights[0:1, 1:2] * sign_strip - field
    strip_hops[0, inside, :] = s_on
    strip_hops[1, inside, :] = s_right
    strip_hops[2, inside, :] = s_down

    last = tiles - 1
    for row in range(0, rows, TILE):
        at = pl.ds(TILE + row, TILE)
        sides = beside(block, strip[0, at, :])
        hop_first = turned(strip_hops[1, at, :], -(STEPS - 1))
        hops[2, 0, at, :] = jnp.where(lane == 0, hop_first, hops[2, 0, at, :])
        hop_last = hops[1, last, at, :]
        for g in range(block.groups):
            spot = block.at(g, 0, row)
            x1[spot] = x1[spot] + jnp.where(lane == 0, hop_first * sides[g], 0.0)
            spot = block.at(g, last, row)
            x1[spot] = x1[spot] + jnp.where(lane == LANES - 1, hop_last * sides[g], 0.0)
        if 0 < row < rows - TILE:
            total = None
            for p in range(probes):
                q = probes + p
                term = x0[block.at(p, last, row)] * sides[q] + sides[p] * x0[block.at(q, last, row)]
                total = term if total is None else total + term
            spot = (0, pl.ds(row, TILE), lanes(last))
            forces[spot] = forces[spot] + jnp.where(lane == LANES - 1, total, 0.0)

    for step in (1, 2):
        strip_rows(block, strip, strip_base, strip_hops, step - 1, 0, rows)
        for row in range(0, rows, TILE):
            inner = 0 < row < rows - TILE
            if step == 2 and not inner:
                continue
            now, before = (x1, x0) if step == 1 else (x2, x1)
            tile_step(
                block,
                row,
                now,
                hops,
                beside(block, strip[step, pl.ds(TILE + row, TILE), :]),
                field_reader(block, before, row),
                sign_reader(signs, weights, step, row),
                field_storer(block, x2, row) if step == 1 else block_storer(adj_out, fwd_out, row),
                force_adder(forces, row, False) if inner else None,
            )


def outer_kernel(
    weights, adj_next, fwd_next, signs, strip_base, received_odd, received_even, *refs
):
    x0, x1, x2, hops, forces, adj_out, fwd_out, strip, strip_hops, message = refs[9:]
    block = Block(*signs.shape)
    rows, groups, span = block.rows, block.groups, block.span
    odd = lax.rem(lax.axis_index("strip"), 2) == 1
    message[0] = jnp.where(odd, received_even[...], received_odd[...])
    message[1] = jnp.where(odd, received_odd[...], received_even[...])
    above, below = message.at[0], message.at[1]
    misc = 3 * groups
    corner_above = above[misc + 3 : misc + 4, 0 : 4 * LANES]
    corner_below = below[misc + 3 : misc + 4, 0 : 4 * LANES]
    over, under = TILE - 1, TILE + rows
    strip[0, over : over + 1, :] = corner_above[:, :LANES]
    strip[0, under : under + 1, :] = corner_below[:, :LANES]
    s_over = corner_above[:, 2 * LANES : 3 * LANES]
    s_under = strip_hops[2, under - 1 : under, :]
    strip_hops[2, over : over + 1, :] = s_over
    one_above = corner_above[:, LANES : 2 * LANES] + s_over * strip[0, TILE : TILE + 1, :]
    one_below = corner_below[:, LANES : 2 * LANES] + s_under * strip[0, under - 1 : under, :]
    strip[1, over : over + 1, :] = one_above
    strip[1, under : under + 1, :] = one_below
    for c in range(block.tiles):
        hops[3, c, over : over + 1, :] = above[misc + 2 : misc + 3, c * LANES : (c + 1) * LANES]
    block.scattered(x0, -1, above[0:groups, :])
    block.scattered(x0, rows, below[0:groups, :])

    edges = (0, rows - TILE)
    hop_above = block.hop_row(hops, 3, -1)
    hop_below = block.hop_row(hops, 3, rows - 1)
    for step in range(STEPS):
        now = (x0, x1, x2)[step]
        for row in edges:
            previous = (
                block_reader(adj_next, fwd_next, row) if step == 0 else field_reader(block, (x0, x1)[step - 1], row)
            )
            store = (
                block_storer(adj_out, fwd_out, row)
                if step == STEPS - 1
                else field_storer(block, (x1, x2)[step], row)
            )
            tile_step(
                block,
                row,
                now,
                hops,
                beside(block, strip[step, pl.ds(TILE + row, TILE), :]),
                previous,
                sign_reader(signs, weights, step, row),
                store,
                force_adder(forces, row, step == 0),
            )
        if step == STEPS - 1:
            break
        for row in edges:
            strip_rows(block, strip, strip_base, strip_hops, step, row, TILE)
        if step == 0:
            block.scattered(x1, -1, above[groups : 2 * groups, :] + hop_above * block.gathered(x0, 0))
            block.scattered(x1, rows, below[groups : 2 * groups, :] + hop_below * block.gathered(x0, rows - 1))
        else:
            for source, hop, corner, strip_row, edge, inside in (
                (above, hop_above, corner_above, one_above, -1, 0),
                (below, hop_below, corner_below, one_below, rows, rows - 1),
            ):
                line = block.gathered(x1, edge)
                value = (
                    source[2 * groups : 3 * groups, :]
                    + source[misc : misc + 1, :] * line
                    + sideways(line, source[misc + 1 : misc + 2, :], strip_row, corner[:, 3 * LANES :], span)
                    + hop * block.gathered(x1, inside)
                )
                block.scattered(x2, edge, value)


def sum_kernel(mine, other, right_out, down_out, site_out):
    for at, out in enumerate((right_out, down_out, site_out)):
        out[...] = (mine[at] + other[at]) * SCALE


def in_vmem(*arrays):
    return tuple(pltpu.with_memory_space_constraint(v, pltpu.VMEM) for v in arrays)


def local(
    signs,
    onsite,
    hop_right,
    hop_down,
    moment_weights,
    forward_now,
    forward_next,
    adjoint_now,
    adjoint_next,
):
    probes, rows, cols = forward_now.shape
    block = Block(probes, rows, cols)
    groups, tiles, tall = block.groups, block.tiles, block.tall
    f32 = jnp.float32
    vmem = pl.BlockSpec(memory_space=pltpu.VMEM)
    hbm = pl.BlockSpec(memory_space=pltpu.HBM)
    params = pltpu.CompilerParams(vmem_limit_bytes=VMEM_LIMIT)

    def call(kernel, name, inputs, outs, scratch=(), aliases=None, flops=0, in_spec=vmem):
        return pl.pallas_call(
            kernel,
            out_shape=outs,
            in_specs=[in_spec] * len(inputs),
            out_specs=(vmem,) * len(outs),
            scratch_shapes=list(scratch),
            input_output_aliases=aliases or {},
            compiler_params=params,
            cost_estimate=pl.CostEstimate(flops=flops, bytes_accessed=flops, transcendentals=0),
            name=name,
        )(*inputs)

    def like(v, dtype=f32):
        return pltpu.VMEM(v.shape, dtype)

    sources = (
        moment_weights.reshape(1, STEPS),
        adjoint_now,
        forward_now,
        adjoint_next,
        forward_next,
        signs,
        onsite,
        hop_right,
        hop_down,
    )
    sources = tuple(pltpu.with_memory_space_constraint(v, pltpu.HBM) for v in sources)
    x0, adj_next, fwd_next, sign, on, hr, hd, weights, packed = call(
        load_kernel,
        "load",
        sources,
        (
            pltpu.VMEM((groups, tiles, tall, LANES), f32),
            like(adjoint_next),
            like(forward_next),
            like(signs, jnp.int32),
            like(onsite),
            like(hop_right),
            like(hop_down),
            pltpu.VMEM((1, STEPS), f32),
            pltpu.VMEM((rows, LANES), f32),
        ),
        [pltpu.SemaphoreType.DMA((7 + 2 * tiles,))],
        in_spec=hbm,
    )
    x0 = x0.reshape(block.field_shape)
    left = shifted(packed, "col", 1)
    right = left if lax.axis_size("col") == 2 else shifted(packed, "col", -1)

    x0, adj_next, fwd_next, sign, on, hr, hd, weights = in_vmem(
        x0, adj_next, fwd_next, sign, on, hr, hd, weights
    )
    field = pltpu.VMEM(block.field_shape, f32)
    hops_shape = pltpu.VMEM((4, tiles, tall, LANES), f32)
    forces_shape = pltpu.VMEM((3, rows, cols), f32)
    x1, hops, forces = call(
        first_kernel,
        "first_step",
        (weights, x0, adj_next, fwd_next, sign, on, hr, hd),
        (field, hops_shape, forces_shape),
        flops=COST,
    )

    x1, hops, forces, own, left, right = in_vmem(x1, hops, forces, packed, left, right)
    message = pltpu.VMEM((3 * groups + TILE, cols), f32)
    to_odd, to_even = call(
        rows_kernel,
        "edge_rows",
        (weights, x0, adj_next, fwd_next, sign, hops, own, left, right),
        (message, message),
        [pltpu.VMEM((2, 3 * groups + TILE, cols), f32)],
    )
    received_odd = pair_swap(to_odd, "strip", 1)
    received_even = pair_swap(to_even, "strip", 0)

    (sent,) = in_vmem(to_even)
    x1, hops, forces, x2, adj_out, fwd_out, strip, strip_base, strip_hops = call(
        inner_kernel,
        "inner_steps",
        (weights, x0, sign, own, left, right, sent, x1, hops, forces),
        (
            field,
            hops_shape,
            forces_shape,
            field,
            like(adjoint_now),
            like(forward_now),
            pltpu.VMEM((STEPS, tall, LANES), f32),
            pltpu.VMEM((2, rows, LANES), f32),
            pltpu.VMEM((3, tall, LANES), f32),
        ),
        aliases={7: 0, 8: 1, 9: 2},
        flops=COST,
    )

    kept = in_vmem(x0, x1, x2, hops, forces, adj_out, fwd_out, strip, strip_hops)
    read = (weights, adj_next, fwd_next, sign) + in_vmem(strip_base, received_odd, received_even)
    outs = call(
        outer_kernel,
        "outer_rows",
        read + kept,
        tuple(like(v) for v in kept),
        [pltpu.VMEM((2, 3 * groups + TILE, cols), f32)],
        aliases={len(read) + i: i for i in range(len(kept))},
        flops=COST,
    )
    forces, adjoint_out, forward_out = outs[4:7]

    other = shifted(forces, "probe", 1)
    plain = jax.ShapeDtypeStruct((rows, cols), f32)
    right_force, down_force, site_force = call(
        sum_kernel, "force_sums", in_vmem(forces, other), (plain, plain, plain)
    )
    return right_force, down_force, site_force, forward_out, adjoint_out


def solution(mesh):
    placed = (
        P(("parts", "probe"), "strip", "col"),
        P(("parts", "strip"), "col"),
        P(("parts", "strip"), "col"),
        P(("parts", "strip"), "col"),
        P(),
        P(("parts", "probe"), "strip", "col"),
        P(("parts", "probe"), "strip", "col"),
        P(("parts", "probe"), "strip", "col"),
        P(("parts", "probe"), "strip", "col"),
    )
    return jax.shard_map(
        local,
        mesh=mesh,
        in_specs=placed,
        out_specs=(
            P(("parts", "strip"), "col"),
            P(("parts", "strip"), "col"),
            P(("parts", "strip"), "col"),
            P(("parts", "probe"), "strip", "col"),
            P(("parts", "probe"), "strip", "col"),
        ),
        check_vma=False,
    )
```

time: 109 us -> 20.7 us (0.19)
  waiting for transfers between devices: 48.3 us -> 2.23 us
  other arithmetic: 21.9 us -> 0 us
  between operations: 14.3 us -> 0.69 us
  starting transfers between devices: 20.6 us -> 7.27 us
  Pallas kernels: 0 us -> 8.78 us
  local copies, waits for them, and re-layouts: 3.41 us -> 1.59 us
    ppermute x12 -> x2, waiting for transfers between devices: 32.2 us -> 1.15 us  [pair_swap(): return lax.ppermute(x, axis, pairs)]
    psum x1 -> x0, waiting for transfers between devices: 15.2 us -> none  [local(): lax.psum((right_acc, down_acc, site_acc), 'probe')]
    ppermute x12 -> x2, starting transfers between devices: 15.8 us -> 4.2 us  [pair_swap(): return lax.ppermute(x, axis, pairs)]
    pallas_call x0 -> x6, Pallas kernels: none -> 8.78 us  [call(): pl.pallas_call(kernel, out_shape=outs, in_specs=[in_spec] * len(inputs),...]
    mul x3 -> x0, other arithmetic: 4.71 us -> none  [the longest x1 1.57 us: local(): right_sum * factor]
    div x3 -> x0, other arithmetic: 3.74 us -> none  [stencil(): return total / spectral_half]
    concatenate x7 -> x0, other arithmetic: 3.29 us -> none  [the longest x5 2.28 us: with_halo(): block = jnp.concatenate([low, block, high], axis=dim)]
    slice x3 -> x0, local copies, waits for them, and re-layouts: 2.99 us -> none  [the longest x1 1.36 us: local(): moment_weights[moment] * sign_field + 2.0 * images[1] - adjoint_prev]
  transfers between devices with their start and end apart: 15 -> 4, of which waited for: 11 -> 3; matrix products, arithmetic and copies ran while one was open for 11% -> 8% of each run, Pallas kernels for 0% -> 20%
where the time goes in v2:
time: 20.7 us; the launch traced here: 20.6 us
  Pallas kernels  8.78 us (42%)
  starting transfers between devices  7.27 us (35%)
  waiting for transfers between devices  2.23 us (11%)
  local copies, waits for them, and re-layouts  1.59 us (8%)
  between operations  0.69 us (3%)
    pallas_call x6, Pallas kernels, call(): pl.pallas_call(kernel, out_shape=outs, in_specs=[in_spec] * len(inputs),...  8.78 us
    ppermute x2, starting transfers between devices, pair_swap(): return lax.ppermute(x, axis, pairs)  4.2 us
    ppermute x2, starting transfers between devices, shifted(): return lax.ppermute(x, axis, [(i, (i + by) % size) for i in range(size)])  3.07 us
    unnamed x2, local copies, waits for them, and re-layouts  1.59 us
    ppermute x2, waiting for transfers between devices, pair_swap(): return lax.ppermute(x, axis, pairs)  1.15 us
    ppermute x2, waiting for transfers between devices, shifted(): return lax.ppermute(x, axis, [(i, (i + by) % size) for i in range(size)])  1.07 us
  transfers between devices with their start and end apart: 4, of which 3 were waited for; matrix products, arithmetic and copies ran while one was open for 8% of the time, Pallas kernels for 20%

profile of v2, /device:TPU:0, one launch (start us, length us, event | category | flops | bytes accessed | tf_op | source)
XLA Modules:
  0.0 20.6 jit_solution(7681013775232010559)
XLA Ops:
  0.6 2.3 %load.1 = (f32[8,4,80,128]{3,2,1,0:T(8,128)S(1)}, f32[4,64,512]{2,1,0:T(8,128)S(1)}, f32[4,64,512]{2,1,0:T(8,128)S(1)}, s32[4,64,512]{2,1,0:T(8,128)S(1)}, f32[6...) custom-call(f32[1,3]{1,0:T(1,128)} %bitcast.6, ...), custom_call_target="tpu_custom_call" | custom-call | tf_op jit(solution)/shard_map/load/pallas_call | solution.py:572
  3.0 3.0 %collective-permute-start = (f32[64,128]{1,0:T(8,128)S(1)}, f32[64,128]{1,0:T(8,128)S(1)}, u32[]{:S(2)}, u32[]{:S(2)}) collective-permute-start(f32[64,128]{1,0:T(8,128)S(1)} %get-tuple-element.39.own), channel_id=1, source_target_pairs={{0,2},{2,0},{1,3},{3,1},{4,6},{6,4},{5,7},{7,5},{8,10},{10,8},{9,1... | collective-permute-start | bytes 98312 | tf_op jit(solution)/shard_map/ppermute | solution.py:21
  6.0 0.9 %first_step.1 = (f32[2560,128]{1,0:T(8,128)S(1)}, f32[4,4,80,128]{3,2,1,0:T(8,128)S(1)}, f32[3,64,512]{2,1,0:T(8,128)S(1)}) custom-call(f32[1,3]{1,0:T(1,128)S(1)} %get-tuple-element.34.weights, f32[2560,128]{1,0:T(8,128)S(1)} %bitcast.2, f32[4,64,512]{2,1,0:T(8,128)S(1)} %get-tuple-element.35.adj_next, f32[4,64,512]{2,1,0:T(8,128)S(1)} %get-tuple-element.36.fwd_next, ...), custom_call_target="tpu_custom_call" | custom-call | flops 4000000 | bytes 4000000 | tf_op jit(solution)/shard_map/first_step/pallas_call | solution.py:572
  6.9 1.0 %collective-permute-done.left.right = f32[64,128]{1,0:T(8,128)S(1)} collective-permute-done((f32[64,128]{1,0:T(8,128)S(1)}, f32[64,128]{1,0:T(8,128)S(1)}, u32[]{:S(2)}, u32[]{:S(2)}) %collective-permute-start) | collective-permute-done | bytes 32800 | tf_op jit(solution)/shard_map/ppermute | solution.py:21
  7.9 0.4 %edge_rows.1 = (f32[32,512]{1,0:T(8,128)S(1)}, f32[32,512]{1,0:T(8,128)S(1)}) custom-call(f32[1,3]{1,0:T(1,128)S(1)} %get-tuple-element.34.weights, f32[2560,128]{1,0:T(8,128)S(1)} %bitcast.3, f32[4,64,512]{2,1,0:T(8,128)S(1)} %get-tuple-element.35.adj_next, f32[4,64,512]{2,1,0:T(8,128)S(1)} %get-tuple-element.36.fwd_next, ...), custom_call_target="tpu_custom_call" | custom-call | tf_op jit(solution)/shard_map/edge_rows/pallas_call | solution.py:572
  8.3 4.2 %collective-permute-start.1 = (f32[32,512]{1,0:T(8,128)S(1)}, f32[32,512]{1,0:T(8,128)S(1)}, u32[]{:S(2)}, u32[]{:S(2)}) collective-permute-start(f32[32,512]{1,0:T(8,128)S(1)} %get-tuple-element.48), channel_id=1, source_target_pairs={{4,8},{8,4},{12,0},{0,12},{5,9},{9,5},{13,1},{1,13},{6,10},{10,6},... | collective-permute-start | bytes 196616 | tf_op jit(solution)/shard_map/ppermute | solution.py:37
  12.5 0.0 collective-permute-start.2
  12.5 3.1 %inner_steps.1 = (f32[2560,128]{1,0:T(8,128)S(1)}, f32[4,4,80,128]{3,2,1,0:T(8,128)S(1)}, f32[3,64,512]{2,1,0:T(8,128)S(1)}, f32[2560,128]{1,0:T(8,128)S(1)}, f3...) custom-call(f32[1,3]{1,0:T(1,128)S(1)} %get-tuple-element.34.weights, ...), custom_call_target="tpu_custom_call", output_to_operand_aliasing={{0}: (7, {}), {1}: (8, {}), {2}: (9, {})} | custom-call | flops 4000000 | bytes 4000000 | tf_op jit(solution)/shard_map/inner_steps/pallas_call | solution.py:572
  15.6 0.0 collective-permute-done.1.received_odd
  15.6 1.1 %collective-permute-done.2.received_even = f32[32,512]{1,0:T(8,128)S(1)} collective-permute-done((f32[32,512]{1,0:T(8,128)S(1)}, f32[32,512]{1,0:T(8,128)S(1)}, u32[]{:S(2)}, u32[]{:S(2)}) %collective-permute-start.2) | collective-permute-done | bytes 65568 | tf_op jit(solution)/shard_map/ppermute | solution.py:37
  16.8 1.2 %outer_rows.1 = (f32[2560,128]{1,0:T(8,128)S(1)}, f32[2560,128]{1,0:T(8,128)S(1)}, f32[2560,128]{1,0:T(8,128)S(1)}, f32[4,4,80,128]{3,2,1,0:T(8,128)S(1)}, f32[3...) custom-call(f32[1,3]{1,0:T(1,128)S(1)} %get-tuple-element.34.weights, ...), custom_call_target="tpu_custom_call", output_to_operand_aliasing={{0}: (7, {}), {1}: (8, {}), {2}: (9, {}), {3}: (10, {}), {4... | custom-call | flops 4000000 | bytes 4000000 | tf_op jit(solution)/shard_map/outer_rows/pallas_call | solution.py:572
  18.0 0.1 collective-permute-start.3
  18.1 0.8 %copy.38 = f32[4,64,512]{2,1,0:T(8,128)} copy(f32[4,64,512]{2,1,0:T(8,128)S(1)} %get-tuple-element.66) | data formatting | bytes 1048576
  18.8 0.8 %copy.39 = f32[4,64,512]{2,1,0:T(8,128)} copy(f32[4,64,512]{2,1,0:T(8,128)S(1)} %get-tuple-element.67) | data formatting | bytes 1048576
  19.6 0.1 collective-permute-done.3.other
  19.8 0.8 %force_sums.1 = (f32[64,512]{1,0:T(8,128)}, f32[64,512]{1,0:T(8,128)}, f32[64,512]{1,0:T(8,128)}) custom-call(f32[3,64,512]{2,1,0:T(8,128)S(1)} %get-tuple-element.57.mine, f32[3,64,512]{2,1,0:T(8,128)S(1)} %collective-permute-done.3.other), custom_call_target="tpu_custom_call" | custom-call | tf_op jit(solution)/shard_map/force_sums/pallas_call | solution.py:572
Async XLA Ops:
  3.0 4.9 %collective-permute-start = (f32[64,128]{1,0:T(8,128)S(1)}, f32[64,128]{1,0:T(8,128)S(1)}, u32[]{:S(2)}, u32[]{:S(2)}) collective-permute-start(f32[64,128]{1,0:T(8,128)S(1)} %get-tuple-element.39.own), channel_id=1, source_target_pairs={{0,2},{2,0},{1,3},{3,1},{4,6},{6,4},{5,7},{7,5},{8,10},{10,8},{9,1... | collective-permute-start | bytes 98312 | tf_op jit(solution)/shard_map/ppermute | solution.py:21
  8.3 7.3 %collective-permute-start.1 = (f32[32,512]{1,0:T(8,128)S(1)}, f32[32,512]{1,0:T(8,128)S(1)}, u32[]{:S(2)}, u32[]{:S(2)}) collective-permute-start(f32[32,512]{1,0:T(8,128)S(1)} %get-tuple-element.48), channel_id=1, source_target_pairs={{4,8},{8,4},{12,0},{0,12},{5,9},{9,5},{13,1},{1,13},{6,10},{10,6},... | collective-permute-start | bytes 196616 | tf_op jit(solution)/shard_map/ppermute | solution.py:37
  12.5 4.3 %collective-permute-start.2 = (f32[32,512]{1,0:T(8,128)S(1)}, f32[32,512]{1,0:T(8,128)S(1)}, u32[]{:S(2)}, u32[]{:S(2)}) collective-permute-start(f32[32,512]{1,0:T(8,128)S(1)} %get-tuple-element.44.sent), channel_id=1, source_target_pairs={{0,4},{4,0},{8,12},{12,8},{1,5},{5,1},{9,13},{13,9},{2,6},{6,2},{1... | collective-permute-start | bytes 196616 | tf_op jit(solution)/shard_map/ppermute | solution.py:37
  18.0 1.8 %collective-permute-start.3 = (f32[3,64,512]{2,1,0:T(8,128)S(1)}, f32[3,64,512]{2,1,0:T(8,128)S(1)}, u32[]{:S(2)}, u32[]{:S(2)}) collective-permute-start(f32[3,64,512]{2,1,0:T(8,128)S(1)} %get-tuple-element.57.mine), channel_id=1, source_target_pairs={{0,1},{1,0},{2,3},{3,2},{4,5},{5,4},{6,7},{7,6},{8,9},{9,8},{10,11... | collective-permute-start | bytes 1179656 | tf_op jit(solution)/shard_map/ppermute | solution.py:21

commit v3 on v2

--- a/solution.py
+++ b/solution.py
@@ -35,6 +35,39 @@
     for i in range(odd, size, 2):
         pairs += [(i, (i + 1) % size), ((i + 1) % size, i)]
     return lax.ppermute(x, axis, pairs)
+
+
+def pack(shape, now, following, signs, lattice, weight):
+    groups = len(now)
+    span = WIDE * groups
+    lane = lane_of(shape)
+
+    def joined(pair):
+        return jnp.where(lane < LANES // 2, pair[0], pair[1])
+
+    packed = jnp.zeros(shape, jnp.float32)
+
+    def put(packed, x, start):
+        return jnp.where((lane >= start) & (lane < start + WIDE), turned(x, start + STEPS), packed)
+
+    first, last = LANES - STEPS, STEPS - 1
+    for g in range(groups):
+        if g < len(signs):
+            sign = joined(signs[g]).astype(jnp.float32)
+            base = weight * sign - joined(following[g])
+            base = jnp.where(lane == first, turned(sign, -2), jnp.where(lane == last, turned(sign, 2), base))
+        else:
+            base = jnp.where((lane == first) | (lane == last), 0.0, -joined(following[g]))
+        packed = put(packed, joined(now[g]), WIDE * g)
+        packed = put(packed, base, span + WIDE * g)
+    for at, pair in enumerate(lattice):
+        packed = put(packed, joined(pair), 2 * span + WIDE * at)
+    return packed
+
+
+def ends(ref, *at):
+    cols = ref.shape[-1]
+    return tuple(ref[(*at, slice(None), pl.ds(start, LANES))] for start in (0, cols - LANES))
 
 
 def load_kernel(
@@ -55,13 +88,13 @@
     hop_right,
     hop_down,
     weights,
-    out,
+    packed,
     done,
 ):
     probes, rows, cols = adj_in.shape
+    groups = 2 * probes
     tiles = cols // LANES
-    span = WIDE * 2 * probes
-    lane = lane_of(out.shape)
+    inside = pl.ds(TILE, rows)
     copies = []
 
     def copy(source, target):
@@ -70,60 +103,76 @@
 
     def copy_tile(c):
         for f, source in enumerate((adj_in, fwd_in)):
-            copy(
-                source.at[:, :, pl.ds(c * LANES, LANES)],
-                x0.at[pl.ds(f * probes, probes), c, pl.ds(TILE, rows), :],
-            )
+            copy(source.at[:, :, lanes(c)], x0.at[pl.ds(f * probes, probes), c, inside, :])
+
+    def copy_lanes(start, count):
+        part = pl.ds(start, count)
+        for source, target in ((adj_next_in, adj_next), (fwd_next_in, fwd_next), (signs_in, signs)):
+            copy(source.at[:, :, part], target.at[:, :, part])
 
     copy(weights_in, weights)
-    copy_tile(0)
-    copy_tile(tiles - 1)
-    copy(signs_in, signs)
-    copy(adj_next_in, adj_next)
-    copy(fwd_next_in, fwd_next)
+    for c in (0, tiles - 1):
+        copy_tile(c)
+        copy_lanes(c * LANES, LANES)
     copy(onsite_in, onsite)
     copy(hop_right_in, hop_right)
     copy(hop_down_in, hop_down)
     needed = len(copies)
     for c in range(1, tiles - 1):
         copy_tile(c)
+    copy_lanes(LANES, cols - 2 * LANES)
     for at in range(needed):
         copies[at].wait()
-
-    first_lanes, last_lanes = pl.ds(0, LANES), pl.ds(cols - LANES, LANES)
-
-    def joined(low, high):
-        return jnp.where(lane < LANES // 2, low, high)
-
-    def joined_field(ref, probe):
-        return joined(ref[probe, :, first_lanes], ref[probe, :, last_lanes])
-
-    def joined_now(g):
-        return joined(x0[g, 0, pl.ds(TILE, rows), :], x0[g, tiles - 1, pl.ds(TILE, rows), :])
-
-    packed = jnp.zeros(out.shape, jnp.float32)
-
-    def put(packed, x, start):
-        return jnp.where((lane >= start) & (lane < start + WIDE), turned(x, start + STEPS), packed)
-
-    first, last = LANES - STEPS, STEPS - 1
-    weight = weights[0:1, 0:1]
-    for probe in range(probes):
-        group = WIDE * probe
-        sign = joined_field(signs, probe).astype(jnp.float32)
-        base = weight * sign - joined_field(adj_next, probe)
-        base = jnp.where(lane == first, turned(sign, -2), jnp.where(lane == last, turned(sign, 2), base))
-        packed = put(packed, joined_now(probe), group)
-        packed = put(packed, base, span + group)
-        group = WIDE * (probes + probe)
-        base = jnp.where((lane == first) | (lane == last), 0.0, -joined_field(fwd_next, probe))
-        packed = put(packed, joined_now(probes + probe), group)
-        packed = put(packed, base, span + group)
-    for at, ref in enumerate((onsite, hop_right, hop_down)):
-        packed = put(packed, joined(ref[:, first_lanes], ref[:, last_lanes]), 2 * span + WIDE * at)
-    out[...] = packed
+    packed[...] = pack(
+        packed.shape,
+        [(x0[g, 0, inside, :], x0[g, tiles - 1, inside, :]) for g in range(groups)],
+        [ends(ref, p) for ref in (adj_next, fwd_next) for p in range(probes)],
+        [ends(signs, p) for p in range(probes)],
+        [ends(ref) for ref in (onsite, hop_right, hop_down)],
+        weights[0:1, 0:1],
+    )
     for at in range(needed, len(copies)):
         copies[at].wait()
+
+
+def edge_rows(block, weights, x0, adj_next, fwd_next, signs, lattice, lines, out):
+    edge, second, third = lines
+    groups, cols = block.groups, block.cols
+    lane = lane_of((groups, cols))
+
+    def next_rows(row):
+        return jnp.concatenate([adj_next[:, row, :], fwd_next[:, row, :]], axis=0)
+
+    def sign_rows(step, row):
+        sign = weights[0:1, step : step + 1] * signs[:, row, :].astype(jnp.float32)
+        return jnp.concatenate([sign, jnp.zeros_like(sign)], axis=0)
+
+    def hop(kind, row):
+        return lattice[kind][row : row + 1, :] * SCALE
+
+    def across(x, row):
+        right = jnp.broadcast_to(hop(1, row), x.shape)
+        after = jnp.where(lane == cols - 1, 0.0, right * turned(x, -1))
+        return hop(0, row) * x + after + jnp.where(lane == 0, 0.0, turned(right * x, 1))
+
+    x_edge, x_second, x_third = (block.gathered(x0, row) for row in lines)
+    down = hop(2, min(edge, second))
+    one = (
+        sign_rows(0, second)
+        - next_rows(second)
+        + across(x_second, second)
+        + down * x_edge
+        + hop(2, min(second, third)) * x_third
+    )
+    out[0:groups, :] = x_edge
+    out[groups : 2 * groups, :] = (
+        sign_rows(0, edge) - next_rows(edge) + across(x_edge, edge) + down * x_second
+    )
+    out[2 * groups : 3 * groups, :] = sign_rows(1, edge) - x_edge + down * one
+    misc = 3 * groups
+    for kind in range(3):
+        out[misc + kind : misc + kind + 1, :] = hop(kind, edge)
+    out[misc + 3 : misc + TILE, :] = jnp.zeros((TILE - 3, cols), jnp.float32)
 
 
 def strips(own, left, right, span):
@@ -204,10 +253,10 @@
     return [turned(both, -(WIDE * g + STEPS - 1)) for g in range(block.groups)]
 
 
-def tile_step(block, row, now, hops, sides, previous, sign, store, add):
+def tile_step(block, row, now, hops, sides, previous, sign, store, add, columns=None):
     lane = lane_of((TILE, LANES))
     tiles = block.tiles
-    for c in range(tiles):
+    for c in range(tiles) if columns is None else columns:
         at = pl.ds(TILE + row, TILE)
         hop_site, hop_after, hop_before, hop_under = (hops[kind, c, at, :] for kind in range(4))
         hop_over = hops[3, c, pl.ds(TILE + row - 1, TILE), :]
@@ -283,9 +332,27 @@
     return store
 
 
-def first_kernel(weights, x0, adj_next, fwd_next, signs, onsite, hop_right, hop_down, x1, hops, forces):
+def first_kernel(
+    weights, x0, adj_next, fwd_next, signs, onsite, hop_right, hop_down, x0_out, x1, hops, forces, messages
+):
     block = Block(*signs.shape)
     rows = block.rows
+    nothing = jnp.zeros((block.groups, block.cols), jnp.float32)
+    for row in (-1, rows):
+        block.scattered(x0_out, row, nothing)
+        block.scattered(x1, row, nothing)
+    for side, lines in enumerate(((0, 1, 2), (rows - 1, rows - 2, rows - 3))):
+        edge_rows(
+            block,
+            weights,
+            x0,
+            adj_next,
+            fwd_next,
+            signs,
+            (onsite, hop_right, hop_down),
+            lines,
+            messages.at[side],
+        )
     wide_lane = lane_of((rows, LANES))
     inside = pl.ds(TILE, rows)
     hop_before = 0.0
@@ -296,83 +363,63 @@
         hops[1, c, inside, :] = hop
         hops[2, c, inside, :] = jnp.where(wide_lane == 0, hop_before, hop_turned)
         hops[3, c, inside, :] = hop_down[:, lanes(c)] * SCALE
+        hops[3, c, pl.ds(TILE - 1, 1), :] = jnp.zeros((1, LANES), jnp.float32)
         hop_before = hop_turned
     for row in range(0, rows, TILE):
-        inner = 0 < row < rows - TILE
         tile_step(
             block,
             row,
-            x0,
+            x0_out,
             hops,
             None,
             block_reader(adj_next, fwd_next, row),
             sign_reader(signs, weights, 0, row),
             field_storer(block, x1, row),
-            force_adder(forces, row, True) if inner else None,
+            force_adder(forces, row, True),
         )
 
 
-def edge_rows(block, weights, x0, adj_next, fwd_next, signs, hops, strip_tile, rows, at, out):
-    edge, second, third = rows
-    groups, span = block.groups, block.span
-    field, base, (s_on, s_right, s_down) = strip_tile
-
-    def line(x, i):
-        return x[i : i + 1, :]
-
-    def next_rows(row):
-        return jnp.concatenate([adj_next[:, row, :], fwd_next[:, row, :]], axis=0)
-
-    def sign_rows(step, row):
-        sign = weights[0:1, step : step + 1] * signs[:, row, :].astype(jnp.float32)
-        return jnp.concatenate([sign, jnp.zeros_like(sign)], axis=0)
-
-    x_edge, x_second, x_third = (block.gathered(x0, row) for row in rows)
-    down = block.hop_row(hops, 3, min(edge, second))
-
-    def across(x, row, i):
-        return block.hop_row(hops, 0, row) * x + sideways(
-            x, block.hop_row(hops, 1, row), line(field, i), line(s_right, i), span
-        )
-
-    one = (
-        sign_rows(0, second)
-        - next_rows(second)
-        + across(x_second, second, at[1])
-        + down * x_edge
-        + block.hop_row(hops, 3, min(second, third)) * x_third
-    )
-    part_one = sign_rows(0, edge) - next_rows(edge) + across(x_edge, edge, at[0]) + down * x_second
-    part_two = sign_rows(1, edge) - x_edge + down * one
-    level = base + s_on * field + s_right * turned(field, -1) + turned(s_right, 1) * turned(field, 1)
-    strip_one = line(level, at[0]) + line(s_down, min(at[0], at[1])) * line(field, at[1])
-    out[0:groups, :] = x_edge
-    out[groups : 2 * groups, :] = part_one
-    out[2 * groups : 3 * groups, :] = part_two
+def at_ends(block, row):
+    return column_of(row, block.groups, STEPS - 1), column_of(row, block.groups, block.span + STEPS)
+
+
+def send_kernel(own, left, right, messages, to_odd, to_even, message):
+    rows, cols = own.shape[0], to_odd.shape[1]
+    groups = (to_odd.shape[0] - TILE) // 3
+    span = WIDE * groups
     misc = 3 * groups
-    out[misc : misc + 1, :] = block.hop_row(hops, 0, edge)
-    out[misc + 1 : misc + 2, :] = block.hop_row(hops, 1, edge)
-    out[misc + 2 : misc + 3, :] = block.hop_row(hops, 3, edge)
-    out[misc + 3 : misc + 4, 0 : 4 * LANES] = jnp.concatenate(
-        [line(field, at[0]), strip_one, line(s_down, at[0]), line(s_right, at[0])], axis=1
-    )
-    out[misc + 4 : misc + TILE, :] = jnp.zeros((TILE - 4, out.shape[1]), jnp.float32)
-
-
-def rows_kernel(weights, x0, adj_next, fwd_next, signs, hops, own, left, right, out_odd, out_even, message):
-    block = Block(*signs.shape)
-    rows = block.rows
-    for side, (lines, at, start) in enumerate(
-        (((0, 1, 2), (0, 1, 2), 0), ((rows - 1, rows - 2, rows - 3), (TILE - 1, TILE - 2, TILE - 3), rows - TILE))
-    ):
-        part = pl.ds(start, TILE)
-        strip_tile = strips(own[part, :], left[part, :], right[part, :], block.span)
-        edge_rows(
-            block, weights, x0, adj_next, fwd_next, signs, hops, strip_tile, lines, at, message.at[side]
+    lane = lane_of((groups, LANES))
+    left_part = lane_of((TILE, LANES)) < span
+    message[...] = messages[...]
+    for side, (edge, second) in enumerate(((0, 1), (TILE - 1, TILE - 2))):
+        part = pl.ds(side * (rows - TILE), TILE)
+        field, base, (s_on, s_right, s_down) = strips(own[part, :], left[part, :], right[part, :], span)
+        before = turned(s_right, 1)
+        level = base + s_on * field + s_right * turned(field, -1) + before * turned(field, 1)
+        inward = jnp.where(left_part, s_right, before) * field
+        down_inward = jnp.where(left_part, turned(s_down, -1), turned(s_down, 1))
+        bond = min(edge, second)
+        one = inward[edge : edge + 1, :]
+        two = down_inward[bond : bond + 1, :] * inward[second : second + 1, :]
+        for at, row in ((groups, one), (2 * groups, two)):
+            for start, value, spot in (
+                (0, column_of(row, groups, STEPS - 1), 0),
+                (cols - LANES, column_of(row, groups, span + STEPS), LANES - 1),
+            ):
+                where = (side, pl.ds(at, groups), pl.ds(start, LANES))
+                message[where] = message[where] + jnp.where(lane == spot, value, 0.0)
+        message[side, misc + 3 : misc + 4, 0 : 4 * LANES] = jnp.concatenate(
+            [
+                field[edge : edge + 1, :],
+                level[edge : edge + 1, :] + s_down[bond : bond + 1, :] * field[second : second + 1, :],
+                s_down[edge : edge + 1, :],
+                s_right[edge : edge + 1, :],
+            ],
+            axis=1,
         )
     odd = lax.rem(lax.axis_index("strip"), 2) == 1
-    out_odd[...] = jnp.where(odd, message[1], message[0])
-    out_even[...] = jnp.where(odd, message[0], message[1])
+    to_odd[...] = jnp.where(odd, message[1], message[0])
+    to_even[...] = jnp.where(odd, message[0], message[1])
 
 
 def strip_rows(block, strip, strip_base, strip_hops, step, row, count):
@@ -415,6 +462,13 @@
     rows, tiles, probes = block.rows, block.tiles, block.probes
     inside = pl.ds(TILE, rows)
     lane = lane_of((TILE, LANES))
+    nothing = jnp.zeros((block.groups, block.cols), jnp.float32)
+    for row in (-1, rows):
+        block.scattered(x2, row, nothing)
+    for row in (TILE - 1, TILE + rows):
+        strip_hops[2, row : row + 1, :] = jnp.zeros((1, LANES), jnp.float32)
+        for step in range(2):
+            strip[step, row : row + 1, :] = jnp.zeros((1, LANES), jnp.float32)
     field, base, (s_on, s_right, s_down) = strips(own[...], left[...], right[...], block.span)
     sign_strip = jnp.where(lane_of(base.shape) < block.span, turned(base, 2), turned(base, -2))
     strip[0, inside, :] = field
@@ -436,22 +490,18 @@
             x1[spot] = x1[spot] + jnp.where(lane == 0, hop_first * sides[g], 0.0)
             spot = block.at(g, last, row)
             x1[spot] = x1[spot] + jnp.where(lane == LANES - 1, hop_last * sides[g], 0.0)
-        if 0 < row < rows - TILE:
-            total = None
-            for p in range(probes):
-                q = probes + p
-                term = x0[block.at(p, last, row)] * sides[q] + sides[p] * x0[block.at(q, last, row)]
-                total = term if total is None else total + term
-            spot = (0, pl.ds(row, TILE), lanes(last))
-            forces[spot] = forces[spot] + jnp.where(lane == LANES - 1, total, 0.0)
+        total = None
+        for p in range(probes):
+            q = probes + p
+            term = x0[block.at(p, last, row)] * sides[q] + sides[p] * x0[block.at(q, last, row)]
+            total = term if total is None else total + term
+        spot = (0, pl.ds(row, TILE), lanes(last))
+        forces[spot] = forces[spot] + jnp.where(lane == LANES - 1, total, 0.0)
 
     for step in (1, 2):
         strip_rows(block, strip, strip_base, strip_hops, step - 1, 0, rows)
+        now, before = (x1, x0) if step == 1 else (x2, x1)
         for row in range(0, rows, TILE):
-            inner = 0 < row < rows - TILE
-            if step == 2 and not inner:
-                continue
-            now, before = (x1, x0) if step == 1 else (x2, x1)
             tile_step(
                 block,
                 row,
@@ -461,88 +511,139 @@
                 field_reader(block, before, row),
                 sign_reader(signs, weights, step, row),
                 field_storer(block, x2, row) if step == 1 else block_storer(adj_out, fwd_out, row),
-                force_adder(forces, row, False) if inner else None,
+                force_adder(forces, row, False),
             )
 
 
-def outer_kernel(
-    weights, adj_next, fwd_next, signs, strip_base, received_odd, received_even, *refs
-):
-    x0, x1, x2, hops, forces, adj_out, fwd_out, strip, strip_hops, message = refs[9:]
-    block = Block(*signs.shape)
-    rows, groups, span = block.rows, block.groups, block.span
+def sorted_messages(received_odd, received_even, message):
     odd = lax.rem(lax.axis_index("strip"), 2) == 1
     message[0] = jnp.where(odd, received_even[...], received_odd[...])
     message[1] = jnp.where(odd, received_odd[...], received_even[...])
-    above, below = message.at[0], message.at[1]
+    return message.at[0], message.at[1]
+
+
+def other_field(x):
+    return pltpu.roll(x, x.shape[0] // 2, 0)
+
+
+def outer_kernel(
+    x0, x1, x2, hops, strip, strip_hops, received_odd, received_even, forces_in, adj_in, fwd_in, *refs
+):
+    del forces_in, adj_in, fwd_in
+    forces, adj_out, fwd_out, message = refs
+    probes, rows, cols = adj_out.shape
+    block = Block(probes, rows, cols)
+    groups, span = block.groups, block.span
     misc = 3 * groups
-    corner_above = above[misc + 3 : misc + 4, 0 : 4 * LANES]
-    corner_below = below[misc + 3 : misc + 4, 0 : 4 * LANES]
-    over, under = TILE - 1, TILE + rows
-    strip[0, over : over + 1, :] = corner_above[:, :LANES]
-    strip[0, under : under + 1, :] = corner_below[:, :LANES]
-    s_over = corner_above[:, 2 * LANES : 3 * LANES]
-    s_under = strip_hops[2, under - 1 : under, :]
-    strip_hops[2, over : over + 1, :] = s_over
-    one_above = corner_above[:, LANES : 2 * LANES] + s_over * strip[0, TILE : TILE + 1, :]
-    one_below = corner_below[:, LANES : 2 * LANES] + s_under * strip[0, under - 1 : under, :]
-    strip[1, over : over + 1, :] = one_above
-    strip[1, under : under + 1, :] = one_below
-    for c in range(block.tiles):
-        hops[3, c, over : over + 1, :] = above[misc + 2 : misc + 3, c * LANES : (c + 1) * LANES]
-    block.scattered(x0, -1, above[0:groups, :])
-    block.scattered(x0, rows, below[0:groups, :])
-
-    edges = (0, rows - TILE)
-    hop_above = block.hop_row(hops, 3, -1)
-    hop_below = block.hop_row(hops, 3, rows - 1)
-    for step in range(STEPS):
-        now = (x0, x1, x2)[step]
-        for row in edges:
-            previous = (
-                block_reader(adj_next, fwd_next, row) if step == 0 else field_reader(block, (x0, x1)[step - 1], row)
+    lane = lane_of((groups, cols))
+    messages = sorted_messages(received_odd, received_even, message)
+
+    def s_line(ref, at, row):
+        return ref[at, TILE + row : TILE + row + 1, :]
+
+    def neighbours(x, strip_row):
+        first, last = at_ends(block, strip_row)
+        before = jnp.where(lane == 0, first, turned(x, 1))
+        return before, jnp.where(lane == cols - 1, last, turned(x, -1))
+
+    for side, source in enumerate(messages):
+        edge, second, third = (0, 1, 2) if side == 0 else (rows - 1, rows - 2, rows - 3)
+        bond, next_bond = (edge, second) if side == 0 else (second, third)
+        corner = source[misc + 3 : misc + 4, 0 : 4 * LANES]
+        c_field, c_one, c_down, c_right = (corner[:, k * LANES : (k + 1) * LANES] for k in range(4))
+        hop_out = source[misc + 2 : misc + 3, :] if side == 0 else block.hop_row(hops, 3, edge)
+        s_out = c_down if side == 0 else s_line(strip_hops, 2, edge)
+        hop_in, hop_next = block.hop_row(hops, 3, bond), block.hop_row(hops, 3, next_bond)
+
+        def across(x, pair, row):
+            before, after = pair
+            return (
+                block.hop_row(hops, 0, row) * x
+                + block.hop_row(hops, 1, row) * after
+                + block.hop_row(hops, 2, row) * before
             )
-            store = (
-                block_storer(adj_out, fwd_out, row)
-                if step == STEPS - 1
-                else field_storer(block, (x1, x2)[step], row)
+
+        s_right = s_line(strip_hops, 1, edge)
+        s_one_beyond = c_one + s_out * s_line(strip, 0, edge)
+        s_one = s_out * c_field
+        s_two = (
+            s_line(strip_hops, 0, edge) * s_one
+            + s_right * turned(s_one, -1)
+            + turned(s_right, 1) * turned(s_one, 1)
+            + s_out * s_one_beyond
+        )
+        s_two_second = s_line(strip_hops, 2, bond) * s_one
+
+        x0_edge, x1_edge, x2_edge = (block.gathered(x, edge) for x in (x0, x1, x2))
+        x1_second, x2_second = (block.gathered(x, second) for x in (x1, x2))
+        x2_third = block.gathered(x2, third)
+        x0_beyond = source[0:groups, :]
+        one = hop_out * x0_beyond
+        one_pair = neighbours(one, s_one)
+        x1_beyond = source[groups : 2 * groups, :] + hop_out * x0_edge
+        two = across(one, one_pair, edge) + hop_out * x1_beyond
+        two_pair = neighbours(two, s_two)
+        two_second = hop_in * one
+        two_second_pair = neighbours(two_second, s_two_second)
+        x1_new = x1_edge + one
+        x2_beyond = (
+            source[2 * groups : 3 * groups, :]
+            + source[misc : misc + 1, :] * x1_beyond
+            + sideways(x1_beyond, source[misc + 1 : misc + 2, :], s_one_beyond, c_right, span)
+            + hop_out * x1_new
+        )
+        x2_new, x2_second_new = x2_edge + two, x2_second + two_second
+        changes = (
+            (edge, across(two, two_pair, edge) + hop_in * two_second + hop_out * x2_beyond - one),
+            (second, across(two_second, two_second_pair, second) + hop_in * two),
+            (third, hop_next * two_second),
+        )
+        for row, change in changes:
+            adj_out[:, row, :] = adj_out[:, row, :] + change[:probes]
+            fwd_out[:, row, :] = fwd_out[:, row, :] + change[probes:]
+
+        def changed(x, change, new, other, other_change):
+            return change * other_field(other) + x * other_field(other_change)
+
+        def right_of(x, strip_row):
+            return jnp.where(lane == cols - 1, column_of(strip_row, groups, span + STEPS), turned(x, -1))
+
+        one_right = right_of(x1_new, s_line(strip, 1, edge) + s_one)
+        two_right = right_of(x2_new, s_line(strip, 2, edge) + s_two)
+        second_right = right_of(x2_second_new, s_line(strip, 2, second) + s_two_second)
+        terms = [
+            (
+                0,
+                edge,
+                changed(x1_edge, one, x1_new, one_right, one_pair[1])
+                + changed(x2_edge, two, x2_new, two_right, two_pair[1]),
+            ),
+            (0, second, changed(x2_second, two_second, x2_second_new, second_right, two_second_pair[1])),
+            (1, bond, changed(x2_edge, two, x2_new, x2_second_new, two_second) + one * other_field(x1_second)),
+            (1, next_bond, two_second * other_field(x2_third)),
+            (2, edge, 0.5 * (changed(x1_edge, one, x1_new, x1_new, one) + changed(x2_edge, two, x2_new, x2_new, two))),
+            (2, second, 0.5 * changed(x2_second, two_second, x2_second_new, x2_second_new, two_second)),
+        ]
+        if side == 1:
+            outward = (
+                x0_edge * other_field(x0_beyond)
+                + x1_new * other_field(x1_beyond)
+                + x2_new * other_field(x2_beyond)
             )
-            tile_step(
-                block,
-                row,
-                now,
-                hops,
-                beside(block, strip[step, pl.ds(TILE + row, TILE), :]),
-                previous,
-                sign_reader(signs, weights, step, row),
-                store,
-                force_adder(forces, row, step == 0),
-            )
-        if step == STEPS - 1:
-            break
-        for row in edges:
-            strip_rows(block, strip, strip_base, strip_hops, step, row, TILE)
-        if step == 0:
-            block.scattered(x1, -1, above[groups : 2 * groups, :] + hop_above * block.gathered(x0, 0))
-            block.scattered(x1, rows, below[groups : 2 * groups, :] + hop_below * block.gathered(x0, rows - 1))
-        else:
-            for source, hop, corner, strip_row, edge, inside in (
-                (above, hop_above, corner_above, one_above, -1, 0),
-                (below, hop_below, corner_below, one_below, rows, rows - 1),
-            ):
-                line = block.gathered(x1, edge)
-                value = (
-                    source[2 * groups : 3 * groups, :]
-                    + source[misc : misc + 1, :] * line
-                    + sideways(line, source[misc + 1 : misc + 2, :], strip_row, corner[:, 3 * LANES :], span)
-                    + hop * block.gathered(x1, inside)
-                )
-                block.scattered(x2, edge, value)
+            terms.append((1, edge, outward))
+        for kind, row, term in terms:
+            spot = (kind, pl.ds(row, 1), slice(None))
+            forces[spot] = forces[spot] + jnp.sum(term, axis=0, keepdims=True)
 
 
 def sum_kernel(mine, other, right_out, down_out, site_out):
     for at, out in enumerate((right_out, down_out, site_out)):
         out[...] = (mine[at] + other[at]) * SCALE
+
+
+def both_sides(x):
+    left = shifted(x, "col", 1)
+    return left, left if lax.axis_size("col") == 2 else shifted(x, "col", -1)
 
 
 def in_vmem(*arrays):
@@ -596,6 +697,7 @@
         hop_down,
     )
     sources = tuple(pltpu.with_memory_space_constraint(v, pltpu.HBM) for v in sources)
+    strip_tile = pltpu.VMEM((rows, LANES), f32)
     x0, adj_next, fwd_next, sign, on, hr, hd, weights, packed = call(
         load_kernel,
         "load",
@@ -609,37 +711,34 @@
             like(hop_right),
             like(hop_down),
             pltpu.VMEM((1, STEPS), f32),
-            pltpu.VMEM((rows, LANES), f32),
+            strip_tile,
         ),
-        [pltpu.SemaphoreType.DMA((7 + 2 * tiles,))],
+        [pltpu.SemaphoreType.DMA((13 + 2 * tiles,))],
         in_spec=hbm,
     )
     x0 = x0.reshape(block.field_shape)
-    left = shifted(packed, "col", 1)
-    right = left if lax.axis_size("col") == 2 else shifted(packed, "col", -1)
-
-    x0, adj_next, fwd_next, sign, on, hr, hd, weights = in_vmem(
-        x0, adj_next, fwd_next, sign, on, hr, hd, weights
-    )
+    left, right = both_sides(packed)
+
+    x0, adj_next, fwd_next, sign, on, hr, hd, weights, packed = in_vmem(
+        x0, adj_next, fwd_next, sign, on, hr, hd, weights, packed
+    )
+    message = pltpu.VMEM((3 * groups + TILE, cols), f32)
+    both_messages = pltpu.VMEM((2, 3 * groups + TILE, cols), f32)
     field = pltpu.VMEM(block.field_shape, f32)
     hops_shape = pltpu.VMEM((4, tiles, tall, LANES), f32)
     forces_shape = pltpu.VMEM((3, rows, cols), f32)
-    x1, hops, forces = call(
+    x0, x1, hops, forces, messages = call(
         first_kernel,
-        "first_step",
+        "step_0",
         (weights, x0, adj_next, fwd_next, sign, on, hr, hd),
-        (field, hops_shape, forces_shape),
+        (field, field, hops_shape, forces_shape, both_messages),
+        aliases={1: 0},
         flops=COST,
     )
 
-    x1, hops, forces, own, left, right = in_vmem(x1, hops, forces, packed, left, right)
-    message = pltpu.VMEM((3 * groups + TILE, cols), f32)
+    x0, x1, hops, forces, messages, left, right = in_vmem(x0, x1, hops, forces, messages, left, right)
     to_odd, to_even = call(
-        rows_kernel,
-        "edge_rows",
-        (weights, x0, adj_next, fwd_next, sign, hops, own, left, right),
-        (message, message),
-        [pltpu.VMEM((2, 3 * groups + TILE, cols), f32)],
+        send_kernel, "edge_rows", (packed, left, right, messages), (message, message), [both_messages]
     )
     received_odd = pair_swap(to_odd, "strip", 1)
     received_even = pair_swap(to_even, "strip", 0)
@@ -648,7 +747,7 @@
     x1, hops, forces, x2, adj_out, fwd_out, strip, strip_base, strip_hops = call(
         inner_kernel,
         "inner_steps",
-        (weights, x0, sign, own, left, right, sent, x1, hops, forces),
+        (weights, x0, sign, packed, left, right, sent, x1, hops, forces),
         (
             field,
             hops_shape,
@@ -664,18 +763,17 @@
         flops=COST,
     )
 
-    kept = in_vmem(x0, x1, x2, hops, forces, adj_out, fwd_out, strip, strip_hops)
-    read = (weights, adj_next, fwd_next, sign) + in_vmem(strip_base, received_odd, received_even)
-    outs = call(
+    kept = in_vmem(forces, adj_out, fwd_out)
+    read = (x0,) + in_vmem(x1, x2, hops, strip, strip_hops, received_odd, received_even)
+    forces, adjoint_out, forward_out = call(
         outer_kernel,
         "outer_rows",
         read + kept,
         tuple(like(v) for v in kept),
-        [pltpu.VMEM((2, 3 * groups + TILE, cols), f32)],
+        [both_messages],
         aliases={len(read) + i: i for i in range(len(kept))},
         flops=COST,
     )
-    forces, adjoint_out, forward_out = outs[4:7]
 
     other = shifted(forces, "probe", 1)
     plain = jax.ShapeDtypeStruct((rows, cols), f32)

time: 20.7 us -> 19.9 us (0.961)
  waiting for transfers between devices: 2.23 us -> 1.22 us
  Pallas kernels: 8.78 us -> 9.03 us
    ppermute x2, waiting for transfers between devices: 1.15 us -> 0.26 us  [pair_swap(): return lax.ppermute(x, axis, pairs)]
    pallas_call x6, Pallas kernels: 8.78 us -> 9.03 us  [call(): pl.pallas_call(kernel, out_shape=outs, in_specs=[in_spec] * len(inputs),...]
  transfers between devices with their start and end apart: 4 -> 4, of which waited for: 3 -> 3; matrix products, arithmetic and copies ran while one was open for 8% -> 8% of each run, Pallas kernels for 20% -> 26%
where the time goes in v3:
time: 19.9 us; the launch traced here: 19.8 us
  Pallas kernels  9.03 us (45%)
  starting transfers between devices  7.26 us (36%)
  local copies, waits for them, and re-layouts  1.59 us (8%)
  waiting for transfers between devices  1.22 us (6%)
  between operations  0.67 us (3%)
    pallas_call x6, Pallas kernels, call(): pl.pallas_call(kernel, out_shape=outs, in_specs=[in_spec] * len(inputs),...  9.03 us
    ppermute x2, starting transfers between devices, pair_swap(): return lax.ppermute(x, axis, pairs)  4.18 us
    ppermute x2, starting transfers between devices, shifted(): return lax.ppermute(x, axis, [(i, (i + by) % size) for i in range(size)])  3.07 us
    unnamed x2, local copies, waits for them, and re-layouts  1.59 us
    ppermute x2, waiting for transfers between devices, shifted(): return lax.ppermute(x, axis, [(i, (i + by) % size) for i in range(size)])  0.95 us
  transfers between devices with their start and end apart: 4, of which 3 were waited for; matrix products, arithmetic and copies ran while one was open for 8% of the time, Pallas kernels for 26%

profile of v3, /device:TPU:0, one launch (start us, length us, event | category | flops | bytes accessed | tf_op | source)
XLA Modules:
  0.0 19.8 jit_solution(12403311255582852218)
XLA Ops:
  0.6 2.2 %load.1 = (f32[8,4,80,128]{3,2,1,0:T(8,128)S(1)}, f32[4,64,512]{2,1,0:T(8,128)S(1)}, f32[4,64,512]{2,1,0:T(8,128)S(1)}, s32[4,64,512]{2,1,0:T(8,128)S(1)}, f32[6...) custom-call(f32[1,3]{1,0:T(1,128)} %bitcast.3, ...), custom_call_target="tpu_custom_call" | custom-call | tf_op jit(solution)/shard_map/load/pallas_call | solution.py:673
  2.8 3.0 %collective-permute-start = (f32[64,128]{1,0:T(8,128)S(1)}, f32[64,128]{1,0:T(8,128)S(1)}, u32[]{:S(2)}, u32[]{:S(2)}) collective-permute-start(f32[64,128]{1,0:T(8,128)S(1)} %get-tuple-element.44.own), channel_id=1, source_target_pairs={{0,2},{2,0},{1,3},{3,1},{4,6},{6,4},{5,7},{7,5},{8,10},{10,8},{9,1... | collective-permute-start | bytes 98312 | tf_op jit(solution)/shard_map/ppermute | solution.py:21
  5.8 1.1 %step_0.1 = (f32[2560,128]{1,0:T(8,128)S(1)}, f32[2560,128]{1,0:T(8,128)S(1)}, f32[4,4,80,128]{3,2,1,0:T(8,128)S(1)}, f32[3,64,512]{2,1,0:T(8,128)S(1)}, f32[2,32,512]{2,1,0:T(8,128)S(1)}) custom-call(f32[1,3]{1,0:T(1,128)S(1)} %get-tuple-element.35.weights, f32[2560,128]{1,0:T(8,128)S(1)} %bitcast.2, ...), custom_call_target="tpu_custom_call", output_to_operand_aliasing={{0}: (1, {})} | custom-call | flops 4000000 | bytes 4000000 | tf_op jit(solution)/shard_map/step_0/pallas_call | solution.py:673
  6.9 0.8 %collective-permute-done.left.right = f32[64,128]{1,0:T(8,128)S(1)} collective-permute-done((f32[64,128]{1,0:T(8,128)S(1)}, f32[64,128]{1,0:T(8,128)S(1)}, u32[]{:S(2)}, u32[]{:S(2)}) %collective-permute-start) | collective-permute-done | bytes 32800 | tf_op jit(solution)/shard_map/ppermute | solution.py:21
  7.7 0.4 %edge_rows.1 = (f32[32,512]{1,0:T(8,128)S(1)}, f32[32,512]{1,0:T(8,128)S(1)}) custom-call(f32[64,128]{1,0:T(8,128)S(1)} %get-tuple-element.44.own, f32[64,128]{1,0:T(8,128)S(1)} %collective-permute-done.left.right, f32[64,128]{1,0:T(8,128)S(1)} %collective-permute-done.left.right, f32[2,32,512]{2,1,0:T(8,128)S(1)} %get-tuple-element.45.messages), custom_call_target="tpu_custom_call" | custom-call | tf_op jit(solution)/shard_map/edge_rows/pallas_call | solution.py:673
  8.1 4.2 %collective-permute-start.1 = (f32[32,512]{1,0:T(8,128)S(1)}, f32[32,512]{1,0:T(8,128)S(1)}, u32[]{:S(2)}, u32[]{:S(2)}) collective-permute-start(f32[32,512]{1,0:T(8,128)S(1)} %get-tuple-element.55), channel_id=1, source_target_pairs={{4,8},{8,4},{12,0},{0,12},{5,9},{9,5},{13,1},{1,13},{6,10},{10,6},... | collective-permute-start | bytes 196616 | tf_op jit(solution)/shard_map/ppermute | solution.py:37
  12.3 0.0 collective-permute-start.2
  12.3 4.0 %inner_steps.1 = (f32[2560,128]{1,0:T(8,128)S(1)}, f32[4,4,80,128]{3,2,1,0:T(8,128)S(1)}, f32[3,64,512]{2,1,0:T(8,128)S(1)}, f32[2560,128]{1,0:T(8,128)S(1)}, f3...) custom-call(f32[1,3]{1,0:T(1,128)S(1)} %get-tuple-element.35.weights, ...), custom_call_target="tpu_custom_call", output_to_operand_aliasing={{0}: (7, {}), {1}: (8, {}), {2}: (9, {})} | custom-call | flops 4000000 | bytes 4000000 | tf_op jit(solution)/shard_map/inner_steps/pallas_call | solution.py:673
  16.3 0.0 collective-permute-done.1.received_odd
  16.3 0.3 %collective-permute-done.2.received_even = f32[32,512]{1,0:T(8,128)S(1)} collective-permute-done((f32[32,512]{1,0:T(8,128)S(1)}, f32[32,512]{1,0:T(8,128)S(1)}, u32[]{:S(2)}, u32[]{:S(2)}) %collective-permute-start.2) | collective-permute-done | bytes 65568 | tf_op jit(solution)/shard_map/ppermute | solution.py:37
  16.6 0.6 %outer_rows.1 = (f32[3,64,512]{2,1,0:T(8,128)S(1)}, f32[4,64,512]{2,1,0:T(8,128)S(1)}, f32[4,64,512]{2,1,0:T(8,128)S(1)}) custom-call(f32[2560,128]{1,0:T(8,128)S(1)} %get-tuple-element.43.x0, f32[2560,128]{1,0:T(8,128)S(1)} %get-tuple-element.50.x1, ...), custom_call_target="tpu_custom_call", output_to_operand_aliasing={{0}: (8, {}), {1}: (9, {}), {2}: (10, {})} | custom-call | flops 4000000 | bytes 4000000 | tf_op jit(solution)/shard_map/outer_rows/pallas_call | solution.py:673
  17.2 0.1 collective-permute-start.3
  17.3 0.8 %copy.28 = f32[4,64,512]{2,1,0:T(8,128)} copy(f32[4,64,512]{2,1,0:T(8,128)S(1)} %get-tuple-element.68) | data formatting | bytes 1048576
  18.1 0.8 %copy.29 = f32[4,64,512]{2,1,0:T(8,128)} copy(f32[4,64,512]{2,1,0:T(8,128)S(1)} %get-tuple-element.69) | data formatting | bytes 1048576
  18.9 0.1 collective-permute-done.3.other
  19.0 0.8 %force_sums.1 = (f32[64,512]{1,0:T(8,128)}, f32[64,512]{1,0:T(8,128)}, f32[64,512]{1,0:T(8,128)}) custom-call(f32[3,64,512]{2,1,0:T(8,128)S(1)} %get-tuple-element.59.mine, f32[3,64,512]{2,1,0:T(8,128)S(1)} %collective-permute-done.3.other), custom_call_target="tpu_custom_call" | custom-call | tf_op jit(solution)/shard_map/force_sums/pallas_call | solution.py:673
Async XLA Ops:
  2.8 4.9 %collective-permute-start = (f32[64,128]{1,0:T(8,128)S(1)}, f32[64,128]{1,0:T(8,128)S(1)}, u32[]{:S(2)}, u32[]{:S(2)}) collective-permute-start(f32[64,128]{1,0:T(8,128)S(1)} %get-tuple-element.44.own), channel_id=1, source_target_pairs={{0,2},{2,0},{1,3},{3,1},{4,6},{6,4},{5,7},{7,5},{8,10},{10,8},{9,1... | collective-permute-start | bytes 98312 | tf_op jit(solution)/shard_map/ppermute | solution.py:21
  8.1 8.2 %collective-permute-start.1 = (f32[32,512]{1,0:T(8,128)S(1)}, f32[32,512]{1,0:T(8,128)S(1)}, u32[]{:S(2)}, u32[]{:S(2)}) collective-permute-start(f32[32,512]{1,0:T(8,128)S(1)} %get-tuple-element.55), channel_id=1, source_target_pairs={{4,8},{8,4},{12,0},{0,12},{5,9},{9,5},{13,1},{1,13},{6,10},{10,6},... | collective-permute-start | bytes 196616 | tf_op jit(solution)/shard_map/ppermute | solution.py:37
  12.3 4.3 %collective-permute-start.2 = (f32[32,512]{1,0:T(8,128)S(1)}, f32[32,512]{1,0:T(8,128)S(1)}, u32[]{:S(2)}, u32[]{:S(2)}) collective-permute-start(f32[32,512]{1,0:T(8,128)S(1)} %get-tuple-element.46.sent), channel_id=1, source_target_pairs={{0,4},{4,0},{8,12},{12,8},{1,5},{5,1},{9,13},{13,9},{2,6},{6,2},{1... | collective-permute-start | bytes 196616 | tf_op jit(solution)/shard_map/ppermute | solution.py:37
  17.2 1.8 %collective-permute-start.3 = (f32[3,64,512]{2,1,0:T(8,128)S(1)}, f32[3,64,512]{2,1,0:T(8,128)S(1)}, u32[]{:S(2)}, u32[]{:S(2)}) collective-permute-start(f32[3,64,512]{2,1,0:T(8,128)S(1)} %get-tuple-element.59.mine), channel_id=1, source_target_pairs={{0,1},{1,0},{2,3},{3,2},{4,5},{5,4},{6,7},{7,6},{8,9},{9,8},{10,11... | collective-permute-start | bytes 1179656 | tf_op jit(solution)/shard_map/ppermute | solution.py:21

commit v4 on v3

--- a/solution.py
+++ b/solution.py
@@ -23,6 +23,10 @@
 
 def lane_of(shape):
     return lax.broadcasted_iota(jnp.int32, shape, len(shape) - 1)
+
+
+def lanes_from(x, source):
+    return jnp.take_along_axis(x, source, axis=1, mode="promise_in_bounds")
 
 
 def turned(x, by):
@@ -185,31 +189,23 @@
     base = jnp.where(below, turned(low, -span), high)
     coefficients = []
     for at in range(3):
-        start = 2 * span + WIDE * at
-        x = jnp.where(
-            lane < WIDE,
-            turned(low, -start),
-            jnp.where((lane >= span) & (lane < span + WIDE), turned(high, span - start), 0.0),
-        )
-        reach = WIDE
-        while reach < span:
-            x = x + turned(x, reach)
-            reach *= 2
-        coefficients.append(x * SCALE)
+        source = 2 * span + WIDE * at + lax.rem(lane, WIDE)
+        coefficients.append(jnp.where(below, lanes_from(low, source), lanes_from(high, source)) * SCALE)
     return field, base, coefficients
 
 
-def column_of(row, groups, at):
+def column_of(row, groups, at, cols=LANES):
     shape = (groups, LANES)
-    wanted = WIDE * lax.broadcasted_iota(jnp.int32, shape, 0) + at
-    return jnp.sum(jnp.where(lane_of(shape) == wanted, row, 0.0), axis=1, keepdims=True)
+    source = WIDE * lax.broadcasted_iota(jnp.int32, shape, 0) + at
+    value = lanes_from(jnp.broadcast_to(row, shape), source)
+    return jnp.concatenate([value] * (cols // LANES), axis=1)
 
 
 def sideways(x, hop, strip_row, hop_row, span):
     groups, cols = x.shape
     lane = lane_of(x.shape)
-    before = jnp.where(lane == 0, column_of(strip_row, groups, STEPS - 1), turned(x, 1))
-    after = jnp.where(lane == cols - 1, column_of(strip_row, groups, span + STEPS), turned(x, -1))
+    before = jnp.where(lane == 0, column_of(strip_row, groups, STEPS - 1, cols), turned(x, 1))
+    after = jnp.where(lane == cols - 1, column_of(strip_row, groups, span + STEPS, cols), turned(x, -1))
     hop = jnp.broadcast_to(hop, x.shape)
     hop_before = jnp.where(lane == 0, hop_row[:, STEPS - 1 : STEPS], turned(hop, 1))
     return hop * after + hop_before * before
@@ -333,14 +329,14 @@
 
 
 def first_kernel(
-    weights, x0, adj_next, fwd_next, signs, onsite, hop_right, hop_down, x0_out, x1, hops, forces, messages
+    weights, x0, adj_next, fwd_next, signs, onsite, hop_right, hop_down, x0_out, x1, x2, hops, forces, messages
 ):
     block = Block(*signs.shape)
     rows = block.rows
     nothing = jnp.zeros((block.groups, block.cols), jnp.float32)
     for row in (-1, rows):
-        block.scattered(x0_out, row, nothing)
-        block.scattered(x1, row, nothing)
+        for x in (x0_out, x1, x2):
+            block.scattered(x, row, nothing)
     for side, lines in enumerate(((0, 1, 2), (rows - 1, rows - 2, rows - 3))):
         edge_rows(
             block,
@@ -377,10 +373,26 @@
             field_storer(block, x1, row),
             force_adder(forces, row, True),
         )
+    for row in range(0, rows, TILE):
+        tile_step(
+            block,
+            row,
+            x1,
+            hops,
+            None,
+            field_reader(block, x0_out, row),
+            sign_reader(signs, weights, 1, row),
+            field_storer(block, x2, row),
+            force_adder(forces, row, False),
+            range(1, block.tiles - 1),
+        )
 
 
 def at_ends(block, row):
-    return column_of(row, block.groups, STEPS - 1), column_of(row, block.groups, block.span + STEPS)
+    return (
+        column_of(row, block.groups, STEPS - 1, block.cols),
+        column_of(row, block.groups, block.span + STEPS, block.cols),
+    )
 
 
 def send_kernel(own, left, right, messages, to_odd, to_even, message):
@@ -445,26 +457,24 @@
     right,
     sent,
     x1_in,
+    x2_in,
     hops_in,
     forces_in,
     x1,
+    x2,
     hops,
     forces,
-    x2,
     adj_out,
     fwd_out,
     strip,
     strip_base,
     strip_hops,
 ):
-    del sent, x1_in, hops_in, forces_in
+    del sent, x1_in, x2_in, hops_in, forces_in
     block = Block(*signs.shape)
     rows, tiles, probes = block.rows, block.tiles, block.probes
     inside = pl.ds(TILE, rows)
     lane = lane_of((TILE, LANES))
-    nothing = jnp.zeros((block.groups, block.cols), jnp.float32)
-    for row in (-1, rows):
-        block.scattered(x2, row, nothing)
     for row in (TILE - 1, TILE + rows):
         strip_hops[2, row : row + 1, :] = jnp.zeros((1, LANES), jnp.float32)
         for step in range(2):
@@ -512,6 +522,7 @@
                 sign_reader(signs, weights, step, row),
                 field_storer(block, x2, row) if step == 1 else block_storer(adj_out, fwd_out, row),
                 force_adder(forces, row, False),
+                sorted({0, last}) if step == 1 else None,
             )
 
 
@@ -606,7 +617,7 @@
             return change * other_field(other) + x * other_field(other_change)
 
         def right_of(x, strip_row):
-            return jnp.where(lane == cols - 1, column_of(strip_row, groups, span + STEPS), turned(x, -1))
+            return jnp.where(lane == cols - 1, column_of(strip_row, groups, span + STEPS, cols), turned(x, -1))
 
         one_right = right_of(x1_new, s_line(strip, 1, edge) + s_one)
         two_right = right_of(x2_new, s_line(strip, 2, edge) + s_two)
@@ -636,6 +647,16 @@
             forces[spot] = forces[spot] + jnp.sum(term, axis=0, keepdims=True)
 
 
+def store_kernel(adj, fwd, adj_out, fwd_out, done):
+    copies = []
+    for source, target in ((adj, adj_out), (fwd, fwd_out)):
+        for p in range(source.shape[0]):
+            copies.append(pltpu.make_async_copy(source.at[p], target.at[p], done.at[len(copies)]))
+            copies[-1].start()
+    for each in copies:
+        each.wait()
+
+
 def sum_kernel(mine, other, right_out, down_out, site_out):
     for at, out in enumerate((right_out, down_out, site_out)):
         out[...] = (mine[at] + other[at]) * SCALE
@@ -669,12 +690,12 @@
     hbm = pl.BlockSpec(memory_space=pltpu.HBM)
     params = pltpu.CompilerParams(vmem_limit_bytes=VMEM_LIMIT)
 
-    def call(kernel, name, inputs, outs, scratch=(), aliases=None, flops=0, in_spec=vmem):
+    def call(kernel, name, inputs, outs, scratch=(), aliases=None, flops=0, in_spec=vmem, out_spec=vmem):
         return pl.pallas_call(
             kernel,
             out_shape=outs,
             in_specs=[in_spec] * len(inputs),
-            out_specs=(vmem,) * len(outs),
+            out_specs=(out_spec,) * len(outs),
             scratch_shapes=list(scratch),
             input_output_aliases=aliases or {},
             compiler_params=params,
@@ -727,16 +748,17 @@
     field = pltpu.VMEM(block.field_shape, f32)
     hops_shape = pltpu.VMEM((4, tiles, tall, LANES), f32)
     forces_shape = pltpu.VMEM((3, rows, cols), f32)
-    x0, x1, hops, forces, messages = call(
+    x0, x1, x2, hops, forces, messages = call(
         first_kernel,
         "step_0",
         (weights, x0, adj_next, fwd_next, sign, on, hr, hd),
-        (field, field, hops_shape, forces_shape, both_messages),
+        (field, field, field, hops_shape, forces_shape, both_messages),
         aliases={1: 0},
         flops=COST,
     )
 
-    x0, x1, hops, forces, messages, left, right = in_vmem(x0, x1, hops, forces, messages, left, right)
+    x0, x1, x2, hops, forces = in_vmem(x0, x1, x2, hops, forces)
+    messages, left, right = in_vmem(messages, left, right)
     to_odd, to_even = call(
         send_kernel, "edge_rows", (packed, left, right, messages), (message, message), [both_messages]
     )
@@ -744,22 +766,22 @@
     received_even = pair_swap(to_even, "strip", 0)
 
     (sent,) = in_vmem(to_even)
-    x1, hops, forces, x2, adj_out, fwd_out, strip, strip_base, strip_hops = call(
+    x1, x2, hops, forces, adj_out, fwd_out, strip, strip_base, strip_hops = call(
         inner_kernel,
         "inner_steps",
-        (weights, x0, sign, packed, left, right, sent, x1, hops, forces),
+        (weights, x0, sign, packed, left, right, sent, x1, x2, hops, forces),
         (
+            field,
             field,
             hops_shape,
             forces_shape,
-            field,
             like(adjoint_now),
             like(forward_now),
             pltpu.VMEM((STEPS, tall, LANES), f32),
             pltpu.VMEM((2, rows, LANES), f32),
             pltpu.VMEM((3, tall, LANES), f32),
         ),
-        aliases={7: 0, 8: 1, 9: 2},
+        aliases={7: 0, 8: 1, 9: 2, 10: 3},
         flops=COST,
     )
 
@@ -776,6 +798,16 @@
     )
 
     other = shifted(forces, "probe", 1)
+    whole = jax.ShapeDtypeStruct(adjoint_now.shape, f32)
+    adjoint_out, forward_out = call(
+        store_kernel,
+        "store",
+        in_vmem(adjoint_out, forward_out),
+        (whole, whole),
+        [pltpu.SemaphoreType.DMA((2 * probes,))],
+        flops=COST,
+        out_spec=hbm,
+    )
     plain = jax.ShapeDtypeStruct((rows, cols), f32)
     right_force, down_force, site_force = call(
         sum_kernel, "force_sums", in_vmem(forces, other), (plain, plain, plain)

time: 19.9 us -> 19.5 us (0.980)
  local copies, waits for them, and re-layouts: 1.59 us -> 0 us
  waiting for transfers between devices: 1.22 us -> 2.22 us
    unnamed x2 -> x0, local copies, waits for them, and re-layouts: 1.59 us -> none
    ppermute x2, waiting for transfers between devices: 0.26 us -> 1.07 us  [pair_swap(): return lax.ppermute(x, axis, pairs)]
    pallas_call x6 -> x7, Pallas kernels: 9.03 us -> 9.16 us  [call(): pl.pallas_call(kernel, out_shape=outs, in_specs=[in_spec] * len(inputs),...]
  transfers between devices with their start and end apart: 4 -> 4, of which waited for: 3 -> 3; matrix products, arithmetic and copies ran while one was open for 8% -> 0% of each run, Pallas kernels for 26% -> 29%
where the time goes in v4:
time: 19.5 us; the launch traced here: 19.3 us
  Pallas kernels  9.16 us (47%)
  starting transfers between devices  7.27 us (37%)
  waiting for transfers between devices  2.22 us (11%)
  between operations  0.68 us (3%)
    pallas_call x7, Pallas kernels, call(): pl.pallas_call(kernel, out_shape=outs, in_specs=[in_spec] * len(inputs),...  9.16 us
    ppermute x2, starting transfers between devices, pair_swap(): return lax.ppermute(x, axis, pairs)  4.2 us
    ppermute x2, starting transfers between devices, shifted(): return lax.ppermute(x, axis, [(i, (i + by) % size) for i in range(size)])  3.07 us
    ppermute x2, waiting for transfers between devices, shifted(): return lax.ppermute(x, axis, [(i, (i + by) % size) for i in range(size)])  1.15 us
    ppermute x2, waiting for transfers between devices, pair_swap(): return lax.ppermute(x, axis, pairs)  1.07 us
  transfers between devices with their start and end apart: 4, of which 3 were waited for; matrix products, arithmetic and copies ran while one was open for 0% of the time, Pallas kernels for 29%

profile of v4, /device:TPU:0, one launch (start us, length us, event | category | flops | bytes accessed | tf_op | source)
XLA Modules:
  0.0 19.3 jit_solution(15921004026878612443)
XLA Ops:
  0.6 2.2 %load.1 = (f32[8,4,80,128]{3,2,1,0:T(8,128)S(1)}, f32[4,64,512]{2,1,0:T(8,128)S(1)}, f32[4,64,512]{2,1,0:T(8,128)S(1)}, s32[4,64,512]{2,1,0:T(8,128)S(1)}, f32[6...) custom-call(f32[1,3]{1,0:T(1,128)} %bitcast.3, ...), custom_call_target="tpu_custom_call" | custom-call | tf_op jit(solution)/shard_map/load/pallas_call | solution.py:694
  2.8 3.0 %collective-permute-start = (f32[64,128]{1,0:T(8,128)S(1)}, f32[64,128]{1,0:T(8,128)S(1)}, u32[]{:S(2)}, u32[]{:S(2)}) collective-permute-start(f32[64,128]{1,0:T(8,128)S(1)} %get-tuple-element.47.own), channel_id=1, source_target_pairs={{0,2},{2,0},{1,3},{3,1},{4,6},{6,4},{5,7},{7,5},{8,10},{10,8},{9,1... | collective-permute-start | bytes 98312 | tf_op jit(solution)/shard_map/ppermute | solution.py:21
  5.8 1.4 %step_0.1 = (f32[2560,128]{1,0:T(8,128)S(1)}, f32[2560,128]{1,0:T(8,128)S(1)}, f32[2560,128]{1,0:T(8,128)S(1)}, f32[4,4,80,128]{3,2,1,0:T(8,128)S(1)}, f32[3,64,...) custom-call(f32[1,3]{1,0:T(1,128)S(1)} %get-tuple-element.38.weights, ...), custom_call_target="tpu_custom_call", output_to_operand_aliasing={{0}: (1, {})} | custom-call | flops 4000000 | bytes 4000000 | tf_op jit(solution)/shard_map/step_0/pallas_call | solution.py:694
  7.2 0.5 %collective-permute-done.left.right = f32[64,128]{1,0:T(8,128)S(1)} collective-permute-done((f32[64,128]{1,0:T(8,128)S(1)}, f32[64,128]{1,0:T(8,128)S(1)}, u32[]{:S(2)}, u32[]{:S(2)}) %collective-permute-start) | collective-permute-done | bytes 32800 | tf_op jit(solution)/shard_map/ppermute | solution.py:21
  7.7 0.2 %edge_rows.1 = (f32[32,512]{1,0:T(8,128)S(1)}, f32[32,512]{1,0:T(8,128)S(1)}) custom-call(f32[64,128]{1,0:T(8,128)S(1)} %get-tuple-element.47.own, f32[64,128]{1,0:T(8,128)S(1)} %collective-permute-done.left.right, f32[64,128]{1,0:T(8,128)S(1)} %collective-permute-done.left.right, f32[2,32,512]{2,1,0:T(8,128)S(1)} %get-tuple-element.48.messages), custom_call_target="tpu_custom_call" | custom-call | tf_op jit(solution)/shard_map/edge_rows/pallas_call | solution.py:694
  7.9 4.2 %collective-permute-start.1 = (f32[32,512]{1,0:T(8,128)S(1)}, f32[32,512]{1,0:T(8,128)S(1)}, u32[]{:S(2)}, u32[]{:S(2)}) collective-permute-start(f32[32,512]{1,0:T(8,128)S(1)} %get-tuple-element.59), channel_id=1, source_target_pairs={{4,8},{8,4},{12,0},{0,12},{5,9},{9,5},{13,1},{1,13},{6,10},{10,6},... | collective-permute-start | bytes 196616 | tf_op jit(solution)/shard_map/ppermute | solution.py:41
  12.1 0.0 collective-permute-start.2
  12.1 3.2 %inner_steps.1 = (f32[2560,128]{1,0:T(8,128)S(1)}, f32[2560,128]{1,0:T(8,128)S(1)}, f32[4,4,80,128]{3,2,1,0:T(8,128)S(1)}, f32[3,64,512]{2,1,0:T(8,128)S(1)}, f3...) custom-call(f32[1,3]{1,0:T(1,128)S(1)} %get-tuple-element.38.weights, ...), custom_call_target="tpu_custom_call", output_to_operand_aliasing={{0}: (7, {}), {1}: (8, {}), {2}: (9, {}), {3}: (10, {})} | custom-call | flops 4000000 | bytes 4000000 | tf_op jit(solution)/shard_map/inner_steps/pallas_call | solution.py:694
  15.3 0.0 collective-permute-done.1.received_odd
  15.3 1.1 %collective-permute-done.2.received_even = f32[32,512]{1,0:T(8,128)S(1)} collective-permute-done((f32[32,512]{1,0:T(8,128)S(1)}, f32[32,512]{1,0:T(8,128)S(1)}, u32[]{:S(2)}, u32[]{:S(2)}) %collective-permute-start.2) | collective-permute-done | bytes 65568 | tf_op jit(solution)/shard_map/ppermute | solution.py:41
  16.4 0.3 %outer_rows.1 = (f32[3,64,512]{2,1,0:T(8,128)S(1)}, f32[4,64,512]{2,1,0:T(8,128)S(1)}, f32[4,64,512]{2,1,0:T(8,128)S(1)}) custom-call(f32[2560,128]{1,0:T(8,128)S(1)} %get-tuple-element.46.x0, f32[2560,128]{1,0:T(8,128)S(1)} %get-tuple-element.54.x1, ...), custom_call_target="tpu_custom_call", output_to_operand_aliasing={{0}: (8, {}), {1}: (9, {}), {2}: (10, {})} | custom-call | flops 4000000 | bytes 4000000 | tf_op jit(solution)/shard_map/outer_rows/pallas_call | solution.py:694
  16.8 0.1 collective-permute-start.3
  16.8 1.0 %store.1 = (f32[4,64,512]{2,1,0:T(8,128)}, f32[4,64,512]{2,1,0:T(8,128)}) custom-call(f32[4,64,512]{2,1,0:T(8,128)S(1)} %get-tuple-element.67.adj, f32[4,64,512]{2,1,0:T(8,128)S(1)} %get-tuple-element.68.fwd), custom_call_target="tpu_custom_call" | custom-call | flops 4000000 | bytes 4000000 | tf_op jit(solution)/shard_map/store/pallas_call | solution.py:694
  17.9 0.7 %collective-permute-done.3.other = f32[3,64,512]{2,1,0:T(8,128)S(1)} collective-permute-done((f32[3,64,512]{2,1,0:T(8,128)S(1)}, f32[3,64,512]{2,1,0:T(8,128)S(1)}, u32[]{:S(2)}, u32[]{:S(2)}) %collective-permute-start.3) | collective-permute-done | bytes 393248 | tf_op jit(solution)/shard_map/ppermute | solution.py:21
  18.5 0.8 %force_sums.1 = (f32[64,512]{1,0:T(8,128)}, f32[64,512]{1,0:T(8,128)}, f32[64,512]{1,0:T(8,128)}) custom-call(f32[3,64,512]{2,1,0:T(8,128)S(1)} %get-tuple-element.63.mine, f32[3,64,512]{2,1,0:T(8,128)S(1)} %collective-permute-done.3.other), custom_call_target="tpu_custom_call" | custom-call | tf_op jit(solution)/shard_map/force_sums/pallas_call | solution.py:694
Async XLA Ops:
  2.8 4.9 %collective-permute-start = (f32[64,128]{1,0:T(8,128)S(1)}, f32[64,128]{1,0:T(8,128)S(1)}, u32[]{:S(2)}, u32[]{:S(2)}) collective-permute-start(f32[64,128]{1,0:T(8,128)S(1)} %get-tuple-element.47.own), channel_id=1, source_target_pairs={{0,2},{2,0},{1,3},{3,1},{4,6},{6,4},{5,7},{7,5},{8,10},{10,8},{9,1... | collective-permute-start | bytes 98312 | tf_op jit(solution)/shard_map/ppermute | solution.py:21
  7.9 7.4 %collective-permute-start.1 = (f32[32,512]{1,0:T(8,128)S(1)}, f32[32,512]{1,0:T(8,128)S(1)}, u32[]{:S(2)}, u32[]{:S(2)}) collective-permute-start(f32[32,512]{1,0:T(8,128)S(1)} %get-tuple-element.59), channel_id=1, source_target_pairs={{4,8},{8,4},{12,0},{0,12},{5,9},{9,5},{13,1},{1,13},{6,10},{10,6},... | collective-permute-start | bytes 196616 | tf_op jit(solution)/shard_map/ppermute | solution.py:41
  12.1 4.3 %collective-permute-start.2 = (f32[32,512]{1,0:T(8,128)S(1)}, f32[32,512]{1,0:T(8,128)S(1)}, u32[]{:S(2)}, u32[]{:S(2)}) collective-permute-start(f32[32,512]{1,0:T(8,128)S(1)} %get-tuple-element.49.sent), channel_id=1, source_target_pairs={{0,4},{4,0},{8,12},{12,8},{1,5},{5,1},{9,13},{13,9},{2,6},{6,2},{1... | collective-permute-start | bytes 196616 | tf_op jit(solution)/shard_map/ppermute | solution.py:41
  16.8 1.8 %collective-permute-start.3 = (f32[3,64,512]{2,1,0:T(8,128)S(1)}, f32[3,64,512]{2,1,0:T(8,128)S(1)}, u32[]{:S(2)}, u32[]{:S(2)}) collective-permute-start(f32[3,64,512]{2,1,0:T(8,128)S(1)} %get-tuple-element.63.mine), channel_id=1, source_target_pairs={{0,1},{1,0},{2,3},{3,2},{4,5},{5,4},{6,7},{7,6},{8,9},{9,8},{10,11... | collective-permute-start | bytes 1179656 | tf_op jit(solution)/shard_map/ppermute | solution.py:21

commit v5 on v4

--- a/solution.py
+++ b/solution.py
@@ -31,14 +31,6 @@
 
 def turned(x, by):
     return pltpu.roll(x, by % x.shape[1], 1)
-
-
-def pair_swap(x, axis, odd):
-    size = lax.axis_size(axis)
-    pairs = []
-    for i in range(odd, size, 2):
-        pairs += [(i, (i + 1) % size), ((i + 1) % size, i)]
-    return lax.ppermute(x, axis, pairs)
 
 
 def pack(shape, now, following, signs, lattice, weight):
@@ -395,15 +387,16 @@
     )
 
 
-def send_kernel(own, left, right, messages, to_odd, to_even, message):
-    rows, cols = own.shape[0], to_odd.shape[1]
-    groups = (to_odd.shape[0] - TILE) // 3
+def send_kernel(own, left, right, messages, to_above, to_below):
+    rows, cols = own.shape[0], to_above.shape[1]
+    groups = (to_above.shape[0] - TILE) // 3
     span = WIDE * groups
     misc = 3 * groups
     lane = lane_of((groups, LANES))
     left_part = lane_of((TILE, LANES)) < span
-    message[...] = messages[...]
     for side, (edge, second) in enumerate(((0, 1), (TILE - 1, TILE - 2))):
+        message = (to_above, to_below)[side]
+        message[...] = messages[side]
         part = pl.ds(side * (rows - TILE), TILE)
         field, base, (s_on, s_right, s_down) = strips(own[part, :], left[part, :], right[part, :], span)
         before = turned(s_right, 1)
@@ -418,9 +411,9 @@
                 (0, column_of(row, groups, STEPS - 1), 0),
                 (cols - LANES, column_of(row, groups, span + STEPS), LANES - 1),
             ):
-                where = (side, pl.ds(at, groups), pl.ds(start, LANES))
+                where = (pl.ds(at, groups), pl.ds(start, LANES))
                 message[where] = message[where] + jnp.where(lane == spot, value, 0.0)
-        message[side, misc + 3 : misc + 4, 0 : 4 * LANES] = jnp.concatenate(
+        message[misc + 3 : misc + 4, 0 : 4 * LANES] = jnp.concatenate(
             [
                 field[edge : edge + 1, :],
                 level[edge : edge + 1, :] + s_down[bond : bond + 1, :] * field[second : second + 1, :],
@@ -429,9 +422,6 @@
             ],
             axis=1,
         )
-    odd = lax.rem(lax.axis_index("strip"), 2) == 1
-    to_odd[...] = jnp.where(odd, message[1], message[0])
-    to_even[...] = jnp.where(odd, message[0], message[1])
 
 
 def strip_rows(block, strip, strip_base, strip_hops, step, row, count):
@@ -526,28 +516,20 @@
             )
 
 
-def sorted_messages(received_odd, received_even, message):
-    odd = lax.rem(lax.axis_index("strip"), 2) == 1
-    message[0] = jnp.where(odd, received_even[...], received_odd[...])
-    message[1] = jnp.where(odd, received_odd[...], received_even[...])
-    return message.at[0], message.at[1]
-
-
 def other_field(x):
     return pltpu.roll(x, x.shape[0] // 2, 0)
 
 
 def outer_kernel(
-    x0, x1, x2, hops, strip, strip_hops, received_odd, received_even, forces_in, adj_in, fwd_in, *refs
+    x0, x1, x2, hops, strip, strip_hops, above, below, forces_in, adj_in, fwd_in, *refs
 ):
     del forces_in, adj_in, fwd_in
-    forces, adj_out, fwd_out, message = refs
+    forces, adj_out, fwd_out = refs
     probes, rows, cols = adj_out.shape
     block = Block(probes, rows, cols)
     groups, span = block.groups, block.span
     misc = 3 * groups
     lane = lane_of((groups, cols))
-    messages = sorted_messages(received_odd, received_even, message)
 
     def s_line(ref, at, row):
         return ref[at, TILE + row : TILE + row + 1, :]
@@ -557,7 +539,7 @@
         before = jnp.where(lane == 0, first, turned(x, 1))
         return before, jnp.where(lane == cols - 1, last, turned(x, -1))
 
-    for side, source in enumerate(messages):
+    for side, source in enumerate((above, below)):
         edge, second, third = (0, 1, 2) if side == 0 else (rows - 1, rows - 2, rows - 3)
         bond, next_bond = (edge, second) if side == 0 else (second, third)
         corner = source[misc + 3 : misc + 4, 0 : 4 * LANES]
@@ -759,13 +741,13 @@
 
     x0, x1, x2, hops, forces = in_vmem(x0, x1, x2, hops, forces)
     messages, left, right = in_vmem(messages, left, right)
-    to_odd, to_even = call(
-        send_kernel, "edge_rows", (packed, left, right, messages), (message, message), [both_messages]
-    )
-    received_odd = pair_swap(to_odd, "strip", 1)
-    received_even = pair_swap(to_even, "strip", 0)
-
-    (sent,) = in_vmem(to_even)
+    to_above, to_below = call(
+        send_kernel, "edge_rows", (packed, left, right, messages), (message, message)
+    )
+    above = shifted(to_below, "strip", 1)
+    below = shifted(to_above, "strip", -1)
+
+    (sent,) = in_vmem(to_above)
     x1, x2, hops, forces, adj_out, fwd_out, strip, strip_base, strip_hops = call(
         inner_kernel,
         "inner_steps",
@@ -786,13 +768,12 @@
     )
 
     kept = in_vmem(forces, adj_out, fwd_out)
-    read = (x0,) + in_vmem(x1, x2, hops, strip, strip_hops, received_odd, received_even)
+    read = (x0,) + in_vmem(x1, x2, hops, strip, strip_hops, above, below)
     forces, adjoint_out, forward_out = call(
         outer_kernel,
         "outer_rows",
         read + kept,
         tuple(like(v) for v in kept),
-        [both_messages],
         aliases={len(read) + i: i for i in range(len(kept))},
         flops=COST,
     )

time: 19.5 us -> 18.5 us (0.949)
  waiting for transfers between devices: 2.22 us -> 1.16 us
    ppermute x2 -> x4, starting transfers between devices: 3.07 us -> 7.32 us  [shifted(): return lax.ppermute(x, axis, [(i, (i + by) % size) for i in range(size)])]
    ppermute x2 -> x0, starting transfers between devices: 4.2 us -> none  [pair_swap(): return lax.ppermute(x, axis, pairs)]
    ppermute x2 -> x0, waiting for transfers between devices: 1.07 us -> none  [pair_swap(): return lax.ppermute(x, axis, pairs)]
    ppermute x2 -> x4, waiting for transfers between devices: 1.15 us -> 1.16 us  [shifted(): return lax.ppermute(x, axis, [(i, (i + by) % size) for i in range(size)])]
  transfers between devices with their start and end apart: 4 -> 4, of which waited for: 3 -> 2; matrix products, arithmetic and copies ran while one was open for 0% -> 0% of each run, Pallas kernels for 29% -> 31%
where the time goes in v5:
time: 18.5 us; the launch traced here: 18.3 us
  Pallas kernels  9.14 us (49%)
  starting transfers between devices  7.32 us (40%)
  waiting for transfers between devices  1.16 us (6%)
  between operations  0.68 us (4%)
    pallas_call x7, Pallas kernels, call(): pl.pallas_call(kernel, out_shape=outs, in_specs=[in_spec] * len(inputs),...  9.14 us
    ppermute x4, starting transfers between devices, shifted(): return lax.ppermute(x, axis, [(i, (i + by) % size) for i in range(size)])  7.32 us
    ppermute x4, waiting for transfers between devices, shifted(): return lax.ppermute(x, axis, [(i, (i + by) % size) for i in range(size)])  1.16 us
  transfers between devices with their start and end apart: 4, of which 2 were waited for; matrix products, arithmetic and copies ran while one was open for 0% of the time, Pallas kernels for 31%

profile of v5, /device:TPU:0, one launch (start us, length us, event | category | flops | bytes accessed | tf_op | source)
XLA Modules:
  0.0 18.3 jit_solution(14499538453881643133)
XLA Ops:
  0.6 2.2 %load.1 = (f32[8,4,80,128]{3,2,1,0:T(8,128)S(1)}, f32[4,64,512]{2,1,0:T(8,128)S(1)}, f32[4,64,512]{2,1,0:T(8,128)S(1)}, s32[4,64,512]{2,1,0:T(8,128)S(1)}, f32[6...) custom-call(f32[1,3]{1,0:T(1,128)} %bitcast.3, ...), custom_call_target="tpu_custom_call" | custom-call | tf_op jit(solution)/shard_map/load/pallas_call | solution.py:676
  2.8 3.0 %collective-permute-start = (f32[64,128]{1,0:T(8,128)S(1)}, f32[64,128]{1,0:T(8,128)S(1)}, u32[]{:S(2)}, u32[]{:S(2)}) collective-permute-start(f32[64,128]{1,0:T(8,128)S(1)} %get-tuple-element.47.own), channel_id=1, source_target_pairs={{0,2},{2,0},{1,3},{3,1},{4,6},{6,4},{5,7},{7,5},{8,10},{10,8},{9,1... | collective-permute-start | bytes 98312 | tf_op jit(solution)/shard_map/ppermute | solution.py:21
  5.8 1.4 %step_0.1 = (f32[2560,128]{1,0:T(8,128)S(1)}, f32[2560,128]{1,0:T(8,128)S(1)}, f32[2560,128]{1,0:T(8,128)S(1)}, f32[4,4,80,128]{3,2,1,0:T(8,128)S(1)}, f32[3,64,...) custom-call(f32[1,3]{1,0:T(1,128)S(1)} %get-tuple-element.38.weights, ...), custom_call_target="tpu_custom_call", output_to_operand_aliasing={{0}: (1, {})} | custom-call | flops 4000000 | bytes 4000000 | tf_op jit(solution)/shard_map/step_0/pallas_call | solution.py:676
  7.2 0.5 %collective-permute-done.left.right = f32[64,128]{1,0:T(8,128)S(1)} collective-permute-done((f32[64,128]{1,0:T(8,128)S(1)}, f32[64,128]{1,0:T(8,128)S(1)}, u32[]{:S(2)}, u32[]{:S(2)}) %collective-permute-start) | collective-permute-done | bytes 32800 | tf_op jit(solution)/shard_map/ppermute | solution.py:21
  7.7 0.2 %edge_rows.1 = (f32[32,512]{1,0:T(8,128)S(1)}, f32[32,512]{1,0:T(8,128)S(1)}) custom-call(f32[64,128]{1,0:T(8,128)S(1)} %get-tuple-element.47.own, f32[64,128]{1,0:T(8,128)S(1)} %collective-permute-done.left.right, f32[64,128]{1,0:T(8,128)S(1)} %collective-permute-done.left.right, f32[2,32,512]{2,1,0:T(8,128)S(1)} %get-tuple-element.48.messages), custom_call_target="tpu_custom_call" | custom-call | tf_op jit(solution)/shard_map/edge_rows/pallas_call | solution.py:676
  7.9 2.2 %collective-permute-start.1 = (f32[32,512]{1,0:T(8,128)S(1)}, f32[32,512]{1,0:T(8,128)S(1)}, u32[]{:S(2)}, u32[]{:S(2)}) collective-permute-start(f32[32,512]{1,0:T(8,128)S(1)} %get-tuple-element.59), channel_id=1, source_target_pairs={{0,4},{4,8},{8,12},{12,0},{1,5},{5,9},{9,13},{13,1},{2,6},{6,10},{... | collective-permute-start | bytes 196616 | tf_op jit(solution)/shard_map/ppermute | solution.py:21
  10.1 2.1 %collective-permute-start.2 = (f32[32,512]{1,0:T(8,128)S(1)}, f32[32,512]{1,0:T(8,128)S(1)}, u32[]{:S(2)}, u32[]{:S(2)}) collective-permute-start(f32[32,512]{1,0:T(8,128)S(1)} %get-tuple-element.49.sent), channel_id=1, source_target_pairs={{0,12},{4,0},{8,4},{12,8},{1,13},{5,1},{9,5},{13,9},{2,14},{6,2},{... | collective-permute-start | bytes 196616 | tf_op jit(solution)/shard_map/ppermute | solution.py:21
  12.2 3.2 %inner_steps.1 = (f32[2560,128]{1,0:T(8,128)S(1)}, f32[2560,128]{1,0:T(8,128)S(1)}, f32[4,4,80,128]{3,2,1,0:T(8,128)S(1)}, f32[3,64,512]{2,1,0:T(8,128)S(1)}, f3...) custom-call(f32[1,3]{1,0:T(1,128)S(1)} %get-tuple-element.38.weights, ...), custom_call_target="tpu_custom_call", output_to_operand_aliasing={{0}: (7, {}), {1}: (8, {}), {2}: (9, {}), {3}: (10, {})} | custom-call | flops 4000000 | bytes 4000000 | tf_op jit(solution)/shard_map/inner_steps/pallas_call | solution.py:676
  15.4 0.0 collective-permute-done.1.above
  15.4 0.0 collective-permute-done.2.below
  15.4 0.3 %outer_rows.1 = (f32[3,64,512]{2,1,0:T(8,128)S(1)}, f32[4,64,512]{2,1,0:T(8,128)S(1)}, f32[4,64,512]{2,1,0:T(8,128)S(1)}) custom-call(f32[2560,128]{1,0:T(8,128)S(1)} %get-tuple-element.46.x0, f32[2560,128]{1,0:T(8,128)S(1)} %get-tuple-element.54.x1, ...), custom_call_target="tpu_custom_call", output_to_operand_aliasing={{0}: (8, {}), {1}: (9, {}), {2}: (10, {})} | custom-call | flops 4000000 | bytes 4000000 | tf_op jit(solution)/shard_map/outer_rows/pallas_call | solution.py:676
  15.7 0.1 collective-permute-start.3
  15.8 1.0 %store.1 = (f32[4,64,512]{2,1,0:T(8,128)}, f32[4,64,512]{2,1,0:T(8,128)}) custom-call(f32[4,64,512]{2,1,0:T(8,128)S(1)} %get-tuple-element.67.adj, f32[4,64,512]{2,1,0:T(8,128)S(1)} %get-tuple-element.68.fwd), custom_call_target="tpu_custom_call" | custom-call | flops 4000000 | bytes 4000000 | tf_op jit(solution)/shard_map/store/pallas_call | solution.py:676
  16.8 0.7 %collective-permute-done.3.other = f32[3,64,512]{2,1,0:T(8,128)S(1)} collective-permute-done((f32[3,64,512]{2,1,0:T(8,128)S(1)}, f32[3,64,512]{2,1,0:T(8,128)S(1)}, u32[]{:S(2)}, u32[]{:S(2)}) %collective-permute-start.3) | collective-permute-done | bytes 393248 | tf_op jit(solution)/shard_map/ppermute | solution.py:21
  17.5 0.8 %force_sums.1 = (f32[64,512]{1,0:T(8,128)}, f32[64,512]{1,0:T(8,128)}, f32[64,512]{1,0:T(8,128)}) custom-call(f32[3,64,512]{2,1,0:T(8,128)S(1)} %get-tuple-element.63.mine, f32[3,64,512]{2,1,0:T(8,128)S(1)} %collective-permute-done.3.other), custom_call_target="tpu_custom_call" | custom-call | tf_op jit(solution)/shard_map/force_sums/pallas_call | solution.py:676
Async XLA Ops:
  2.8 4.9 %collective-permute-start = (f32[64,128]{1,0:T(8,128)S(1)}, f32[64,128]{1,0:T(8,128)S(1)}, u32[]{:S(2)}, u32[]{:S(2)}) collective-permute-start(f32[64,128]{1,0:T(8,128)S(1)} %get-tuple-element.47.own), channel_id=1, source_target_pairs={{0,2},{2,0},{1,3},{3,1},{4,6},{6,4},{5,7},{7,5},{8,10},{10,8},{9,1... | collective-permute-start | bytes 98312 | tf_op jit(solution)/shard_map/ppermute | solution.py:21
  7.9 7.4 %collective-permute-start.1 = (f32[32,512]{1,0:T(8,128)S(1)}, f32[32,512]{1,0:T(8,128)S(1)}, u32[]{:S(2)}, u32[]{:S(2)}) collective-permute-start(f32[32,512]{1,0:T(8,128)S(1)} %get-tuple-element.59), channel_id=1, source_target_pairs={{0,4},{4,8},{8,12},{12,0},{1,5},{5,9},{9,13},{13,1},{2,6},{6,10},{... | collective-permute-start | bytes 196616 | tf_op jit(solution)/shard_map/ppermute | solution.py:21
  10.1 5.3 %collective-permute-start.2 = (f32[32,512]{1,0:T(8,128)S(1)}, f32[32,512]{1,0:T(8,128)S(1)}, u32[]{:S(2)}, u32[]{:S(2)}) collective-permute-start(f32[32,512]{1,0:T(8,128)S(1)} %get-tuple-element.49.sent), channel_id=1, source_target_pairs={{0,12},{4,0},{8,4},{12,8},{1,13},{5,1},{9,5},{13,9},{2,14},{6,2},{... | collective-permute-start | bytes 196616 | tf_op jit(solution)/shard_map/ppermute | solution.py:21
  15.7 1.8 %collective-permute-start.3 = (f32[3,64,512]{2,1,0:T(8,128)S(1)}, f32[3,64,512]{2,1,0:T(8,128)S(1)}, u32[]{:S(2)}, u32[]{:S(2)}) collective-permute-start(f32[3,64,512]{2,1,0:T(8,128)S(1)} %get-tuple-element.63.mine), channel_id=1, source_target_pairs={{0,1},{1,0},{2,3},{3,2},{4,5},{5,4},{6,7},{7,6},{8,9},{9,8},{10,11... | collective-permute-start | bytes 1179656 | tf_op jit(solution)/shard_map/ppermute | solution.py:21

commit v6 on v5

--- a/solution.py
+++ b/solution.py
@@ -173,7 +173,8 @@
 
 def strips(own, left, right, span):
     lane = lane_of(own.shape)
-    inner = lax.rem(lane, WIDE) < STEPS
+    within = lane - WIDE * ((lane * (256 // WIDE + 1)) >> 8)
+    inner = within < STEPS
     low = jnp.where(inner, left, own)
     high = jnp.where(inner, own, right)
     below = lane < span
@@ -181,7 +182,7 @@
     base = jnp.where(below, turned(low, -span), high)
     coefficients = []
     for at in range(3):
-        source = 2 * span + WIDE * at + lax.rem(lane, WIDE)
+        source = 2 * span + WIDE * at + within
         coefficients.append(jnp.where(below, lanes_from(low, source), lanes_from(high, source)) * SCALE)
     return field, base, coefficients
 
@@ -235,10 +236,11 @@
 
 
 def beside(block, strip_tile):
-    lane = lane_of(strip_tile.shape)
-    picked = (lax.rem(lane, WIDE) == STEPS - 1) & (lane < block.span)
-    both = jnp.where(picked, strip_tile, turned(strip_tile, -(block.span + 2)))
-    return [turned(both, -(WIDE * g + STEPS - 1)) for g in range(block.groups)]
+    first = lane_of(strip_tile.shape) < LANES // 2
+    left, right = STEPS - 1, block.span + STEPS
+    return [
+        lanes_from(strip_tile, jnp.where(first, WIDE * g + left, WIDE * g + right)) for g in range(block.groups)
+    ]
 
 
 def tile_step(block, row, now, hops, sides, previous, sign, store, add, columns=None):

time: 18.5 us -> 18.1 us (0.978)
  Pallas kernels: 9.14 us -> 8.07 us
  waiting for transfers between devices: 1.16 us -> 1.89 us
    pallas_call x7, Pallas kernels: 9.14 us -> 8.07 us  [call(): pl.pallas_call(kernel, out_shape=outs, in_specs=[in_spec] * len(inputs),...]
    ppermute x4, waiting for transfers between devices: 1.16 us -> 1.89 us  [shifted(): return lax.ppermute(x, axis, [(i, (i + by) % size) for i in range(size)])]
  transfers between devices with their start and end apart: 4 -> 4, of which waited for: 2 -> 4; matrix products, arithmetic and copies ran while one was open for 0% -> 0% of each run, Pallas kernels for 31% -> 25%
where the time goes in v6:
time: 18.1 us; the launch traced here: 18 us
  Pallas kernels  8.07 us (45%)
  starting transfers between devices  7.32 us (40%)
  waiting for transfers between devices  1.89 us (10%)
  between operations  0.68 us (4%)
    pallas_call x7, Pallas kernels, call(): pl.pallas_call(kernel, out_shape=outs, in_specs=[in_spec] * len(inputs),...  8.07 us
    ppermute x4, starting transfers between devices, shifted(): return lax.ppermute(x, axis, [(i, (i + by) % size) for i in range(size)])  7.32 us
    ppermute x4, waiting for transfers between devices, shifted(): return lax.ppermute(x, axis, [(i, (i + by) % size) for i in range(size)])  1.89 us
  transfers between devices with their start and end apart: 4, of which 4 were waited for; matrix products, arithmetic and copies ran while one was open for 0% of the time, Pallas kernels for 25%

profile of v6, /device:TPU:0, one launch (start us, length us, event | category | flops | bytes accessed | tf_op | source)
XLA Modules:
  0.0 18.0 jit_solution(3993506724510671161)
XLA Ops:
  0.6 2.2 %load.1 = (f32[8,4,80,128]{3,2,1,0:T(8,128)S(1)}, f32[4,64,512]{2,1,0:T(8,128)S(1)}, f32[4,64,512]{2,1,0:T(8,128)S(1)}, s32[4,64,512]{2,1,0:T(8,128)S(1)}, f32[6...) custom-call(f32[1,3]{1,0:T(1,128)} %bitcast.3, ...), custom_call_target="tpu_custom_call" | custom-call | tf_op jit(solution)/shard_map/load/pallas_call | solution.py:678
  2.8 3.0 %collective-permute-start = (f32[64,128]{1,0:T(8,128)S(1)}, f32[64,128]{1,0:T(8,128)S(1)}, u32[]{:S(2)}, u32[]{:S(2)}) collective-permute-start(f32[64,128]{1,0:T(8,128)S(1)} %get-tuple-element.47.own), channel_id=1, source_target_pairs={{0,2},{2,0},{1,3},{3,1},{4,6},{6,4},{5,7},{7,5},{8,10},{10,8},{9,1... | collective-permute-start | bytes 98312 | tf_op jit(solution)/shard_map/ppermute | solution.py:21
  5.8 1.4 %step_0.1 = (f32[2560,128]{1,0:T(8,128)S(1)}, f32[2560,128]{1,0:T(8,128)S(1)}, f32[2560,128]{1,0:T(8,128)S(1)}, f32[4,4,80,128]{3,2,1,0:T(8,128)S(1)}, f32[3,64,...) custom-call(f32[1,3]{1,0:T(1,128)S(1)} %get-tuple-element.38.weights, ...), custom_call_target="tpu_custom_call", output_to_operand_aliasing={{0}: (1, {})} | custom-call | flops 4000000 | bytes 4000000 | tf_op jit(solution)/shard_map/step_0/pallas_call | solution.py:678
  7.2 0.5 %collective-permute-done.left.right = f32[64,128]{1,0:T(8,128)S(1)} collective-permute-done((f32[64,128]{1,0:T(8,128)S(1)}, f32[64,128]{1,0:T(8,128)S(1)}, u32[]{:S(2)}, u32[]{:S(2)}) %collective-permute-start) | collective-permute-done | bytes 32800 | tf_op jit(solution)/shard_map/ppermute | solution.py:21
  7.7 0.2 %edge_rows.1 = (f32[32,512]{1,0:T(8,128)S(1)}, f32[32,512]{1,0:T(8,128)S(1)}) custom-call(f32[64,128]{1,0:T(8,128)S(1)} %get-tuple-element.47.own, f32[64,128]{1,0:T(8,128)S(1)} %collective-permute-done.left.right, f32[64,128]{1,0:T(8,128)S(1)} %collective-permute-done.left.right, f32[2,32,512]{2,1,0:T(8,128)S(1)} %get-tuple-element.48.messages), custom_call_target="tpu_custom_call" | custom-call | tf_op jit(solution)/shard_map/edge_rows/pallas_call | solution.py:678
  7.9 2.2 %collective-permute-start.1 = (f32[32,512]{1,0:T(8,128)S(1)}, f32[32,512]{1,0:T(8,128)S(1)}, u32[]{:S(2)}, u32[]{:S(2)}) collective-permute-start(f32[32,512]{1,0:T(8,128)S(1)} %get-tuple-element.59), channel_id=1, source_target_pairs={{0,4},{4,8},{8,12},{12,0},{1,5},{5,9},{9,13},{13,1},{2,6},{6,10},{... | collective-permute-start | bytes 196616 | tf_op jit(solution)/shard_map/ppermute | solution.py:21
  10.1 2.1 %collective-permute-start.2 = (f32[32,512]{1,0:T(8,128)S(1)}, f32[32,512]{1,0:T(8,128)S(1)}, u32[]{:S(2)}, u32[]{:S(2)}) collective-permute-start(f32[32,512]{1,0:T(8,128)S(1)} %get-tuple-element.49.sent), channel_id=1, source_target_pairs={{0,12},{4,0},{8,4},{12,8},{1,13},{5,1},{9,5},{13,9},{2,14},{6,2},{... | collective-permute-start | bytes 196616 | tf_op jit(solution)/shard_map/ppermute | solution.py:21
  12.2 2.1 %inner_steps.1 = (f32[2560,128]{1,0:T(8,128)S(1)}, f32[2560,128]{1,0:T(8,128)S(1)}, f32[4,4,80,128]{3,2,1,0:T(8,128)S(1)}, f32[3,64,512]{2,1,0:T(8,128)S(1)}, f3...) custom-call(f32[1,3]{1,0:T(1,128)S(1)} %get-tuple-element.38.weights, ...), custom_call_target="tpu_custom_call", output_to_operand_aliasing={{0}: (7, {}), {1}: (8, {}), {2}: (9, {}), {3}: (10, {})} | custom-call | flops 4000000 | bytes 4000000 | tf_op jit(solution)/shard_map/inner_steps/pallas_call | solution.py:678
  14.3 0.3 %collective-permute-done.1.above = f32[32,512]{1,0:T(8,128)S(1)} collective-permute-done((f32[32,512]{1,0:T(8,128)S(1)}, f32[32,512]{1,0:T(8,128)S(1)}, u32[]{:S(2)}, u32[]{:S(2)}) %collective-permute-start.1) | collective-permute-done | bytes 65568 | tf_op jit(solution)/shard_map/ppermute | solution.py:21
  14.6 0.5 %collective-permute-done.2.below = f32[32,512]{1,0:T(8,128)S(1)} collective-permute-done((f32[32,512]{1,0:T(8,128)S(1)}, f32[32,512]{1,0:T(8,128)S(1)}, u32[]{:S(2)}, u32[]{:S(2)}) %collective-permute-start.2) | collective-permute-done | bytes 65568 | tf_op jit(solution)/shard_map/ppermute | solution.py:21
  15.1 0.3 %outer_rows.1 = (f32[3,64,512]{2,1,0:T(8,128)S(1)}, f32[4,64,512]{2,1,0:T(8,128)S(1)}, f32[4,64,512]{2,1,0:T(8,128)S(1)}) custom-call(f32[2560,128]{1,0:T(8,128)S(1)} %get-tuple-element.46.x0, f32[2560,128]{1,0:T(8,128)S(1)} %get-tuple-element.54.x1, ...), custom_call_target="tpu_custom_call", output_to_operand_aliasing={{0}: (8, {}), {1}: (9, {}), {2}: (10, {})} | custom-call | flops 4000000 | bytes 4000000 | tf_op jit(solution)/shard_map/outer_rows/pallas_call | solution.py:678
  15.4 0.1 collective-permute-start.3
  15.5 1.0 %store.1 = (f32[4,64,512]{2,1,0:T(8,128)}, f32[4,64,512]{2,1,0:T(8,128)}) custom-call(f32[4,64,512]{2,1,0:T(8,128)S(1)} %get-tuple-element.67.adj, f32[4,64,512]{2,1,0:T(8,128)S(1)} %get-tuple-element.68.fwd), custom_call_target="tpu_custom_call" | custom-call | flops 4000000 | bytes 4000000 | tf_op jit(solution)/shard_map/store/pallas_call | solution.py:678
  16.5 0.7 %collective-permute-done.3.other = f32[3,64,512]{2,1,0:T(8,128)S(1)} collective-permute-done((f32[3,64,512]{2,1,0:T(8,128)S(1)}, f32[3,64,512]{2,1,0:T(8,128)S(1)}, u32[]{:S(2)}, u32[]{:S(2)}) %collective-permute-start.3) | collective-permute-done | bytes 393248 | tf_op jit(solution)/shard_map/ppermute | solution.py:21
  17.2 0.8 %force_sums.1 = (f32[64,512]{1,0:T(8,128)}, f32[64,512]{1,0:T(8,128)}, f32[64,512]{1,0:T(8,128)}) custom-call(f32[3,64,512]{2,1,0:T(8,128)S(1)} %get-tuple-element.63.mine, f32[3,64,512]{2,1,0:T(8,128)S(1)} %collective-permute-done.3.other), custom_call_target="tpu_custom_call" | custom-call | tf_op jit(solution)/shard_map/force_sums/pallas_call | solution.py:678
Async XLA Ops:
  2.8 4.9 %collective-permute-start = (f32[64,128]{1,0:T(8,128)S(1)}, f32[64,128]{1,0:T(8,128)S(1)}, u32[]{:S(2)}, u32[]{:S(2)}) collective-permute-start(f32[64,128]{1,0:T(8,128)S(1)} %get-tuple-element.47.own), channel_id=1, source_target_pairs={{0,2},{2,0},{1,3},{3,1},{4,6},{6,4},{5,7},{7,5},{8,10},{10,8},{9,1... | collective-permute-start | bytes 98312 | tf_op jit(solution)/shard_map/ppermute | solution.py:21
  7.9 6.6 %collective-permute-start.1 = (f32[32,512]{1,0:T(8,128)S(1)}, f32[32,512]{1,0:T(8,128)S(1)}, u32[]{:S(2)}, u32[]{:S(2)}) collective-permute-start(f32[32,512]{1,0:T(8,128)S(1)} %get-tuple-element.59), channel_id=1, source_target_pairs={{0,4},{4,8},{8,12},{12,0},{1,5},{5,9},{9,13},{13,1},{2,6},{6,10},{... | collective-permute-start | bytes 196616 | tf_op jit(solution)/shard_map/ppermute | solution.py:21
  10.1 5.0 %collective-permute-start.2 = (f32[32,512]{1,0:T(8,128)S(1)}, f32[32,512]{1,0:T(8,128)S(1)}, u32[]{:S(2)}, u32[]{:S(2)}) collective-permute-start(f32[32,512]{1,0:T(8,128)S(1)} %get-tuple-element.49.sent), channel_id=1, source_target_pairs={{0,12},{4,0},{8,4},{12,8},{1,13},{5,1},{9,5},{13,9},{2,14},{6,2},{... | collective-permute-start | bytes 196616 | tf_op jit(solution)/shard_map/ppermute | solution.py:21
  15.4 1.8 %collective-permute-start.3 = (f32[3,64,512]{2,1,0:T(8,128)S(1)}, f32[3,64,512]{2,1,0:T(8,128)S(1)}, u32[]{:S(2)}, u32[]{:S(2)}) collective-permute-start(f32[3,64,512]{2,1,0:T(8,128)S(1)} %get-tuple-element.63.mine), channel_id=1, source_target_pairs={{0,1},{1,0},{2,3},{3,2},{4,5},{5,4},{6,7},{7,6},{8,9},{9,8},{10,11... | collective-permute-start | bytes 1179656 | tf_op jit(solution)/shard_map/ppermute | solution.py:21

commit v7 on v6

--- a/solution.py
+++ b/solution.py
@@ -33,8 +33,8 @@
     return pltpu.roll(x, by % x.shape[1], 1)
 
 
-def pack(shape, now, following, signs, lattice, weight):
-    groups = len(now)
+def pack(shape, probes, now, following, sign, lattice, weight):
+    groups = 2 * probes
     span = WIDE * groups
     lane = lane_of(shape)
 
@@ -47,17 +47,18 @@
         return jnp.where((lane >= start) & (lane < start + WIDE), turned(x, start + STEPS), packed)
 
     first, last = LANES - STEPS, STEPS - 1
+    for at in range(3):
+        packed = put(packed, joined(lattice(at)), 2 * span + WIDE * at)
     for g in range(groups):
-        if g < len(signs):
-            sign = joined(signs[g]).astype(jnp.float32)
-            base = weight * sign - joined(following[g])
-            base = jnp.where(lane == first, turned(sign, -2), jnp.where(lane == last, turned(sign, 2), base))
+        packed = put(packed, joined(now(g)), WIDE * g)
+    for g in reversed(range(groups)):
+        if g < probes:
+            own_sign = joined(sign(g)).astype(jnp.float32)
+            base = weight() * own_sign - joined(following(g))
+            base = jnp.where(lane == first, turned(own_sign, -2), jnp.where(lane == last, turned(own_sign, 2), base))
         else:
-            base = jnp.where((lane == first) | (lane == last), 0.0, -joined(following[g]))
-        packed = put(packed, joined(now[g]), WIDE * g)
+            base = jnp.where((lane == first) | (lane == last), 0.0, -joined(following(g)))
         packed = put(packed, base, span + WIDE * g)
-    for at, pair in enumerate(lattice):
-        packed = put(packed, joined(pair), 2 * span + WIDE * at)
     return packed
 
 
@@ -88,47 +89,64 @@
     done,
 ):
     probes, rows, cols = adj_in.shape
-    groups = 2 * probes
     tiles = cols // LANES
     inside = pl.ds(TILE, rows)
     copies = []
-
-    def copy(source, target):
+    started = {}
+
+    def copy(name, source, target):
         copies.append(pltpu.make_async_copy(source, target, done.at[len(copies)]))
         copies[-1].start()
-
-    def copy_tile(c):
-        for f, source in enumerate((adj_in, fwd_in)):
-            copy(source.at[:, :, lanes(c)], x0.at[pl.ds(f * probes, probes), c, inside, :])
-
-    def copy_lanes(start, count):
-        part = pl.ds(start, count)
-        for source, target in ((adj_next_in, adj_next), (fwd_next_in, fwd_next), (signs_in, signs)):
-            copy(source.at[:, :, part], target.at[:, :, part])
-
-    copy(weights_in, weights)
-    for c in (0, tiles - 1):
-        copy_tile(c)
-        copy_lanes(c * LANES, LANES)
-    copy(onsite_in, onsite)
-    copy(hop_right_in, hop_right)
-    copy(hop_down_in, hop_down)
-    needed = len(copies)
+        started.setdefault(name, []).append(copies[-1])
+
+    def here(name):
+        for each in started.pop(name, ()):
+            each.wait()
+
+    def copy_tile(name, f, c):
+        source = (adj_in, fwd_in)[f]
+        copy(name, source.at[:, :, lanes(c)], x0.at[pl.ds(f * probes, probes), c, inside, :])
+
+    rest = ((adj_next_in, adj_next), (fwd_next_in, fwd_next), (signs_in, signs))
+    copy("lattice", onsite_in, onsite)
+    copy("lattice", hop_right_in, hop_right)
+    copy("lattice", hop_down_in, hop_down)
+    copy("weights", weights_in, weights)
+    ends_at = (0, tiles - 1)
+    for f in range(2):
+        for c in ends_at:
+            copy_tile(("now", f), f, c)
+    for at in (1, 2, 0):
+        source, target = rest[at]
+        for c in ends_at:
+            copy(("rest", at), source.at[:, :, lanes(c)], target.at[:, :, lanes(c)])
     for c in range(1, tiles - 1):
-        copy_tile(c)
-    copy_lanes(LANES, cols - 2 * LANES)
-    for at in range(needed):
-        copies[at].wait()
-    packed[...] = pack(
-        packed.shape,
-        [(x0[g, 0, inside, :], x0[g, tiles - 1, inside, :]) for g in range(groups)],
-        [ends(ref, p) for ref in (adj_next, fwd_next) for p in range(probes)],
-        [ends(signs, p) for p in range(probes)],
-        [ends(ref) for ref in (onsite, hop_right, hop_down)],
-        weights[0:1, 0:1],
-    )
-    for at in range(needed, len(copies)):
-        copies[at].wait()
+        for f in range(2):
+            copy_tile("others", f, c)
+
+    def now(g):
+        here(("now", g // probes))
+        return x0[g, 0, inside, :], x0[g, tiles - 1, inside, :]
+
+    def following(g):
+        here(("rest", g // probes))
+        return ends(rest[g // probes][1], g % probes)
+
+    def sign(p):
+        here(("rest", 2))
+        return ends(signs, p)
+
+    def lattice(kind):
+        here("lattice")
+        return ends((onsite, hop_right, hop_down)[kind])
+
+    def weight():
+        here("weights")
+        return weights[0:1, 0:1]
+
+    packed[...] = pack(packed.shape, probes, now, following, sign, lattice, weight)
+    for name in list(started):
+        here(name)
 
 
 def edge_rows(block, weights, x0, adj_next, fwd_next, signs, lattice, lines, out):
@@ -323,14 +341,56 @@
 
 
 def first_kernel(
-    weights, x0, adj_next, fwd_next, signs, onsite, hop_right, hop_down, x0_out, x1, x2, hops, forces, messages
+    adj_next_in,
+    fwd_next_in,
+    signs_in,
+    weights,
+    x0_in,
+    adj_next_start,
+    fwd_next_start,
+    signs_start,
+    onsite,
+    hop_right,
+    hop_down,
+    x0,
+    adj_next,
+    fwd_next,
+    signs,
+    x1,
+    x2,
+    hops,
+    forces,
+    messages,
+    done,
 ):
+    del x0_in, adj_next_start, fwd_next_start, signs_start
     block = Block(*signs.shape)
     rows = block.rows
+    part = pl.ds(LANES, block.cols - 2 * LANES)
+    copies = []
+    for source, target in ((adj_next_in, adj_next), (fwd_next_in, fwd_next), (signs_in, signs)):
+        copies.append(
+            pltpu.make_async_copy(source.at[:, :, part], target.at[:, :, part], done.at[len(copies)])
+        )
+        copies[-1].start()
     nothing = jnp.zeros((block.groups, block.cols), jnp.float32)
     for row in (-1, rows):
-        for x in (x0_out, x1, x2):
+        for x in (x0, x1, x2):
             block.scattered(x, row, nothing)
+    wide_lane = lane_of((rows, LANES))
+    inside = pl.ds(TILE, rows)
+    hop_before = 0.0
+    for c in range(block.tiles):
+        hop = hop_right[:, lanes(c)] * SCALE
+        hop_turned = turned(hop, 1)
+        hops[0, c, inside, :] = onsite[:, lanes(c)] * SCALE
+        hops[1, c, inside, :] = hop
+        hops[2, c, inside, :] = jnp.where(wide_lane == 0, hop_before, hop_turned)
+        hops[3, c, inside, :] = hop_down[:, lanes(c)] * SCALE
+        hops[3, c, pl.ds(TILE - 1, 1), :] = jnp.zeros((1, LANES), jnp.float32)
+        hop_before = hop_turned
+    for each in copies:
+        each.wait()
     for side, lines in enumerate(((0, 1, 2), (rows - 1, rows - 2, rows - 3))):
         edge_rows(
             block,
@@ -343,23 +403,11 @@
             lines,
             messages.at[side],
         )
-    wide_lane = lane_of((rows, LANES))
-    inside = pl.ds(TILE, rows)
-    hop_before = 0.0
-    for c in range(block.tiles):
-        hop = hop_right[:, lanes(c)] * SCALE
-        hop_turned = turned(hop, 1)
-        hops[0, c, inside, :] = onsite[:, lanes(c)] * SCALE
-        hops[1, c, inside, :] = hop
-        hops[2, c, inside, :] = jnp.where(wide_lane == 0, hop_before, hop_turned)
-        hops[3, c, inside, :] = hop_down[:, lanes(c)] * SCALE
-        hops[3, c, pl.ds(TILE - 1, 1), :] = jnp.zeros((1, LANES), jnp.float32)
-        hop_before = hop_turned
     for row in range(0, rows, TILE):
         tile_step(
             block,
             row,
-            x0_out,
+            x0,
             hops,
             None,
             block_reader(adj_next, fwd_next, row),
@@ -367,20 +415,6 @@
             field_storer(block, x1, row),
             force_adder(forces, row, True),
         )
-    for row in range(0, rows, TILE):
-        tile_step(
-            block,
-            row,
-            x1,
-            hops,
-            None,
-            field_reader(block, x0_out, row),
-            sign_reader(signs, weights, 1, row),
-            field_storer(block, x2, row),
-            force_adder(forces, row, False),
-            range(1, block.tiles - 1),
-        )
-
 
 def at_ends(block, row):
     return (
@@ -514,7 +548,6 @@
                 sign_reader(signs, weights, step, row),
                 field_storer(block, x2, row) if step == 1 else block_storer(adj_out, fwd_out, row),
                 force_adder(forces, row, False),
-                sorted({0, last}) if step == 1 else None,
             )
 
 
@@ -678,7 +711,7 @@
         return pl.pallas_call(
             kernel,
             out_shape=outs,
-            in_specs=[in_spec] * len(inputs),
+            in_specs=in_spec if isinstance(in_spec, list) else [in_spec] * len(inputs),
             out_specs=(out_spec,) * len(outs),
             scratch_shapes=list(scratch),
             input_output_aliases=aliases or {},
@@ -718,7 +751,7 @@
             pltpu.VMEM((1, STEPS), f32),
             strip_tile,
         ),
-        [pltpu.SemaphoreType.DMA((13 + 2 * tiles,))],
+        [pltpu.SemaphoreType.DMA((10 + 2 * tiles,))],
         in_spec=hbm,
     )
     x0 = x0.reshape(block.field_shape)
@@ -732,14 +765,19 @@
     field = pltpu.VMEM(block.field_shape, f32)
     hops_shape = pltpu.VMEM((4, tiles, tall, LANES), f32)
     forces_shape = pltpu.VMEM((3, rows, cols), f32)
-    x0, x1, x2, hops, forces, messages = call(
+    inputs = sources[3:6] + (weights, x0, adj_next, fwd_next, sign, on, hr, hd)
+    next_shape = like(adjoint_next)
+    x0, adj_next, fwd_next, sign, x1, x2, hops, forces, messages = call(
         first_kernel,
         "step_0",
-        (weights, x0, adj_next, fwd_next, sign, on, hr, hd),
-        (field, field, field, hops_shape, forces_shape, both_messages),
-        aliases={1: 0},
+        inputs,
+        (field, next_shape, next_shape, like(sign, jnp.int32), field, field, hops_shape, forces_shape, both_messages),
+        [pltpu.SemaphoreType.DMA((3,))],
+        aliases={4 + i: i for i in range(4)},
         flops=COST,
-    )
+        in_spec=[hbm] * 3 + [vmem] * 8,
+    )
+    (sign,) = in_vmem(sign)
 
     x0, x1, x2, hops, forces = in_vmem(x0, x1, x2, hops, forces)
     messages, left, right = in_vmem(messages, left, right)

time: 18.1 us -> 18 us (level)
  Pallas kernels: 8.07 us -> 9.09 us
  waiting for transfers between devices: 1.89 us -> 0.88 us
    pallas_call x7, Pallas kernels: 8.07 us -> 9.09 us  [call(): pl.pallas_call(kernel, out_shape=outs, in_specs=in_spec if isinstance(in_...]
    ppermute x4, waiting for transfers between devices: 1.89 us -> 0.88 us  [shifted(): return lax.ppermute(x, axis, [(i, (i + by) % size) for i in range(size)])]
  transfers between devices with their start and end apart: 4 -> 4, of which waited for: 4 -> 2; matrix products, arithmetic and copies ran while one was open for 0% -> 0% of each run, Pallas kernels for 25% -> 32%
where the time goes in v7:
time: 18 us; the launch traced here: 17.8 us
  Pallas kernels  9.09 us (50%)
  starting transfers between devices  7.18 us (40%)
  waiting for transfers between devices  0.88 us (5%)
  between operations  0.69 us (4%)
    pallas_call x7, Pallas kernels, call(): pl.pallas_call(kernel, out_shape=outs, in_specs=in_spec if isinstance(in_...  9.09 us
    ppermute x4, starting transfers between devices, shifted(): return lax.ppermute(x, axis, [(i, (i + by) % size) for i in range(size)])  7.18 us
    ppermute x4, waiting for transfers between devices, shifted(): return lax.ppermute(x, axis, [(i, (i + by) % size) for i in range(size)])  0.88 us
  transfers between devices with their start and end apart: 4, of which 2 were waited for; matrix products, arithmetic and copies ran while one was open for 0% of the time, Pallas kernels for 32%

profile of v7, /device:TPU:0, one launch (start us, length us, event | category | flops | bytes accessed | tf_op | source)
XLA Modules:
  0.0 17.8 jit_solution(6048164048951978686)
XLA Ops:
  0.6 2.0 %load.1 = (f32[8,4,80,128]{3,2,1,0:T(8,128)S(1)}, f32[4,64,512]{2,1,0:T(8,128)S(1)}, f32[4,64,512]{2,1,0:T(8,128)S(1)}, s32[4,64,512]{2,1,0:T(8,128)S(1)}, f32[6...) custom-call(f32[1,3]{1,0:T(1,128)} %bitcast.3, ...), custom_call_target="tpu_custom_call" | custom-call | tf_op jit(solution)/shard_map/load/pallas_call | solution.py:711
  2.6 3.0 %collective-permute-start = (f32[64,128]{1,0:T(8,128)S(1)}, f32[64,128]{1,0:T(8,128)S(1)}, u32[]{:S(2)}, u32[]{:S(2)}) collective-permute-start(f32[64,128]{1,0:T(8,128)S(1)} %get-tuple-element.49.own), channel_id=1, source_target_pairs={{0,2},{2,0},{1,3},{3,1},{4,6},{6,4},{5,7},{7,5},{8,10},{10,8},{9,1... | collective-permute-start | bytes 98312 | tf_op jit(solution)/shard_map/ppermute | solution.py:21
  5.6 2.0 %step_0.1 = (f32[2560,128]{1,0:T(8,128)S(1)}, f32[4,64,512]{2,1,0:T(8,128)S(1)}, f32[4,64,512]{2,1,0:T(8,128)S(1)}, s32[4,64,512]{2,1,0:T(8,128)S(1)}, f32[2560,...) custom-call(f32[4,64,512]{2,1,0:T(8,128)} %adj_next_in.3, ...), custom_call_target="tpu_custom_call", output_to_operand_aliasing={{0}: (4, {}), {1}: (5, {}), {2}: (6, {}), {3}: (7, {})} | custom-call | flops 4000000 | bytes 4000000 | tf_op jit(solution)/shard_map/step_0/pallas_call | solution.py:711
  7.6 0.0 collective-permute-done.left.right
  7.7 0.2 %edge_rows.1 = (f32[32,512]{1,0:T(8,128)S(1)}, f32[32,512]{1,0:T(8,128)S(1)}) custom-call(f32[64,128]{1,0:T(8,128)S(1)} %get-tuple-element.49.own, f32[64,128]{1,0:T(8,128)S(1)} %collective-permute-done.left.right, f32[64,128]{1,0:T(8,128)S(1)} %collective-permute-done.left.right, f32[2,32,512]{2,1,0:T(8,128)S(1)} %get-tuple-element.50.messages), custom_call_target="tpu_custom_call" | custom-call | tf_op jit(solution)/shard_map/edge_rows/pallas_call | solution.py:711
  7.9 2.0 %collective-permute-start.1 = (f32[32,512]{1,0:T(8,128)S(1)}, f32[32,512]{1,0:T(8,128)S(1)}, u32[]{:S(2)}, u32[]{:S(2)}) collective-permute-start(f32[32,512]{1,0:T(8,128)S(1)} %get-tuple-element.61), channel_id=1, source_target_pairs={{0,4},{4,8},{8,12},{12,0},{1,5},{5,9},{9,13},{13,1},{2,6},{6,10},{... | collective-permute-start | bytes 196616 | tf_op jit(solution)/shard_map/ppermute | solution.py:21
  9.9 2.1 %collective-permute-start.2 = (f32[32,512]{1,0:T(8,128)S(1)}, f32[32,512]{1,0:T(8,128)S(1)}, u32[]{:S(2)}, u32[]{:S(2)}) collective-permute-start(f32[32,512]{1,0:T(8,128)S(1)} %get-tuple-element.51.sent), channel_id=1, source_target_pairs={{0,12},{4,0},{8,4},{12,8},{1,13},{5,1},{9,5},{13,9},{2,14},{6,2},{... | collective-permute-start | bytes 196616 | tf_op jit(solution)/shard_map/ppermute | solution.py:21
  12.0 2.7 %inner_steps.1 = (f32[2560,128]{1,0:T(8,128)S(1)}, f32[2560,128]{1,0:T(8,128)S(1)}, f32[4,4,80,128]{3,2,1,0:T(8,128)S(1)}, f32[3,64,512]{2,1,0:T(8,128)S(1)}, f3...) custom-call(f32[1,3]{1,0:T(1,128)S(1)} %get-tuple-element.39.weights, ...), custom_call_target="tpu_custom_call", output_to_operand_aliasing={{0}: (7, {}), {1}: (8, {}), {2}: (9, {}), {3}: (10, {})} | custom-call | flops 4000000 | bytes 4000000 | tf_op jit(solution)/shard_map/inner_steps/pallas_call | solution.py:711
  14.7 0.2 %collective-permute-done.1.above = f32[32,512]{1,0:T(8,128)S(1)} collective-permute-done((f32[32,512]{1,0:T(8,128)S(1)}, f32[32,512]{1,0:T(8,128)S(1)}, u32[]{:S(2)}, u32[]{:S(2)}) %collective-permute-start.1) | collective-permute-done | bytes 65568 | tf_op jit(solution)/shard_map/ppermute | solution.py:21
  14.9 0.0 collective-permute-done.2.below
  14.9 0.3 %outer_rows.1 = (f32[3,64,512]{2,1,0:T(8,128)S(1)}, f32[4,64,512]{2,1,0:T(8,128)S(1)}, f32[4,64,512]{2,1,0:T(8,128)S(1)}) custom-call(f32[2560,128]{1,0:T(8,128)S(1)} %get-tuple-element.47.x0, f32[2560,128]{1,0:T(8,128)S(1)} %get-tuple-element.56.x1, ...), custom_call_target="tpu_custom_call", output_to_operand_aliasing={{0}: (8, {}), {1}: (9, {}), {2}: (10, {})} | custom-call | flops 4000000 | bytes 4000000 | tf_op jit(solution)/shard_map/outer_rows/pallas_call | solution.py:711
  15.3 0.1 collective-permute-start.3
  15.3 1.0 %store.1 = (f32[4,64,512]{2,1,0:T(8,128)}, f32[4,64,512]{2,1,0:T(8,128)}) custom-call(f32[4,64,512]{2,1,0:T(8,128)S(1)} %get-tuple-element.69.adj, f32[4,64,512]{2,1,0:T(8,128)S(1)} %get-tuple-element.70.fwd), custom_call_target="tpu_custom_call" | custom-call | flops 4000000 | bytes 4000000 | tf_op jit(solution)/shard_map/store/pallas_call | solution.py:711
  16.4 0.7 %collective-permute-done.3.other = f32[3,64,512]{2,1,0:T(8,128)S(1)} collective-permute-done((f32[3,64,512]{2,1,0:T(8,128)S(1)}, f32[3,64,512]{2,1,0:T(8,128)S(1)}, u32[]{:S(2)}, u32[]{:S(2)}) %collective-permute-start.3) | collective-permute-done | bytes 393248 | tf_op jit(solution)/shard_map/ppermute | solution.py:21
  17.1 0.8 %force_sums.1 = (f32[64,512]{1,0:T(8,128)}, f32[64,512]{1,0:T(8,128)}, f32[64,512]{1,0:T(8,128)}) custom-call(f32[3,64,512]{2,1,0:T(8,128)S(1)} %get-tuple-element.65.mine, f32[3,64,512]{2,1,0:T(8,128)S(1)} %collective-permute-done.3.other), custom_call_target="tpu_custom_call" | custom-call | tf_op jit(solution)/shard_map/force_sums/pallas_call | solution.py:711
Async XLA Ops:
  2.6 5.0 %collective-permute-start = (f32[64,128]{1,0:T(8,128)S(1)}, f32[64,128]{1,0:T(8,128)S(1)}, u32[]{:S(2)}, u32[]{:S(2)}) collective-permute-start(f32[64,128]{1,0:T(8,128)S(1)} %get-tuple-element.49.own), channel_id=1, source_target_pairs={{0,2},{2,0},{1,3},{3,1},{4,6},{6,4},{5,7},{7,5},{8,10},{10,8},{9,1... | collective-permute-start | bytes 98312 | tf_op jit(solution)/shard_map/ppermute | solution.py:21
  7.9 7.0 %collective-permute-start.1 = (f32[32,512]{1,0:T(8,128)S(1)}, f32[32,512]{1,0:T(8,128)S(1)}, u32[]{:S(2)}, u32[]{:S(2)}) collective-permute-start(f32[32,512]{1,0:T(8,128)S(1)} %get-tuple-element.61), channel_id=1, source_target_pairs={{0,4},{4,8},{8,12},{12,0},{1,5},{5,9},{9,13},{13,1},{2,6},{6,10},{... | collective-permute-start | bytes 196616 | tf_op jit(solution)/shard_map/ppermute | solution.py:21
  9.9 5.0 %collective-permute-start.2 = (f32[32,512]{1,0:T(8,128)S(1)}, f32[32,512]{1,0:T(8,128)S(1)}, u32[]{:S(2)}, u32[]{:S(2)}) collective-permute-start(f32[32,512]{1,0:T(8,128)S(1)} %get-tuple-element.51.sent), channel_id=1, source_target_pairs={{0,12},{4,0},{8,4},{12,8},{1,13},{5,1},{9,5},{13,9},{2,14},{6,2},{... | collective-permute-start | bytes 196616 | tf_op jit(solution)/shard_map/ppermute | solution.py:21
  15.3 1.8 %collective-permute-start.3 = (f32[3,64,512]{2,1,0:T(8,128)S(1)}, f32[3,64,512]{2,1,0:T(8,128)S(1)}, u32[]{:S(2)}, u32[]{:S(2)}) collective-permute-start(f32[3,64,512]{2,1,0:T(8,128)S(1)} %get-tuple-element.65.mine), channel_id=1, source_target_pairs={{0,1},{1,0},{2,3},{3,2},{4,5},{5,4},{6,7},{7,6},{8,9},{9,8},{10,11... | collective-permute-start | bytes 1179656 | tf_op jit(solution)/shard_map/ppermute | solution.py:21
